TPU v7x, 32 devices: a whole 2x2x4 slice. The times are simulated.
32 devices in a mesh: pb: 4 (over y, x), pa: 8 (over z, core).
Axes of the slice: x: 2, y: 2, z: 4, core: 2. Of those that a mesh axis runs over, the one named last changes fastest.
Arguments:
- decoder_states: bfloat16 [4, 16, 64, 1024], P('pb', 'pa'), may hold values from -6 to 6
- encoder_memory: bfloat16 [4, 16, 512, 1024], P('pb', 'pa'), may hold values from -6 to 6
- target_tokens: int32 [4, 16, 64], P('pb', 'pa'), may hold values from 0 to 50303
- log_prior: float32 [4, 16], P('pb', 'pa'), may hold values from -24 to 2
- slot_counts: int32 [4], P('pb'), may hold values from 2 to 16, as said below
- slot_mask: int32 [4, 16], P('pb', 'pa'), may hold values from 0 to 1, as said below
- self_packed: bfloat16 [1024, 3072], P('pa'), may hold values from -0.1875 to 0.1875
- self_output: bfloat16 [1024, 1024], P('pa'), may hold values from -0.75 to 0.75
- cross_query: bfloat16 [1024, 1024], P('pa'), may hold values from -0.1875 to 0.1875
- cross_memory: bfloat16 [1024, 2048], P('pa'), may hold values from -0.1875 to 0.1875
- cross_output: bfloat16 [1024, 1024], P('pa'), may hold values from -1.5 to 1.5
- feed_expand: bfloat16 [1024, 4096], P('pa'), may hold values from -0.1875 to 0.1875
- feed_reduce: bfloat16 [4096, 1024], P('pa'), may hold values from -0.09375 to 0.09375
- embedding: bfloat16 [50304, 1024], P('pa'), may hold values from -0.40625 to 0.40625
- norm_gains: bfloat16 [3, 1024], P(None, 'pa'), may hold values from 0.5 to 1.5
- norm_shifts: bfloat16 [3, 1024], P(None, 'pa'), may hold values from -1.75 to 1.75
Outputs:
- mean_loss: float32 [], replicated
- grad_states: float32 [4, 16, 64, 1024], P('pb', 'pa')
- grad_memory: float32 [4, 16, 512, 1024], P('pb', 'pa')
- grad_prior: float32 [4, 16], P('pb', 'pa')
- grad_self_packed: float32 [1024, 3072], P('pa')
- grad_self_output: float32 [1024, 1024], P('pa')
- grad_cross_query: float32 [1024, 1024], P('pa')
- grad_cross_memory: float32 [1024, 2048], P('pa')
- grad_cross_output: float32 [1024, 1024], P('pa')
- grad_feed_expand: float32 [1024, 4096], P('pa')
- grad_feed_reduce: float32 [4096, 1024], P('pa')
- grad_embedding: float32 [50304, 1024], P('pa')
- grad_norm_gains: float32 [3, 1024], P(None, 'pa')
- grad_norm_shifts: float32 [3, 1024], P(None, 'pa')
Inputs may be any that keep to these rules, and one draw needn't show every extreme that they name: `slot_counts`: for one question, drawn from the seed, all 16 slots are counted. `slot_mask`: slots 0 and 1 of every question are 1.
All inputs are finite; a program needn't handle non-finite values.
Results may differ from a plain program's by a relative error of at most 0.019.
Values may be sent and summed in bfloat16 or wider, within the bound.
A program may use at most 256 MiB of HBM per device.

v0:
```python
import math

import jax
import jax.numpy as jnp
from jax import lax
from jax.sharding import PartitionSpec as P

HEADS = 16
HEAD_DIM = 64


EPSILON = 1e-05
NEGATIVE = -1e30
BFLOAT = jnp.bfloat16


def merged(part, axis, combine):
    gathered = jax.tree.map(lambda a: lax.all_gather(a, axis), part)

    def take(source):
        return jax.tree.map(lambda a: lax.dynamic_index_in_dim(a, source, 0, False), gathered)

    return lax.fori_loop(
        1, lax.axis_size(axis), lambda source, state: combine(state, take(source)), take(0)
    )


def matmul(matrix_left, matrix_right):
    return lax.dot_general(
        matrix_left,
        matrix_right,
        (((matrix_left.ndim - 1,), (0,)), ((), ())),
        preferred_element_type=jnp.float32,
    )


def matmul_back(matrix_left, matrix_right):
    return lax.dot_general(
        matrix_left,
        matrix_right,
        (((matrix_left.ndim - 1,), (1,)), ((), ())),
        preferred_element_type=jnp.float32,
    )


def outer_sum(matrix_left, matrix_right):
    flat_left = matrix_left.reshape(-1, matrix_left.shape[-1])
    flat_right = matrix_right.reshape(-1, matrix_right.shape[-1])
    return lax.dot_general(
        flat_left, flat_right, (((0,), (0,)), ((), ())), preferred_element_type=jnp.float32
    )


def split_heads(values):
    return values.reshape(values.shape[0], values.shape[1], HEADS, HEAD_DIM)


def join_heads(values):
    return values.reshape(values.shape[0], values.shape[1], HEADS * HEAD_DIM)


def exact_gelu(values):
    return jax.nn.gelu(values, approximate=False)


def norm_forward(values, gain_row, shift_row):
    centre = values - jnp.mean(values, -1, keepdims=True)
    inverse = lax.rsqrt(jnp.mean(centre * centre, -1, keepdims=True) + EPSILON)
    normed = centre * inverse
    return (normed * gain_row.astype(jnp.float32) + shift_row.astype(jnp.float32), normed, inverse)


def norm_backward(upstream, normed, inverse, gain_row):
    scaled = upstream * gain_row.astype(jnp.float32)
    mean_scaled = jnp.mean(scaled, -1, keepdims=True)
    along_normed = jnp.mean(scaled * normed, -1, keepdims=True)
    grad_values = inverse * (scaled - mean_scaled - normed * along_normed)
    model_width = upstream.shape[-1]
    grad_gain = jnp.sum((upstream * normed).reshape(-1, model_width), 0)
    grad_shift = jnp.sum(upstream.reshape(-1, model_width), 0)
    return (grad_values, grad_gain, grad_shift)


def score_block(queries, key_rows, causal):
    scores = jnp.einsum(
        "nqhd,nkhd->nhqk", queries, key_rows, preferred_element_type=jnp.float32
    ) * (1.0 / math.sqrt(HEAD_DIM))
    if causal:
        length = queries.shape[1]
        allowed = lax.broadcasted_iota(jnp.int32, (length, length), 0) >= lax.broadcasted_iota(
            jnp.int32, (length, length), 1
        )
        scores = jnp.where(allowed, scores, NEGATIVE)
    return scores


def attend(queries, key_rows, values, causal):
    scores = score_block(queries, key_rows, causal)
    highest = jnp.max(scores, -1, keepdims=True)
    totals = jnp.sum(jnp.exp(scores - highest), -1, keepdims=True)
    logsum = highest + jnp.log(totals)
    probs_low = jnp.exp(scores - logsum).astype(BFLOAT)
    context = jnp.einsum(
        "nhqk,nkhd->nqhd", probs_low, values, preferred_element_type=jnp.float32
    ).astype(BFLOAT)
    return (join_heads(context), logsum)


def attend_back(grad_context, queries, key_rows, values, logsum, causal):
    score_scale = 1.0 / math.sqrt(HEAD_DIM)
    probs_full = jnp.exp(score_block(queries, key_rows, causal) - logsum)
    grad_heads = split_heads(grad_context)
    grad_probs = jnp.einsum(
        "nqhd,nkhd->nhqk", grad_heads, values, preferred_element_type=jnp.float32
    )
    grad_values = jnp.einsum(
        "nhqk,nqhd->nkhd", probs_full.astype(BFLOAT), grad_heads, preferred_element_type=jnp.float32
    ).astype(BFLOAT)
    grad_scores = (
        probs_full * (grad_probs - jnp.sum(probs_full * grad_probs, -1, keepdims=True))
    ).astype(BFLOAT)
    grad_queries = (
        jnp.einsum("nhqk,nkhd->nqhd", grad_scores, key_rows, preferred_element_type=jnp.float32)
        * score_scale
    ).astype(BFLOAT)
    grad_keys = (
        jnp.einsum("nhqk,nqhd->nkhd", grad_scores, queries, preferred_element_type=jnp.float32)
        * score_scale
    ).astype(BFLOAT)
    return (join_heads(grad_queries), join_heads(grad_keys), join_heads(grad_values))


def layer_forward(inputs, encoded, weights):
    (
        packed_weight,
        output_weight,
        query_weight,
        memory_weight,
        cross_weight,
        expand_weight,
        reduce_weight,
        gains,
        shifts,
    ) = weights
    model_width = inputs.shape[-1]
    packed = matmul(inputs, packed_weight).astype(BFLOAT)
    context, self_logsum = attend(
        split_heads(packed[..., :model_width]),
        split_heads(packed[..., model_width : 2 * model_width]),
        split_heads(packed[..., 2 * model_width :]),
        True,
    )
    first_norm, first_normed, first_inverse = norm_forward(
        inputs.astype(jnp.float32) + matmul(context, output_weight), gains[0], shifts[0]
    )
    first_low = first_norm.astype(BFLOAT)
    cross_queries = matmul(first_low, query_weight).astype(BFLOAT)
    memory_pairs = matmul(encoded, memory_weight).astype(BFLOAT)
    cross_context, cross_logsum = attend(
        split_heads(cross_queries),
        split_heads(memory_pairs[..., :model_width]),
        split_heads(memory_pairs[..., model_width:]),
        False,
    )
    second, second_normed, second_inverse = norm_forward(
        first_norm + matmul(cross_context, cross_weight), gains[1], shifts[1]
    )
    second_low = second.astype(BFLOAT)
    inner_pre = matmul(second_low, expand_weight)
    active = exact_gelu(inner_pre).astype(BFLOAT)
    third_norm, third_normed, third_inverse = norm_forward(
        second + matmul(active, reduce_weight), gains[2], shifts[2]
    )
    stored = (
        packed,
        context,
        self_logsum,
        first_normed,
        first_inverse,
        first_low,
        cross_queries,
        memory_pairs,
        cross_context,
        cross_logsum,
        second_normed,
        second_inverse,
        second_low,
        inner_pre,
        active,
        third_normed,
        third_inverse,
    )
    return (third_norm.astype(BFLOAT), stored)


def layer_backward(grad_third, inputs, encoded, weights, stored):
    (
        packed_weight,
        output_weight,
        query_weight,
        memory_weight,
        cross_weight,
        expand_weight,
        reduce_weight,
        gains,
        shifts,
    ) = weights
    (
        packed,
        context,
        self_logsum,
        first_normed,
        first_inverse,
        first_low,
        cross_queries,
        memory_pairs,
        cross_context,
        cross_logsum,
        second_normed,
        second_inverse,
        second_low,
        inner_pre,
        active,
        third_normed,
        third_inverse,
    ) = stored
    model_width = inputs.shape[-1]
    grad_res3, gain_three, shift_three = norm_backward(
        grad_third, third_normed, third_inverse, gains[2]
    )
    grad_output = grad_res3.astype(BFLOAT)
    grad_reduce = outer_sum(active, grad_output)
    grad_active = matmul_back(grad_output, reduce_weight)
    _, gelu_pull = jax.vjp(exact_gelu, inner_pre)
    grad_inner = gelu_pull(grad_active)[0].astype(BFLOAT)
    grad_expand = outer_sum(second_low, grad_inner)
    grad_second = grad_res3 + matmul_back(grad_inner, expand_weight)
    grad_res2, gain_two, shift_two = norm_backward(
        grad_second, second_normed, second_inverse, gains[1]
    )
    grad_mixed = grad_res2.astype(BFLOAT)
    grad_cross_weight = outer_sum(cross_context, grad_mixed)
    grad_cross_context = matmul_back(grad_mixed, cross_weight).astype(BFLOAT)
    grad_cross_queries, grad_memory_keys, grad_memory_values = attend_back(
        grad_cross_context,
        split_heads(cross_queries),
        split_heads(memory_pairs[..., :model_width]),
        split_heads(memory_pairs[..., model_width:]),
        cross_logsum,
        False,
    )
    grad_query_weight = outer_sum(first_low, grad_cross_queries)
    grad_first = grad_res2 + matmul_back(grad_cross_queries, query_weight)
    grad_pairs = jnp.concatenate([grad_memory_keys, grad_memory_values], -1)
    grad_memory_weight = outer_sum(encoded, grad_pairs)
    grad_encoded = matmul_back(grad_pairs, memory_weight)
    grad_res1, gain_one, shift_one = norm_backward(
        grad_first, first_normed, first_inverse, gains[0]
    )
    grad_merged = grad_res1.astype(BFLOAT)
    grad_output_weight = outer_sum(context, grad_merged)
    grad_context = matmul_back(grad_merged, output_weight).astype(BFLOAT)
    grad_queries, grad_keys, grad_values = attend_back(
        grad_context,
        split_heads(packed[..., :model_width]),
        split_heads(packed[..., model_width : 2 * model_width]),
        split_heads(packed[..., 2 * model_width :]),
        self_logsum,
        True,
    )
    grad_packed = jnp.concatenate([grad_queries, grad_keys, grad_values], -1)
    grad_packed_weight = outer_sum(inputs, grad_packed)
    grad_inputs = grad_res1 + matmul_back(grad_packed, packed_weight)
    grad_gains = jnp.stack([gain_one, gain_two, gain_three])
    grad_shifts = jnp.stack([shift_one, shift_two, shift_three])
    return (
        grad_inputs,
        grad_encoded,
        (
            grad_packed_weight,
            grad_output_weight,
            grad_query_weight,
            grad_memory_weight,
            grad_cross_weight,
            grad_expand,
            grad_reduce,
            grad_gains,
            grad_shifts,
        ),
    )


def combine_scores(former, latter):
    highest = jnp.maximum(former[0], latter[0])
    totals = former[1] * jnp.exp(former[0] - highest) + latter[1] * jnp.exp(latter[0] - highest)
    return (highest, totals, former[2] + latter[2])


def combine_pairs(former, latter):
    highest = jnp.maximum(former[0], latter[0])
    totals = former[1] * jnp.exp(former[0] - highest) + latter[1] * jnp.exp(latter[0] - highest)
    return (highest, totals)


def per_device(
    decoder_states,
    encoder_memory,
    target_tokens,
    log_prior,
    slot_counts,
    slot_mask,
    self_packed,
    self_output,
    cross_query,
    cross_memory,
    cross_output,
    feed_expand,
    feed_reduce,
    embedding,
    norm_gains,
    norm_shifts,
):
    weights = (
        lax.all_gather(self_packed, "pa", axis=0, tiled=True),
        lax.all_gather(self_output, "pa", axis=0, tiled=True),
        lax.all_gather(cross_query, "pa", axis=0, tiled=True),
        lax.all_gather(cross_memory, "pa", axis=0, tiled=True),
        lax.all_gather(cross_output, "pa", axis=0, tiled=True),
        lax.all_gather(feed_expand, "pa", axis=0, tiled=True),
        lax.all_gather(feed_reduce, "pa", axis=0, tiled=True),
        lax.all_gather(norm_gains, "pa", axis=1, tiled=True),
        lax.all_gather(norm_shifts, "pa", axis=1, tiled=True),
    )
    questions, slots_here, length, model_width = decoder_states.shape
    mem_length = encoder_memory.shape[2]
    batch_size = questions * slots_here
    inputs = decoder_states.reshape(batch_size, length, model_width)
    encoded = encoder_memory.reshape(batch_size, mem_length, model_width)
    third_low, stored = layer_forward(inputs, encoded, weights)
    tokens_here = batch_size * length
    rows_all, tokens_all = (
        lax.all_gather(third_low.reshape(tokens_here, model_width), "pa", axis=0, tiled=True),
        lax.all_gather(target_tokens.reshape(tokens_here), "pa", axis=0, tiled=True),
    )
    total_rows = rows_all.shape[0]
    block_rows = min(total_rows, 2048)
    block_count = total_rows // block_rows
    vocab_start = lax.axis_index("pa") * embedding.shape[0]
    row_blocks = rows_all.reshape(block_count, block_rows, model_width)
    token_blocks = tokens_all.reshape(block_count, block_rows)

    def vocab_logits(hidden_rows, token_rows):
        logits = matmul_back(hidden_rows, embedding)
        column = lax.broadcasted_iota(jnp.int32, logits.shape, 1) + vocab_start
        return (logits, column == token_rows[:, None])

    def vocab_partial(pieces):
        logits, chosen = vocab_logits(pieces[0], pieces[1])
        highest = jnp.max(logits, -1)
        totals = jnp.sum(jnp.exp(logits - highest[:, None]), -1)
        picked = jnp.sum(jnp.where(chosen, logits, 0.0), -1)
        return (highest, totals, picked)

    highest, totals, picked = lax.map(vocab_partial, (row_blocks, token_blocks))
    highest, totals, picked = merged(
        (highest.reshape(total_rows), totals.reshape(total_rows), picked.reshape(total_rows)),
        "pa",
        combine_scores,
    )
    row_logsum = highest + jnp.log(totals)
    own_start = lax.axis_index("pa") * tokens_here
    own_logsum = lax.dynamic_slice_in_dim(row_logsum, own_start, tokens_here)
    own_picked = lax.dynamic_slice_in_dim(picked, own_start, tokens_here)
    log_probs = (own_picked - own_logsum).reshape(questions, slots_here, length)
    scores = log_prior + jnp.mean(log_probs, -1)
    slot_index = lax.axis_index("pa") * slots_here + lax.broadcasted_iota(
        jnp.int32, (questions, slots_here), 1
    )
    usable = (slot_mask == 1) & (slot_index < slot_counts[:, None])
    masked = jnp.where(usable, scores, NEGATIVE)
    local_high = jnp.max(masked, -1)
    local_total = jnp.sum(jnp.where(usable, jnp.exp(masked - local_high[:, None]), 0.0), -1)
    slot_high, slot_total = merged((local_high, local_total), "pa", combine_pairs)
    marginal = slot_high + jnp.log(slot_total)
    posterior = jnp.where(usable, jnp.exp(scores - marginal[:, None]), 0.0)
    loss_value = -lax.psum(jnp.sum(marginal), "pb") / (questions * lax.axis_size("pb"))
    slot_number = slots_here * lax.axis_size("pa")
    grad_prior = -(slot_number * length) * posterior
    token_grad = jnp.broadcast_to(
        (-slot_number * posterior)[:, :, None], (questions, slots_here, length)
    ).reshape(tokens_here)
    weights_all = lax.all_gather(token_grad, "pa", axis=0, tiled=True)

    def vocab_grads(accumulated, pieces):
        hidden_rows, token_rows, logsum_rows, weight_rows = pieces
        logits, chosen = vocab_logits(hidden_rows, token_rows)
        softmax_rows = jnp.exp(logits - logsum_rows[:, None])
        grad_logits = (weight_rows[:, None] * (jnp.where(chosen, 1.0, 0.0) - softmax_rows)).astype(
            BFLOAT
        )
        return (accumulated + outer_sum(grad_logits, hidden_rows), matmul(grad_logits, embedding))

    grad_embed, grad_rows = lax.scan(
        vocab_grads,
        jnp.zeros(embedding.shape, jnp.float32),
        (
            row_blocks,
            token_blocks,
            row_logsum.reshape(block_count, block_rows),
            weights_all.reshape(block_count, block_rows),
        ),
    )
    grad_third = lax.psum_scatter(
        grad_rows.reshape(total_rows, model_width), "pa", scatter_dimension=0, tiled=True
    ).reshape(batch_size, length, model_width)
    grad_inputs, grad_encoded, grads = layer_backward(grad_third, inputs, encoded, weights, stored)
    shares = (
        lax.psum_scatter(grads[0], "pa", scatter_dimension=0, tiled=True),
        lax.psum_scatter(grads[1], "pa", scatter_dimension=0, tiled=True),
        lax.psum_scatter(grads[2], "pa", scatter_dimension=0, tiled=True),
        lax.psum_scatter(grads[3], "pa", scatter_dimension=0, tiled=True),
        lax.psum_scatter(grads[4], "pa", scatter_dimension=0, tiled=True),
        lax.psum_scatter(grads[5], "pa", scatter_dimension=0, tiled=True),
        lax.psum_scatter(grads[6], "pa", scatter_dimension=0, tiled=True),
        lax.psum_scatter(grads[7], "pa", scatter_dimension=1, tiled=True),
        lax.psum_scatter(grads[8], "pa", scatter_dimension=1, tiled=True),
    )
    outputs = lax.psum(
        (
            shares[0],
            shares[1],
            shares[2],
            shares[3],
            shares[4],
            shares[5],
            shares[6],
            shares[7],
            shares[8],
            grad_embed,
        ),
        "pb",
    )
    return (
        loss_value,
        grad_inputs.reshape(decoder_states.shape),
        grad_encoded.reshape(encoder_memory.shape),
        grad_prior,
        outputs[0],
        outputs[1],
        outputs[2],
        outputs[3],
        outputs[4],
        outputs[5],
        outputs[6],
        outputs[9],
        outputs[7],
        outputs[8],
    )


def solution(mesh):
    return jax.shard_map(
        per_device,
        mesh=mesh,
        in_specs=(
            P("pb", "pa", None, None),
            P("pb", "pa", None, None),
            P("pb", "pa", None),
            P("pb", "pa"),
            P("pb"),
            P("pb", "pa"),
            P("pa", None),
            P("pa", None),
            P("pa", None),
            P("pa", None),
            P("pa", None),
            P("pa", None),
            P("pa", None),
            P("pa", None),
            P(None, "pa"),
            P(None, "pa"),
        ),
        out_specs=(
            P(),
            P("pb", "pa", None, None),
            P("pb", "pa", None, None),
            P("pb", "pa"),
            P("pa", None),
            P("pa", None),
            P("pa", None),
            P("pa", None),
            P("pa", None),
            P("pa", None),
            P("pa", None),
            P("pa", None),
            P(None, "pa"),
            P(None, "pa"),
        ),
        check_vma=False,
    )
```

profile of v0, /device:TPU:0, one launch (start us, length us, event | category | flops | bytes accessed | tf_op | source)
XLA Modules:
  0.0 2089.0 jit_solution(4508826957352134572)
XLA Ops:
  34.4 25.1 %all-gather.18.cloned.1.call-done = bf16[1024,2048]{1,0:T(8,128)(2,1)} async-done(((bf16[128,2048]{1,0:T(8,128)(2,1)}), bf16[1024,2048]{1,0:T(8,128)(2,1)}) %all-gather.18.cloned.1.call-update) | async-done | bytes 4194320 | tf_op jit(solution)/shard_map/all_gather | solution.py:327
  77.3 47.5 %all-gather.14.cloned.1.call-done = bf16[1024,3072]{1,0:T(8,128)(2,1)} async-done(((bf16[128,3072]{1,0:T(8,128)(2,1)}), bf16[1024,3072]{1,0:T(8,128)(2,1)}) %all-gather.14.cloned.1.call-update) | async-done | bytes 6291472 | tf_op jit(solution)/shard_map/all_gather | solution.py:324
  135.1 19.0 all-gather.16.cloned.1.call-done
  156.9 27.4 %all-gather.20.cloned.1.call-done = bf16[1024,1024]{1,0:T(8,128)(2,1)} async-done(((bf16[128,1024]{1,0:T(8,128)(2,1)}), bf16[1024,1024]{1,0:T(8,128)(2,1)}) %all-gather.20.cloned.1.call-update) | async-done | bytes 2097168 | tf_op jit(solution)/shard_map/all_gather | solution.py:326
  195.7 18.6 all-gather.22.cloned.1.call-done
  216.8 80.5 %all-gather.24.cloned.1.call-done = bf16[1024,4096]{1,0:T(8,128)(2,1)} async-done(((bf16[128,4096]{1,0:T(8,128)(2,1)}), bf16[1024,4096]{1,0:T(8,128)(2,1)}) %all-gather.24.cloned.1.call-update) | async-done | bytes 8388624 | tf_op jit(solution)/shard_map/all_gather | solution.py:329
  305.1 74.5 %all-gather.26.cloned.1.call-done = bf16[4096,1024]{1,0:T(8,128)(2,1)} async-done(((bf16[512,1024]{1,0:T(8,128)(2,1)}), bf16[4096,1024]{1,0:T(8,128)(2,1)}) %all-gather.26.cloned.1.call-update) | async-done | bytes 8388624 | tf_op jit(solution)/shard_map/all_gather | solution.py:330
  400.8 17.5 all-gather.28.cloned.1.call-done
  418.3 22.2 %fusion.139 = (f32[1024]{0:T(1024)S(1)}, f32[1024,6288]{0,1:T(8,128)}) fusion(bf16[1024,1024]{1,0:T(8,128)(2,1)} %all-gather.28.cloned.1.call-done, bf16[6288,1024]{1,0:T(8,128)(2,1)} %param.33), kind=kOutput, calls=%fused_computation.203 | convolution fusion | flops 13193329664 | bytes 40734720 | tf_op jit(solution)/shard_map/while/body/eval_jaxpr/dot_general | solution.py:38
  452.2 14.2 all-gather.2
  481.1 14.0 all-gather.1
  507.9 15.3 all-reduce.2
  523.3 18.1 while.48
  567.7 17.3 fusion.140
  589.5 45.3 %reduce-scatter.15.cloned.1.call-done = f32[128,1024]{1,0:T(8,128)} async-done(((f32[1024,1024]{1,0:T(8,128)}), f32[128,1024]{1,0:T(8,128)}) %reduce-scatter.15.cloned.1.call-update) | async-done | bytes 524304 | tf_op jit(solution)/shard_map/reduce_scatter | solution.py:413
  759.1 21.5 %fusion.144 = f32[6288,1024]{1,0:T(8,128)} fusion(bf16[1024,6288]{0,1:T(8,128)(2,1)} %copy-done.13, bf16[1024,1024]{1,0:T(8,128)(2,1)S(1)} %copy-done.62), kind=kOutput, calls=%fused_computation.208 | convolution fusion | flops 13186891776 | bytes 40730624 | tf_op jit(solution)/shard_map/while/body/eval_jaxpr/dot_general | solution.py:49
  780.6 48.2 %reduce-scatter.25.cloned.1.call-done = f32[128,1024]{1,0:T(8,128)} async-done(((f32[1024,1024]{1,0:T(8,128)}), f32[128,1024]{1,0:T(8,128)}) %reduce-scatter.25.cloned.1.call-update) | async-done | bytes 524304 | tf_op jit(solution)/shard_map/reduce_scatter | solution.py:422
  828.8 90.1 %reduce-scatter.23.cloned.1.call-done = f32[128,2048]{0,1:T(8,128)} async-done(((f32[1024,2048]{0,1:T(8,128)}), f32[128,2048]{0,1:T(8,128)}) %reduce-scatter.23.cloned.1.call-update) | async-done | bytes 1048592 | tf_op jit(solution)/shard_map/reduce_scatter | solution.py:421
  918.8 129.7 %reduce-scatter.17.cloned.1.call-done = f32[128,3072]{0,1:T(8,128)} async-done(((f32[1024,3072]{0,1:T(8,128)}), f32[128,3072]{0,1:T(8,128)}) %reduce-scatter.17.cloned.1.call-update) | async-done | bytes 1572880 | tf_op jit(solution)/shard_map/reduce_scatter | solution.py:418
  1048.6 168.9 %reduce-scatter.29.cloned.1.call-done = f32[512,1024]{1,0:T(8,128)} async-done(((f32[4096,1024]{1,0:T(8,128)}), f32[512,1024]{1,0:T(8,128)}) %reduce-scatter.29.cloned.1.call-update) | async-done | bytes 2097168 | tf_op jit(solution)/shard_map/reduce_scatter | solution.py:424
  1217.5 168.8 %reduce-scatter.27.cloned.1.call-done = f32[128,4096]{1,0:T(8,128)} async-done(((f32[1024,4096]{1,0:T(8,128)}), f32[128,4096]{1,0:T(8,128)}) %reduce-scatter.27.cloned.1.call-update) | async-done | bytes 2097168 | tf_op jit(solution)/shard_map/reduce_scatter | solution.py:423
  1419.2 31.0 %reduce-scatter.31.cloned.1.call-done = f32[128,3]{1,0:T(8,128)} async-done(((f32[1024,3]{1,0:T(8,128)}), f32[128,3]{1,0:T(8,128)}) %reduce-scatter.31.cloned.1.call-update) | async-done | bytes 1552
  1469.2 583.2 %all-reduce.7.cloned.1.call-done = (f32[128,3072]{0,1:T(8,128)}, f32[128,1024]{1,0:T(8,128)}, f32[128,1024]{1,0:T(8,128)}, f32[128,2048]{0,1:T(8,128)}, f32[128,...) async-done(((f32[128,3072]{0,1:T(8,128)}, f32[128,1024]{1,0:T(8,128)}, f32[128,1024]{1,0:T(8,128)}, f32[128,2048]{0,1:T(8,128)}, ...) | async-done | bytes 34144272 | tf_op jit(solution)/shard_map/psum | solution.py:428
  2062.9 18.2 copy.202
  (357 shorter events, 365.2 us)
Async XLA Ops:
  7.2 52.4 %copy-start = (bf16[1,2,512,1024]{3,2,1,0:T(8,128)(2,1)S(1)}, bf16[1,2,512,1024]{3,2,1,0:T(8,128)(2,1)}, u32[]{:S(2)}) copy-start(bf16[1,2,512,1024]{3,2,1,0:T(8,128)(2,1)} %param.21) | copy-start | bytes 6291460
  7.2 52.4 %all-gather.18.cloned.1.call-start = ((), (), s32[]{:S(2)}) async-start(), calls=%async_computation.12 | async-start | bytes 4718592 | tf_op jit(solution)/shard_map/all_gather | solution.py:327
  8.0 116.8 %all-gather.14.cloned.1.call-start = ((), (), s32[]{:S(2)}) async-start(), calls=%async_computation.10 | async-start | bytes 7077888 | tf_op jit(solution)/shard_map/all_gather | solution.py:324
  8.7 145.4 %all-gather.16.cloned.1.call-start = ((), (), s32[]{:S(2)}) async-start(), calls=%async_computation.11 | async-start | bytes 2359296 | tf_op jit(solution)/shard_map/all_gather | solution.py:325
  9.4 174.8 %all-gather.20.cloned.1.call-start = ((), (), s32[]{:S(2)}) async-start(), calls=%async_computation.13 | async-start | bytes 2359296 | tf_op jit(solution)/shard_map/all_gather | solution.py:326
  10.0 204.3 %all-gather.22.cloned.1.call-start = ((), (), s32[]{:S(2)}) async-start(), calls=%async_computation.14 | async-start | bytes 2359296 | tf_op jit(solution)/shard_map/all_gather | solution.py:328
  10.6 286.7 %all-gather.24.cloned.1.call-start = ((), (), s32[]{:S(2)}) async-start(), calls=%async_computation.15 | async-start | bytes 9437184 | tf_op jit(solution)/shard_map/all_gather | solution.py:329
  11.2 368.4 %all-gather.26.cloned.1.call-start = ((), (), s32[]{:S(2)}) async-start(), calls=%async_computation.16 | async-start | bytes 9437184 | tf_op jit(solution)/shard_map/all_gather | solution.py:330
  11.9 406.4 %all-gather.28.cloned.1.call-start = ((), (), s32[]{:S(2)}) async-start(), calls=%async_computation.17 | async-start | bytes 2359296 | tf_op jit(solution)/shard_map/all_gather | solution.py:342
  34.4 345.1 %copy-start.51 = (f32[1,1024]{1,0:T(1,128)}, f32[1,1024]{1,0:T(1,128)S(1)}, u32[]{:S(2)}) copy-start(f32[1,1024]{1,0:T(1,128)S(1)} %get-tuple-element.495) | copy-start | bytes 12292
  216.8 162.7 %copy-start.53 = (f32[2,64]{1,0:T(2,128)}, f32[2,64]{1,0:T(2,128)S(1)}, u32[]{:S(2)}) copy-start(f32[2,64]{1,0:T(2,128)S(1)} %add_rsqrt_fusion.1) | copy-start | bytes 1540
  390.5 244.2 %reduce-scatter.15.cloned.1.call-start = ((), (), s32[]{:S(2)}) async-start(), calls=%async_computation.18 | async-start | bytes 4718592 | tf_op jit(solution)/shard_map/reduce_scatter | solution.py:413
  585.1 195.5 %reduce-scatter.19.cloned.1.call-start = ((), (), s32[]{:S(2)}) async-start(), calls=%async_computation.20 | async-start | bytes 4718592 | tf_op jit(solution)/shard_map/reduce_scatter | solution.py:419
  679.7 100.9 %reduce-scatter.21.cloned.1.call-start = ((), (), s32[]{:S(2)}) async-start(), calls=%async_computation.21 | async-start | bytes 4718592 | tf_op jit(solution)/shard_map/reduce_scatter | solution.py:420
  686.1 142.7 %reduce-scatter.25.cloned.1.call-start = ((), (), s32[]{:S(2)}) async-start(), calls=%async_computation.23 | async-start | bytes 4718592 | tf_op jit(solution)/shard_map/reduce_scatter | solution.py:422
  694.2 224.6 %reduce-scatter.23.cloned.1.call-start = ((), (), s32[]{:S(2)}) async-start(), calls=%async_computation.22 | async-start | bytes 9437184 | tf_op jit(solution)/shard_map/reduce_scatter | solution.py:421
  713.5 335.1 %reduce-scatter.17.cloned.1.call-start = ((), (), s32[]{:S(2)}) async-start(), calls=%async_computation.19 | async-start | bytes 14155776 | tf_op jit(solution)/shard_map/reduce_scatter | solution.py:418
  734.7 482.8 %reduce-scatter.29.cloned.1.call-start = ((), (), s32[]{:S(2)}) async-start(), calls=%async_computation.25 | async-start | bytes 18874368 | tf_op jit(solution)/shard_map/reduce_scatter | solution.py:424
  747.1 639.2 %reduce-scatter.27.cloned.1.call-start = ((), (), s32[]{:S(2)}) async-start(), calls=%async_computation.24 | async-start | bytes 18874368 | tf_op jit(solution)/shard_map/reduce_scatter | solution.py:423
  756.5 661.7 %reduce-scatter.33.cloned.1.call-start = ((), (), s32[]{:S(2)}) async-start(), calls=%async_computation.27 | async-start | bytes 589824
  757.9 692.3 %reduce-scatter.31.cloned.1.call-start = ((), (), s32[]{:S(2)}) async-start(), calls=%async_computation.26 | async-start | bytes 589824
  759.0 1293.4 %all-reduce.7.cloned.1.call-start = ((), (), s32[]{:S(2)}) async-start(), calls=%async_computation.28 | async-start | bytes 68288512 | tf_op jit(solution)/shard_map/psum | solution.py:428
  1396.8 54.2 %copy-start.40 = (f32[2,64,1024]{2,1,0:T(8,128)S(1)}, f32[2,64,1024]{2,1,0:T(8,128)}, u32[]{:S(2)}) copy-start(f32[2,64,1024]{2,1,0:T(8,128)} %copy-done.39) | copy-start | bytes 1572868
  1396.9 54.2 %copy-start.50 = (bf16[2,64,1024]{2,1,0:T(8,128)(2,1)S(1)}, bf16[2,64,1024]{2,1,0:T(8,128)(2,1)}, u32[]{:S(2)}) copy-start(bf16[2,64,1024]{2,1,0:T(8,128)(2,1)} %reshape.344) | copy-start | bytes 786436
  (65 other events, 471.4 us)
Sparse Core Ops, SparseCore 0:
  9.7 49.8 all-gather.17
  61.2 63.4 all-gather.13
  126.3 27.7 all-gather.15
  155.6 28.5 all-gather.19
  185.7 28.5 all-gather.21
  215.7 81.5 all-gather.23
  298.9 80.5 all-gather.25
  390.6 27.6 all-gather.27
  585.2 49.5 reduce-scatter.14
  679.8 48.1 reduce-scatter.18
  730.2 48.1 reduce-scatter.20
  780.6 48.1 reduce-scatter.24
  831.1 87.7 reduce-scatter.22
  921.0 127.5 reduce-scatter.16
  1050.8 166.6 reduce-scatter.28
  1219.7 166.5 reduce-scatter.26
  1389.0 29.2 reduce-scatter.32
  1421.1 29.0 reduce-scatter.30
  1455.3 596.9 all-reduce.6
where the time goes:
time: 2090 us
  waiting for transfers between devices  1590 us (76%)
  matrix products  199 us (10%)
  local copies, waits for them, and re-layouts  118 us (6%)
  blocking collectives  109 us (5%)
  other arithmetic  37.9 us (2%)
    psum x1, waiting for transfers between devices, per_device(): lax.psum((shares[0], shares[1], shares[2], shares[3], shares[4], shares[5...  583 us
    reduce_scatter x1, waiting for transfers between devices, per_device(): lax.psum_scatter(grads[6], 'pa', scatter_dimension=0, tiled=True)  169 us
    reduce_scatter x1, waiting for transfers between devices, per_device(): lax.psum_scatter(grads[5], 'pa', scatter_dimension=0, tiled=True)  169 us
    reduce_scatter x1, waiting for transfers between devices, per_device(): lax.psum_scatter(grads[0], 'pa', scatter_dimension=0, tiled=True)  130 us
    reduce_scatter x1, waiting for transfers between devices, per_device(): lax.psum_scatter(grads[3], 'pa', scatter_dimension=0, tiled=True)  90.1 us
    all_gather x1, waiting for transfers between devices, per_device(): lax.all_gather(feed_expand, 'pa', axis=0, tiled=True)  80.5 us
    all_gather x1, waiting for transfers between devices, per_device(): lax.all_gather(feed_reduce, 'pa', axis=0, tiled=True)  74.5 us
    dot_general x8, matrix products, outer_sum(): lax.dot_general(flat_left, flat_right, (((0,), (0,)), ((), ())), preferre...  67.1 us
  transfers between devices with their start and end apart: 19, of which 17 were waited for; matrix products, arithmetic and copies ran while one was open for 8% of the time, Pallas kernels for 0%

commit v1 on v0

--- a/solution.py
+++ b/solution.py
@@ -411,17 +411,20 @@
         ),
     )
     grad_third = lax.psum_scatter(
-        grad_rows.reshape(total_rows, model_width), "pa", scatter_dimension=0, tiled=True
-    ).reshape(batch_size, length, model_width)
+        grad_rows.reshape(total_rows, model_width).astype(BFLOAT),
+        "pa",
+        scatter_dimension=0,
+        tiled=True,
+    ).astype(jnp.float32).reshape(batch_size, length, model_width)
     grad_inputs, grad_encoded, grads = layer_backward(grad_third, inputs, encoded, weights, stored)
     shares = (
-        lax.psum_scatter(grads[0], "pa", scatter_dimension=0, tiled=True),
-        lax.psum_scatter(grads[1], "pa", scatter_dimension=0, tiled=True),
-        lax.psum_scatter(grads[2], "pa", scatter_dimension=0, tiled=True),
-        lax.psum_scatter(grads[3], "pa", scatter_dimension=0, tiled=True),
-        lax.psum_scatter(grads[4], "pa", scatter_dimension=0, tiled=True),
-        lax.psum_scatter(grads[5], "pa", scatter_dimension=0, tiled=True),
-        lax.psum_scatter(grads[6], "pa", scatter_dimension=0, tiled=True),
+        lax.psum_scatter(grads[0].astype(BFLOAT), "pa", scatter_dimension=0, tiled=True),
+        lax.psum_scatter(grads[1].astype(BFLOAT), "pa", scatter_dimension=0, tiled=True),
+        lax.psum_scatter(grads[2].astype(BFLOAT), "pa", scatter_dimension=0, tiled=True),
+        lax.psum_scatter(grads[3].astype(BFLOAT), "pa", scatter_dimension=0, tiled=True),
+        lax.psum_scatter(grads[4].astype(BFLOAT), "pa", scatter_dimension=0, tiled=True),
+        lax.psum_scatter(grads[5].astype(BFLOAT), "pa", scatter_dimension=0, tiled=True),
+        lax.psum_scatter(grads[6].astype(BFLOAT), "pa", scatter_dimension=0, tiled=True),
         lax.psum_scatter(grads[7], "pa", scatter_dimension=1, tiled=True),
         lax.psum_scatter(grads[8], "pa", scatter_dimension=1, tiled=True),
     )
@@ -436,10 +439,11 @@
             shares[6],
             shares[7],
             shares[8],
-            grad_embed,
+            grad_embed.astype(BFLOAT),
         ),
         "pb",
     )
+    outputs = tuple(part.astype(jnp.float32) for part in outputs)
     return (
         loss_value,
         grad_inputs.reshape(decoder_states.shape),

time: 2090 us -> 1490 us (0.71)
  waiting for transfers between devices: 1590 us -> 1010 us
  local copies, waits for them, and re-layouts: 118 us -> 89 us
    reduce_scatter x8 -> x6, waiting for transfers between devices: 651 us -> 325 us  [the longest x1 90.4 us: per_device(): lax.psum_scatter(grads[5].astype(BFLOAT), 'pa', scatter_dimension=0, tile...]
    psum x1, waiting for transfers between devices: 583 us -> 303 us  [per_device(): lax.psum((shares[0], shares[1], shares[2], shares[3], shares[4], shares[5...]
    unnamed x21 -> x23, waiting for transfers between devices: 46.8 us -> 83.4 us
    unnamed x161 -> x157, local copies, waits for them, and re-layouts: 55.9 us -> 45.1 us
  transfers between devices with their start and end apart: 19 -> 19, of which waited for: 17 -> 18; matrix products, arithmetic and copies ran while one was open for 8% -> 11% of each run, Pallas kernels for 0% -> 0%
where the time goes in v1:
time: 1490 us; the launch traced here: 1480 us
  waiting for transfers between devices  1010 us (68%)
  matrix products  186 us (12%)
  blocking collectives  109 us (7%)
  local copies, waits for them, and re-layouts  89 us (6%)
  other arithmetic  48.6 us (3%)
  between operations  17.8 us (1%)
    psum x1, waiting for transfers between devices, per_device(): lax.psum((shares[0], shares[1], shares[2], shares[3], shares[4], shares[5...  303 us
    reduce_scatter x1, waiting for transfers between devices, per_device(): lax.psum_scatter(grads[5].astype(BFLOAT), 'pa', scatter_dimension=0, tile...  90.4 us
    reduce_scatter x1, waiting for transfers between devices, per_device(): lax.psum_scatter(grads[6].astype(BFLOAT), 'pa', scatter_dimension=0, tile...  90.1 us
    unnamed x23, waiting for transfers between devices  83.4 us
    all_gather x1, waiting for transfers between devices, per_device(): lax.all_gather(feed_expand, 'pa', axis=0, tiled=True)  79.6 us
    all_gather x1, waiting for transfers between devices, per_device(): lax.all_gather(feed_reduce, 'pa', axis=0, tiled=True)  69.1 us
    dot_general x8, matrix products, matmul_back(): lax.dot_general(matrix_left, matrix_right, (((matrix_left.ndim - 1,), (1,...  61.7 us
    dot_general x8, matrix products, outer_sum(): lax.dot_general(flat_left, flat_right, (((0,), (0,)), ((), ())), preferre...  52.6 us
  transfers between devices with their start and end apart: 19, of which 18 were waited for; matrix products, arithmetic and copies ran while one was open for 11% of the time, Pallas kernels for 0%

profile of v1, /device:TPU:0, one launch (start us, length us, event | category | flops | bytes accessed | tf_op | source)
XLA Modules:
  0.0 1480.4 jit_solution(14155499140447537353)
XLA Ops:
  34.4 25.1 %all-gather.18.cloned.1.call-done = bf16[1024,2048]{1,0:T(8,128)(2,1)} async-done(((bf16[128,2048]{1,0:T(8,128)(2,1)}), bf16[1024,2048]{1,0:T(8,128)(2,1)}) %all-gather.18.cloned.1.call-update) | async-done | bytes 4194320 | tf_op jit(solution)/shard_map/all_gather | solution.py:327
  77.2 47.6 %all-gather.14.cloned.1.call-done = bf16[1024,3072]{1,0:T(8,128)(2,1)} async-done(((bf16[128,3072]{1,0:T(8,128)(2,1)}), bf16[1024,3072]{1,0:T(8,128)(2,1)}) %all-gather.14.cloned.1.call-update) | async-done | bytes 6291472 | tf_op jit(solution)/shard_map/all_gather | solution.py:324
  135.8 18.3 %all-gather.16.cloned.1.call-done = bf16[1024,1024]{1,0:T(8,128)(2,1)} async-done(((bf16[128,1024]{1,0:T(8,128)(2,1)}), bf16[1024,1024]{1,0:T(8,128)(2,1)}) %all-gather.16.cloned.1.call-update) | async-done | bytes 2097168 | tf_op jit(solution)/shard_map/all_gather | solution.py:325
  157.4 26.8 %all-gather.20.cloned.1.call-done = bf16[1024,1024]{1,0:T(8,128)(2,1)} async-done(((bf16[128,1024]{1,0:T(8,128)(2,1)}), bf16[1024,1024]{1,0:T(8,128)(2,1)}) %all-gather.20.cloned.1.call-update) | async-done | bytes 2097168 | tf_op jit(solution)/shard_map/all_gather | solution.py:326
  196.4 17.9 %all-gather.22.cloned.1.call-done = bf16[1024,1024]{1,0:T(8,128)(2,1)} async-done(((bf16[128,1024]{1,0:T(8,128)(2,1)}), bf16[1024,1024]{1,0:T(8,128)(2,1)}) %all-gather.22.cloned.1.call-update) | async-done | bytes 2097168 | tf_op jit(solution)/shard_map/all_gather | solution.py:328
  217.7 79.6 %all-gather.24.cloned.1.call-done = bf16[1024,4096]{1,0:T(8,128)(2,1)} async-done(((bf16[128,4096]{1,0:T(8,128)(2,1)}), bf16[1024,4096]{1,0:T(8,128)(2,1)}) %all-gather.24.cloned.1.call-update) | async-done | bytes 8388624 | tf_op jit(solution)/shard_map/all_gather | solution.py:329
  310.4 69.1 %all-gather.26.cloned.1.call-done = bf16[4096,1024]{1,0:T(8,128)(2,1)} async-done(((bf16[512,1024]{1,0:T(8,128)(2,1)}), bf16[4096,1024]{1,0:T(8,128)(2,1)}) %all-gather.26.cloned.1.call-update) | async-done | bytes 8388624 | tf_op jit(solution)/shard_map/all_gather | solution.py:330
  396.7 17.5 %all-gather.28.cloned.1.call-done = bf16[1024,1024]{1,0:T(8,128)(2,1)} async-done(((bf16[128,1024]{1,0:T(8,128)(2,1)}), bf16[1024,1024]{1,0:T(8,128)(2,1)}) %all-gather.28.cloned.1.call-update) | async-done | bytes 2097168 | tf_op jit(solution)/shard_map/all_gather | solution.py:342
  414.2 22.2 %fusion.143 = (f32[1024]{0:T(1024)S(1)}, f32[1024,6288]{0,1:T(8,128)}) fusion(bf16[1024,1024]{1,0:T(8,128)(2,1)} %all-gather.28.cloned.1.call-done, bf16[6288,1024]{1,0:T(8,128)(2,1)} %param.33), kind=kOutput, calls=%fused_computation.209 | convolution fusion | flops 13193329664 | bytes 40734720 | tf_op jit(solution)/shard_map/while/body/eval_jaxpr/dot_general | solution.py:38
  462.1 14.0 all-gather.1
  495.8 15.3 %all-reduce.2 = (f32[8]{0:T(128)S(1)}, f32[8]{0:T(128)S(1)}) all-reduce(f32[8]{0:T(128)S(1)} %dynamic-update-slice, f32[8]{0:T(128)S(1)} %dynamic-update-slice.1), channel_id=1, replica_groups=mesh['pb'=4,'pa'=8] {'pa'}, use_global_device_ids=true, to_apply=%add | all-reduce | flops 16 | bytes 128
  511.2 18.5 %while.48 = (s32[]{:T(128)}, f32[1]{0:T(128)}, f32[1]{0:T(128)}, f32[8,1]{0,1:T(1,128)S(1)}, f32[8,1]{0,1:T(1,128)S(1)}, /*index=5*/s32[]{:T(128)}, s32[]{:T(128)}, s32[]{:T(128)}) while((s32[]{:T(128)}, f32[1]{0:T(128)}, f32[1]{0:T(128)}, f32[8,1]{0,1:T(1,128)S(1)}, f32[8,1]{0,1:T(1,128)S(1)}, /*index=5*/s32[]{:T(128)}, s32[]{:T(128)}, ...), condition=%wide.region_19.20_spmd, body=%wide.region_18.19_spmd.sunk | while | flops 11 | bytes 243 | solution.py:23
  538.8 23.2 %convolution_convert_fusion.5 = bf16[1024,1024]{1,0:T(8,128)(2,1)} fusion(bf16[6288,1024]{1,0:T(8,128)(2,1)} %param.33, f32[1024,6288]{0,1:T(8,128)} %get-tuple-element.509, f32[1024]{0:T(1024)S(1)} %log_add_fusion.2, f32[1024]{0:T(1024)S(1)} %bitcast.342, s32[1024]{0:T(1024)S(1)} %bitcast.331, s32[6288]{0:T(1024)S(1)} %iota_add_fusion), kind=kOutput, calls=%fused_computation.89 | convolution fusion | flops 13226573824 | bytes 40768064 | tf_op jit(solution)/shard_map/while/body/eval_jaxpr/dot_general | solution.py:29
  562.2 35.4 %reduce-scatter.19.cloned.1.call-done = bf16[128,1024]{1,0:T(8,128)(2,1)} async-done(((bf16[1024,1024]{1,0:T(8,128)(2,1)}), bf16[128,1024]{1,0:T(8,128)(2,1)}) %reduce-scatter.19.cloned.1.call-update) | async-done | bytes 262160 | tf_op jit(solution)/shard_map/reduce_scatter | solution.py:413
  709.8 22.6 %convolution_convert_fusion = bf16[6288,1024]{1,0:T(8,128)(2,1)} fusion(bf16[1024,1024]{1,0:T(8,128)(2,1)} %all-gather.28.cloned.1.call-done, f32[1024,6288]{0,1:T(8,128)} %get-tuple-element.509, f32[1024]{0:T(1024)S(1)} %log_add_fusion.2, f32[1024]{0:T(1024)S(1)} %bitcast.343, s32[1024]{0:T(1024)S(1)} %bitcast.332, s32[6288]{0:T(1024)S(1)} %iota_add_fusion), kind=kOutput, calls=%fused_computation.15 | convolution fusion | flops 13231964160 | bytes 40768064 | tf_op jit(solution)/shard_map/while/body/eval_jaxpr/dot_general | solution.py:49
  734.5 35.7 %reduce-scatter.31.cloned.1.call-done = bf16[128,3072]{1,0:T(8,128)(2,1)} async-done(((bf16[1024,3072]{1,0:T(8,128)(2,1)}), bf16[128,3072]{1,0:T(8,128)(2,1)}) %reduce-scatter.31.cloned.1.call-update) | async-done | bytes 786448
  772.5 34.6 %reduce-scatter.21.cloned.1.call-done = bf16[128,1024]{1,0:T(8,128)(2,1)} async-done(((bf16[1024,1024]{1,0:T(8,128)(2,1)}), bf16[128,1024]{1,0:T(8,128)(2,1)}) %reduce-scatter.21.cloned.1.call-update) | async-done | bytes 262160 | tf_op jit(solution)/shard_map/reduce_scatter | solution.py:422
  807.1 37.3 %reduce-scatter.23.cloned.1.call-done = bf16[128,1024]{1,0:T(8,128)(2,1)} async-done(((bf16[1024,1024]{1,0:T(8,128)(2,1)}), bf16[128,1024]{1,0:T(8,128)(2,1)}) %reduce-scatter.23.cloned.1.call-update) | async-done | bytes 262160 | tf_op jit(solution)/shard_map/reduce_scatter | solution.py:423
  844.4 37.2 %reduce-scatter.25.cloned.1.call-done = bf16[128,1024]{1,0:T(8,128)(2,1)} async-done(((bf16[1024,1024]{1,0:T(8,128)(2,1)}), bf16[128,1024]{1,0:T(8,128)(2,1)}) %reduce-scatter.25.cloned.1.call-update) | async-done | bytes 262160 | tf_op jit(solution)/shard_map/reduce_scatter | solution.py:425
  881.5 90.4 %reduce-scatter.27.cloned.1.call-done = bf16[128,4096]{1,0:T(8,128)(2,1)} async-done(((bf16[1024,4096]{1,0:T(8,128)(2,1)}), bf16[128,4096]{1,0:T(8,128)(2,1)}) %reduce-scatter.27.cloned.1.call-update) | async-done | bytes 1048592 | tf_op jit(solution)/shard_map/reduce_scatter | solution.py:426
  972.0 90.1 %reduce-scatter.29.cloned.1.call-done = bf16[512,1024]{1,0:T(8,128)(2,1)} async-done(((bf16[4096,1024]{1,0:T(8,128)(2,1)}), bf16[512,1024]{1,0:T(8,128)(2,1)}) %reduce-scatter.29.cloned.1.call-update) | async-done | bytes 1048592 | tf_op jit(solution)/shard_map/reduce_scatter | solution.py:427
  1095.0 31.1 %reduce-scatter.37.cloned.1.call-done = f32[128,3]{1,0:T(8,128)} async-done(((f32[1024,3]{1,0:T(8,128)}), f32[128,3]{1,0:T(8,128)}) %reduce-scatter.37.cloned.1.call-update) | async-done | bytes 1552
  1145.0 303.4 %all-reduce.7.cloned.1.call-done = (bf16[128,3072]{0,1:T(8,128)(2,1)}, bf16[128,2048]{0,1:T(8,128)(2,1)}, bf16[128,1024]{1,0:T(8,128)(2,1)}, bf16[128,1024]{1,0:...) async-done(((bf16[128,3072]{0,1:T(8,128)(2,1)}, bf16[128,2048]{0,1:T(8,128)(2,1)}, ...) | async-done | bytes 17072144 | tf_op jit(solution)/shard_map/psum | solution.py:431
  1457.9 14.7 convert_element_type.297
  (358 shorter events, 339.5 us)
Async XLA Ops:
  7.2 52.4 %copy-start = (bf16[1,2,512,1024]{3,2,1,0:T(8,128)(2,1)S(1)}, bf16[1,2,512,1024]{3,2,1,0:T(8,128)(2,1)}, u32[]{:S(2)}) copy-start(bf16[1,2,512,1024]{3,2,1,0:T(8,128)(2,1)} %param.21) | copy-start | bytes 6291460
  7.2 52.4 %all-gather.18.cloned.1.call-start = ((), (), s32[]{:S(2)}) async-start(), calls=%async_computation.12 | async-start | bytes 4718592 | tf_op jit(solution)/shard_map/all_gather | solution.py:327
  8.0 116.8 %all-gather.14.cloned.1.call-start = ((), (), s32[]{:S(2)}) async-start(), calls=%async_computation.10 | async-start | bytes 7077888 | tf_op jit(solution)/shard_map/all_gather | solution.py:324
  8.7 145.4 %all-gather.16.cloned.1.call-start = ((), (), s32[]{:S(2)}) async-start(), calls=%async_computation.11 | async-start | bytes 2359296 | tf_op jit(solution)/shard_map/all_gather | solution.py:325
  9.4 174.8 %all-gather.20.cloned.1.call-start = ((), (), s32[]{:S(2)}) async-start(), calls=%async_computation.13 | async-start | bytes 2359296 | tf_op jit(solution)/shard_map/all_gather | solution.py:326
  10.0 204.3 %all-gather.22.cloned.1.call-start = ((), (), s32[]{:S(2)}) async-start(), calls=%async_computation.14 | async-start | bytes 2359296 | tf_op jit(solution)/shard_map/all_gather | solution.py:328
  10.6 286.7 %all-gather.24.cloned.1.call-start = ((), (), s32[]{:S(2)}) async-start(), calls=%async_computation.15 | async-start | bytes 9437184 | tf_op jit(solution)/shard_map/all_gather | solution.py:329
  11.2 368.4 %all-gather.26.cloned.1.call-start = ((), (), s32[]{:S(2)}) async-start(), calls=%async_computation.16 | async-start | bytes 9437184 | tf_op jit(solution)/shard_map/all_gather | solution.py:330
  11.9 402.2 %all-gather.28.cloned.1.call-start = ((), (), s32[]{:S(2)}) async-start(), calls=%async_computation.17 | async-start | bytes 2359296 | tf_op jit(solution)/shard_map/all_gather | solution.py:342
  303.1 81.6 %copy-start.54 = (u8[64,4096]{1,0:T(8,128)(4,1)}, u8[64,4096]{1,0:T(8,128)(4,1)S(1)}, u32[]{:S(2)}) copy-start(u8[64,4096]{1,0:T(8,128)(4,1)S(1)} %get-tuple-element.425) | copy-start | bytes 786436
  310.4 76.0 %copy-start.67 = (s32[1,2,64]{2,1,0:T(2,128)S(1)}, s32[1,2,64]{2,1,0:T(2,128)}, u32[]{:S(2)}) copy-start(s32[1,2,64]{2,1,0:T(2,128)} %param.22) | copy-start | bytes 1540
  310.4 76.8 %copy-start.68 = (u32[32]{0:T(128)S(1)}, u32[32]{0:T(128)}, u32[]{:S(2)}) copy-start(u32[32]{0:T(128)} %constant.248) | copy-start | bytes 388
  386.4 211.3 %reduce-scatter.19.cloned.1.call-start = ((), (), s32[]{:S(2)}) async-start(), calls=%async_computation.18 | async-start | bytes 2359296 | tf_op jit(solution)/shard_map/reduce_scatter | solution.py:413
  562.0 170.4 %reduce-scatter.33.cloned.1.call-start = ((), (), s32[]{:S(2)}) async-start(), calls=%async_computation.25 | async-start | bytes 4718592
  651.5 118.7 %reduce-scatter.31.cloned.1.call-start = ((), (), s32[]{:S(2)}) async-start(), calls=%async_computation.24 | async-start | bytes 7077888
  684.4 122.7 %reduce-scatter.21.cloned.1.call-start = ((), (), s32[]{:S(2)}) async-start(), calls=%async_computation.19 | async-start | bytes 2359296 | tf_op jit(solution)/shard_map/reduce_scatter | solution.py:422
  688.3 156.1 %reduce-scatter.23.cloned.1.call-start = ((), (), s32[]{:S(2)}) async-start(), calls=%async_computation.20 | async-start | bytes 2359296 | tf_op jit(solution)/shard_map/reduce_scatter | solution.py:423
  691.3 190.2 %reduce-scatter.25.cloned.1.call-start = ((), (), s32[]{:S(2)}) async-start(), calls=%async_computation.21 | async-start | bytes 2359296 | tf_op jit(solution)/shard_map/reduce_scatter | solution.py:425
  694.4 277.5 %reduce-scatter.27.cloned.1.call-start = ((), (), s32[]{:S(2)}) async-start(), calls=%async_computation.22 | async-start | bytes 9437184 | tf_op jit(solution)/shard_map/reduce_scatter | solution.py:426
  700.2 361.9 %reduce-scatter.29.cloned.1.call-start = ((), (), s32[]{:S(2)}) async-start(), calls=%async_computation.23 | async-start | bytes 9437184 | tf_op jit(solution)/shard_map/reduce_scatter | solution.py:427
  707.5 386.5 %reduce-scatter.35.cloned.1.call-start = ((), (), s32[]{:S(2)}) async-start(), calls=%async_computation.26 | async-start | bytes 589824
  708.7 417.4 %reduce-scatter.37.cloned.1.call-start = ((), (), s32[]{:S(2)}) async-start(), calls=%async_computation.27 | async-start | bytes 589824
  709.8 738.6 %all-reduce.7.cloned.1.call-start = ((), (), s32[]{:S(2)}) async-start(), calls=%async_computation.28 | async-start | bytes 34144256 | tf_op jit(solution)/shard_map/psum | solution.py:431
  1071.9 55.0 %copy-start.50 = (f32[2,64,1024]{2,1,0:T(8,128)S(1)}, f32[2,64,1024]{2,1,0:T(8,128)}, u32[]{:S(2)}) copy-start(f32[2,64,1024]{2,1,0:T(8,128)} %copy-done.49) | copy-start | bytes 1572868
  (64 other events, 402.0 us)
Sparse Core Ops, SparseCore 0:
  9.7 49.8 all-gather.17
  61.2 63.4 all-gather.13
  126.3 27.7 all-gather.15
  155.6 28.5 all-gather.19
  185.7 28.5 all-gather.21
  215.7 81.5 all-gather.23
  298.9 80.5 all-gather.25
  386.5 27.6 all-gather.27
  562.1 35.4 reduce-scatter.18
  651.6 48.2 reduce-scatter.32
  702.2 67.9 reduce-scatter.30
  772.9 34.1 reduce-scatter.20
  810.0 34.3 reduce-scatter.22
  847.1 34.3 reduce-scatter.24
  883.7 88.2 reduce-scatter.26
  974.1 87.9 reduce-scatter.28
  1064.8 29.2 reduce-scatter.34
  1096.8 29.1 reduce-scatter.36
  1131.2 317.2 all-reduce.6

commit v2 on v1

--- a/solution.py
+++ b/solution.py
@@ -1,8 +1,11 @@
+import functools
 import math
 
 import jax
 import jax.numpy as jnp
 from jax import lax
+from jax.experimental import pallas as pl
+from jax.experimental.pallas import tpu as pltpu
 from jax.sharding import PartitionSpec as P
 
 HEADS = 16
@@ -12,6 +15,939 @@
 EPSILON = 1e-05
 NEGATIVE = -1e30
 BFLOAT = jnp.bfloat16
+MESH = pl.DeviceIdType.MESH
+TILE = 1024
+ROWS = 128
+WEIGHT_UNITS = (3, 1, 1, 2, 1, 4, 4)
+UNITS = tuple((w, k) for w, n in enumerate(WEIGHT_UNITS) for k in range(n))
+REDUCE_WEIGHT = 6
+
+
+def whereami():
+    pb = lax.axis_index("pb")
+    pa = lax.axis_index("pa")
+    return lax.rem(pb, 2), pb // 2, pa // 2, lax.rem(pa, 2)
+
+
+def greet(peers):
+    barrier = pltpu.get_barrier_semaphore()
+    for peer in peers:
+        pl.semaphore_signal(barrier, inc=1, device_id=peer, device_id_type=MESH)
+    pl.semaphore_wait(barrier, len(peers))
+
+
+def at(x, y, z, c):
+    return (y * 2 + x, z * 2 + c)
+
+
+def neighbours(x, y, z, c):
+    return [at(1 - x, y, z, c), at(x, 1 - y, z, c), at(x, y, z, 1 - c)] + [
+        at(x, y, lax.rem(z + d, 4), c) for d in (1, 2, 3)
+    ]
+
+
+def shard_view(ref, unit, start, size):
+    weight, block = unit
+    if weight == REDUCE_WEIGHT:
+        return ref.at[pl.ds(block * ROWS + start, size), :]
+    return ref.at[pl.ds(start, size), pl.ds(block * TILE, TILE)]
+
+
+def full_view(ref, unit, place, core, start, size):
+    weight, block = unit
+    if weight == REDUCE_WEIGHT:
+        return ref.at[place, core, block, pl.ds(start, size), :]
+    return ref.at[place, core, pl.ds(start, size), pl.ds(block * TILE, TILE)]
+
+
+Z_FULL = (9, 14)
+
+
+def gather_kernel(*refs):
+    shards, norm, fulls, norm_full = refs[:7], refs[7], refs[8:15], refs[15]
+    (
+        local_sem, z_send, z_recv, one_send, one_recv, two_send, two_recv, d_send, d_recv,
+        norm_sem, nz_send, nz_recv, nd_send, nd_recv,
+    ) = refs[16:]
+    x, y, z, c = whereami()
+    greet(neighbours(x, y, z, c))
+    every = slice(None)
+
+    def copies(u):
+        unit = UNITS[u]
+        shard, full = shards[unit[0]], fulls[unit[0]]
+        wide = u in Z_FULL
+        a, b = (x, y) if u % 2 == 0 else (y, x)
+        first_peer = at(x, 1 - y, z, c) if u % 2 == 0 else at(1 - x, y, z, c)
+        second_peer = at(1 - x, y, z, c) if u % 2 == 0 else at(x, 1 - y, z, c)
+        quarter = pl.multiple_of(64 * a + 32 * b, 32)
+        half = pl.multiple_of(64 * a, 64)
+        rows = (0, ROWS) if wide else (quarter, 32)
+        local = pltpu.make_async_copy(
+            shard_view(shard, unit, *rows), full_view(full, unit, z, c, *rows), local_sem.at[u]
+        )
+        along = [
+            pltpu.make_async_remote_copy(
+                src_ref=shard_view(shard, unit, *rows),
+                dst_ref=full_view(full, unit, z, c, *rows),
+                send_sem=z_send.at[u, d - 1],
+                recv_sem=z_recv.at[u, d - 1],
+                device_id=at(x, y, lax.rem(z + d, 4), c),
+                device_id_type=MESH,
+            )
+            for d in (1, 2, 3)
+        ]
+
+        def cross(start, size, sends, recvs, peer):
+            part = full_view(full, unit, every, c, start, size)
+            return pltpu.make_async_remote_copy(
+                src_ref=part,
+                dst_ref=part,
+                send_sem=sends.at[u],
+                recv_sem=recvs.at[u],
+                device_id=peer,
+                device_id_type=MESH,
+            )
+
+        first = None if wide else cross(quarter, 32, one_send, one_recv, first_peer)
+        second = None if wide else cross(half, 64, two_send, two_recv, second_peer)
+        sibling = cross(0, ROWS, d_send, d_recv, at(x, y, z, 1 - c))
+        return local, along, first, second, sibling
+
+    def norm_copy(src, dst, send, recv, peer):
+        return pltpu.make_async_remote_copy(
+            src_ref=src, dst_ref=dst, send_sem=send, recv_sem=recv, device_id=peer, device_id_type=MESH
+        )
+
+    norm_local = pltpu.make_async_copy(norm, norm_full.at[z, c], norm_sem)
+    norm_along = [
+        norm_copy(
+            norm, norm_full.at[z, c], nz_send.at[d - 1], nz_recv.at[d - 1], at(x, y, lax.rem(z + d, 4), c)
+        )
+        for d in (1, 2, 3)
+    ]
+    norm_sibling = norm_copy(
+        norm_full.at[:, c], norm_full.at[:, c], nd_send, nd_recv, at(x, y, z, 1 - c)
+    )
+    norm_local.start()
+    for copy in norm_along:
+        copy.start()
+    count = len(UNITS)
+    every_copy = [copies(u) for u in range(count)]
+    for local, along, _, _, _ in every_copy:
+        local.start()
+        for copy in along:
+            copy.start()
+    norm_local.wait()
+    for copy in norm_along:
+        copy.wait()
+    norm_sibling.start()
+    norm_sibling.wait()
+    lag_two, lag_sibling = 2, 4
+    for i in range(count + lag_sibling):
+        if i < count:
+            local, along, first, _, _ = every_copy[i]
+            local.wait()
+            for copy in along:
+                copy.wait_recv()
+            if first is not None:
+                first.start()
+        if 0 <= i - lag_two < count:
+            _, _, first, second, _ = every_copy[i - lag_two]
+            if first is not None:
+                first.wait_recv()
+                second.start()
+        if 0 <= i - lag_sibling < count:
+            _, _, _, second, sibling = every_copy[i - lag_sibling]
+            if second is not None:
+                second.wait_recv()
+            sibling.start()
+    for _, along, first, second, sibling in every_copy:
+        for copy in along:
+            copy.wait_send()
+        if first is not None:
+            first.wait_send()
+            second.wait_send()
+        sibling.wait()
+
+
+def gather_weights(weights, norm):
+    count = len(UNITS)
+    shapes = []
+    for w, weight in enumerate(weights):
+        if w == REDUCE_WEIGHT:
+            shapes.append((4, 2, weight.shape[0] // ROWS, ROWS, weight.shape[1]))
+        else:
+            shapes.append((4, 2) + weight.shape)
+    *fulls, norm_full = pl.pallas_call(
+        gather_kernel,
+        out_shape=tuple(jax.ShapeDtypeStruct(shape, BFLOAT) for shape in shapes)
+        + (jax.ShapeDtypeStruct((4, 2) + norm.shape, norm.dtype),),
+        in_specs=[pl.BlockSpec(memory_space=pl.ANY)] * 8,
+        out_specs=(pl.BlockSpec(memory_space=pl.ANY),) * 8,
+        scratch_shapes=[
+            pltpu.SemaphoreType.DMA((count,)),
+            pltpu.SemaphoreType.DMA((count, 3)),
+            pltpu.SemaphoreType.DMA((count, 3)),
+        ]
+        + [pltpu.SemaphoreType.DMA((count,))] * 6
+        + [pltpu.SemaphoreType.DMA]
+        + [pltpu.SemaphoreType.DMA((3,))] * 2
+        + [pltpu.SemaphoreType.DMA] * 2,
+        compiler_params=pltpu.CompilerParams(collective_id=0, has_side_effects=True),
+        name="gather_weights",
+    )(*weights, norm)
+    norm_full = norm_full.reshape(8, norm.shape[0], norm.shape[1]).transpose(1, 0, 2)
+    return (
+        tuple(full.reshape(-1, full.shape[-1]) for full in fulls),
+        norm_full.reshape(norm.shape[0], -1),
+    )
+
+
+LAGS = (0, 2, 4, 6, 8, 10)
+
+
+def reduce_kernel(*refs):
+    grads, norm, outs, norm_out = refs[:7], refs[7], refs[8:15], refs[15]
+    (
+        own, got, one, two, line, done, norm_here, norm_there, norm_line,
+        own_sem, d_send, d_recv, one_send, one_recv, two_send, two_recv,
+        z_send, z_recv, ag_send, ag_recv, ah_send, ah_recv, out_sem,
+        n_send, n_recv, nz_send, nz_recv,
+    ) = refs[16:]
+    x, y, z, c = whereami()
+    greet(neighbours(x, y, z, c))
+    count = len(UNITS)
+    every = slice(None)
+
+    def sibling_copy(u):
+        return pltpu.make_async_remote_copy(
+            src_ref=full_view(grads[UNITS[u][0]], UNITS[u], every, 1 - c, 0, ROWS),
+            dst_ref=got.at[u],
+            send_sem=d_send.at[u],
+            recv_sem=d_recv.at[u],
+            device_id=at(x, y, z, 1 - c),
+            device_id_type=MESH,
+        )
+
+    def own_copy(u):
+        return pltpu.make_async_copy(
+            full_view(grads[UNITS[u][0]], UNITS[u], every, c, 0, ROWS),
+            own.at[u % 2],
+            own_sem.at[u % 2],
+        )
+
+    for u in range(count):
+        sibling_copy(u).start()
+    own_copy(0).start()
+
+    def place(u):
+        even = lax.rem(u, 2) == 0
+        a = jnp.where(even, x, y)
+        b = jnp.where(even, y, x)
+        x_peer = y * 2 + (1 - x)
+        y_peer = (1 - y) * 2 + x
+        a_peer = (jnp.where(even, x_peer, y_peer), z * 2 + c)
+        b_peer = (jnp.where(even, y_peer, x_peer), z * 2 + c)
+        return a, b, a_peer, b_peer
+
+    def remote(src, dst, send, recv, peer):
+        return pltpu.make_async_remote_copy(
+            src_ref=src, dst_ref=dst, send_sem=send, recv_sem=recv, device_id=peer, device_id_type=MESH
+        )
+
+    def one_copy(u):
+        a, _, a_peer, _ = place(u)
+        return remote(
+            got.at[u, :, pl.ds(pl.multiple_of(64 * (1 - a), 64), 64), :],
+            one.at[u], one_send.at[u], one_recv.at[u], a_peer,
+        )
+
+    def two_copy(u):
+        _, b, _, b_peer = place(u)
+        return remote(
+            one.at[u, :, pl.ds(pl.multiple_of(32 * (1 - b), 32), 32), :],
+            two.at[u], two_send.at[u], two_recv.at[u], b_peer,
+        )
+
+    def line_copy(u, d):
+        other = lax.rem(z + d, 4)
+        return remote(
+            two.at[u, other], line.at[u, d - 1], z_send.at[u, d - 1], z_recv.at[u, d - 1],
+            at(x, y, other, c),
+        )
+
+    def ag_copy(u):
+        a, b, _, b_peer = place(u)
+        part = done.at[u, pl.ds(pl.multiple_of(64 * a + 32 * b, 32), 32), :]
+        return remote(part, part, ag_send.at[u], ag_recv.at[u], b_peer)
+
+    def ah_copy(u):
+        a, _, a_peer, _ = place(u)
+        part = done.at[u, pl.ds(pl.multiple_of(64 * a, 64), 64), :]
+        return remote(part, part, ah_send.at[u], ah_recv.at[u], a_peer)
+
+    norm_peers = (at(x, y, z, 1 - c), at(1 - x, y, z, c), at(x, 1 - y, z, c))
+
+    def norm_copy(n):
+        return remote(norm_here.at[n], norm_there.at[n], n_send.at[n], n_recv.at[n], norm_peers[n])
+
+    def norm_line_copy(d):
+        return remote(
+            norm_here.at[3], norm_line.at[d - 1], nz_send.at[d - 1], nz_recv.at[d - 1],
+            at(x, y, lax.rem(z + d, 4), c),
+        )
+
+    norm_here[0] = norm[...]
+    norm_copy(0).start()
+
+    def out_copy(u):
+        return pltpu.make_async_copy(
+            done.at[u], shard_view(outs[UNITS[u][0]], UNITS[u], 0, ROWS), out_sem.at[u]
+        )
+
+    def total(*parts):
+        out = parts[0].astype(jnp.float32)
+        for part in parts[1:]:
+            out = out + part.astype(jnp.float32)
+        return out.astype(BFLOAT)
+
+    @pl.loop(0, count + LAGS[-1])
+    def _(i):
+        u0 = i
+        for k in range(1, count):
+            @pl.when(i + 1 == k)
+            def _():
+                own_copy(k).start()
+
+        @pl.when(i < count)
+        def _():
+            for k in range(count):
+                @pl.when(i == k)
+                def _():
+                    own_copy(k).wait()
+                    sibling_copy(k).wait_recv()
+
+            slot = lax.rem(u0, 2)
+
+            @pl.loop(0, 32)
+            def _(j):
+                zz, r = j // 8, pl.multiple_of(lax.rem(j, 8) * 16, 16)
+                got[u0, zz, pl.ds(r, 16), :] = total(
+                    got[u0, zz, pl.ds(r, 16), :], own[slot, zz, pl.ds(r, 16), :]
+                )
+
+            one_copy(u0).start()
+
+        for n in range(3):
+            @pl.when(i == 2 + 2 * n)
+            def _():
+                norm_copy(n).wait_recv()
+                norm_here[n + 1] = norm_here[n] + norm_there[n]
+                if n < 2:
+                    norm_copy(n + 1).start()
+                else:
+                    for d in (1, 2, 3):
+                        norm_line_copy(d).start()
+
+        @pl.when(i == 9)
+        def _():
+            for d in (1, 2, 3):
+                norm_line_copy(d).wait_recv()
+            norm_out[...] = ((norm_here[3] + norm_line[0]) + norm_line[1]) + norm_line[2]
+
+        u1 = i - LAGS[1]
+
+        @pl.when((u1 >= 0) & (u1 < count))
+        def _():
+            one_copy(u1).wait_recv()
+            a, _, _, _ = place(u1)
+
+            @pl.loop(0, 16)
+            def _(j):
+                zz, r = j // 4, pl.multiple_of(lax.rem(j, 4) * 16, 16)
+                one[u1, zz, pl.ds(r, 16), :] = total(
+                    one[u1, zz, pl.ds(r, 16), :],
+                    got[u1, zz, pl.ds(pl.multiple_of(64 * a + r, 16), 16), :],
+                )
+
+            two_copy(u1).start()
+
+        u2 = i - LAGS[2]
+
+        @pl.when((u2 >= 0) & (u2 < count))
+        def _():
+            two_copy(u2).wait_recv()
+            _, b, _, _ = place(u2)
+
+            @pl.loop(0, 8)
+            def _(j):
+                zz, r = j // 2, pl.multiple_of(lax.rem(j, 2) * 16, 16)
+                two[u2, zz, pl.ds(r, 16), :] = total(
+                    two[u2, zz, pl.ds(r, 16), :],
+                    one[u2, zz, pl.ds(pl.multiple_of(32 * b + r, 16), 16), :],
+                )
+
+            for d in (1, 2, 3):
+                line_copy(u2, d).start()
+
+        u3 = i - LAGS[3]
+
+        @pl.when((u3 >= 0) & (u3 < count))
+        def _():
+            for d in (1, 2, 3):
+                line_copy(u3, d).wait_recv()
+            a, b, _, _ = place(u3)
+
+            @pl.loop(0, 2)
+            def _(j):
+                r = pl.multiple_of(j * 16, 16)
+                done[u3, pl.ds(pl.multiple_of(64 * a + 32 * b + r, 16), 16), :] = total(
+                    two[u3, z, pl.ds(r, 16), :],
+                    line[u3, 0, pl.ds(r, 16), :],
+                    line[u3, 1, pl.ds(r, 16), :],
+                    line[u3, 2, pl.ds(r, 16), :],
+                )
+
+            ag_copy(u3).start()
+
+        u4 = i - LAGS[4]
+
+        @pl.when((u4 >= 0) & (u4 < count))
+        def _():
+            ag_copy(u4).wait_recv()
+            ah_copy(u4).start()
+
+        u5 = i - LAGS[5]
+
+        @pl.when((u5 >= 0) & (u5 < count))
+        def _():
+            ah_copy(u5).wait_recv()
+            for k in range(count):
+                @pl.when(u5 == k)
+                def _():
+                    out_copy(k).start()
+
+    for u in range(count):
+        sibling_copy(u).wait_send()
+
+    @pl.loop(0, count)
+    def _(u):
+        one_copy(u).wait_send()
+        two_copy(u).wait_send()
+        for d in (1, 2, 3):
+            line_copy(u, d).wait_send()
+        ag_copy(u).wait_send()
+        ah_copy(u).wait_send()
+
+    for u in range(count):
+        out_copy(u).wait()
+    for n in range(3):
+        norm_copy(n).wait_send()
+        norm_line_copy(n + 1).wait_send()
+
+
+def reduce_grads(grads, norm):
+    count = len(UNITS)
+    views = []
+    shapes = []
+    for w, grad in enumerate(grads):
+        rows, columns = grad.shape[0] // 8, grad.shape[1]
+        shapes.append((rows, columns))
+        if w == REDUCE_WEIGHT:
+            views.append(grad.reshape(4, 2, rows // ROWS, ROWS, columns))
+        else:
+            views.append(grad.reshape(4, 2, rows, columns))
+    sems = pltpu.SemaphoreType.DMA((count,))
+    every = pl.BlockSpec(memory_space=pl.ANY)
+    vmem = pl.BlockSpec(memory_space=pltpu.VMEM)
+    *shares, norm_sum = pl.pallas_call(
+        reduce_kernel,
+        out_shape=tuple(jax.ShapeDtypeStruct(shape, BFLOAT) for shape in shapes)
+        + (jax.ShapeDtypeStruct(norm.shape, norm.dtype),),
+        in_specs=[every] * 7 + [vmem],
+        out_specs=(every,) * 7 + (vmem,),
+        scratch_shapes=[
+            pltpu.VMEM((2, 4, ROWS, TILE), BFLOAT),
+            pltpu.VMEM((count, 4, ROWS, TILE), BFLOAT),
+            pltpu.VMEM((count, 4, 64, TILE), BFLOAT),
+            pltpu.VMEM((count, 4, 32, TILE), BFLOAT),
+            pltpu.VMEM((count, 3, 32, TILE), BFLOAT),
+            pltpu.VMEM((count, ROWS, TILE), BFLOAT),
+            pltpu.VMEM((4,) + norm.shape, norm.dtype),
+            pltpu.VMEM((3,) + norm.shape, norm.dtype),
+            pltpu.VMEM((3,) + norm.shape, norm.dtype),
+            pltpu.SemaphoreType.DMA((2,)),
+            sems, sems, sems, sems, sems, sems,
+            pltpu.SemaphoreType.DMA((count, 3)),
+            pltpu.SemaphoreType.DMA((count, 3)),
+            sems, sems, sems, sems, sems,
+        ]
+        + [pltpu.SemaphoreType.DMA((3,))] * 4,
+        compiler_params=pltpu.CompilerParams(
+            collective_id=1, has_side_effects=True, vmem_limit_bytes=48 * 2**20
+        ),
+        name="reduce_grads",
+    )(*views, norm)
+    return tuple(share.astype(jnp.float32) for share in shares), norm_sum
+
+VOCAB_CUTS = 3
+
+
+def head_kernel(slots, length, vocab_here, *refs):
+    hid, aux, emb, emb_t = refs[:4]
+    small_out, gemb_out, third_out = refs[4:7]
+    (
+        held, marks, logit, expo, part, sib_part, part_one, part_two, part_z,
+        mine, theirs, lined, prior, usable, weight, scaled, picked_grad,
+    ) = refs[7:24]
+    (
+        local_sem, z_send, z_recv, one_send, one_recv, two_send, two_recv, sib_send, sib_recv,
+        ax_send, ax_recv, axz_send, axz_recv, st_send, st_recv, stz_send, stz_recv,
+        dd_send, dd_recv, r1_send, r1_recv, r2_send, r2_recv, rz_send, rz_recv,
+    ) = refs[24:]
+    x, y, z, c = whereami()
+    pb, pa = y * 2 + x, z * 2 + c
+    size = hid.shape[0]
+    pair = 2 * size
+    width = hid.shape[1]
+    rows = emb.shape[0]
+    cut = rows // VOCAB_CUTS
+    start = jnp.minimum(pb * rows, vocab_here - rows)
+    skip = pb * rows - start
+    base = pa * vocab_here + start
+    own = pb * 4 + z
+
+    def remote(src, dst, send, recv, peer):
+        return pltpu.make_async_remote_copy(
+            src_ref=src, dst_ref=dst, send_sem=send, recv_sem=recv, device_id=peer, device_id_type=MESH
+        )
+
+    sibling = at(x, y, z, 1 - c)
+    x_peer, y_peer = at(1 - x, y, z, c), at(x, 1 - y, z, c)
+
+    def spot(k, core):
+        return held.at[pl.ds(pl.multiple_of((k * 2 + core) * size, size), size), :]
+
+    greet(neighbours(x, y, z, c))
+    own_copy = pltpu.make_async_copy(hid, spot(own, c), local_sem.at[0])
+    own_copy.start()
+    lanes = pl.ds(pl.multiple_of(c * size, size), size)
+    aux_copy = pltpu.make_async_copy(aux, marks.at[y, x, z, :, lanes], local_sem.at[1])
+    aux_copy.start()
+    own_copy.wait()
+
+    def along_copy(d):
+        other = lax.rem(z + d, 4)
+        return remote(hid, spot(own, c), z_send.at[d - 1], z_recv.at[d - 1], at(x, y, other, c))
+
+    def sib_copy(k):
+        return remote(spot(k, c), spot(k, c), sib_send.at[k], sib_recv.at[k], sibling)
+
+    def order(zz):
+        x_first = zz < 2
+        f = jnp.where(x_first, x, y)
+        g = jnp.where(x_first, y, x)
+        first_peer = (jnp.where(x_first, y * 2 + 1 - x, (1 - y) * 2 + x), pa)
+        second_peer = (jnp.where(x_first, (1 - y) * 2 + x, y * 2 + 1 - x), pa)
+
+        def block(first, second):
+            return jnp.where(x_first, second * 2 + first, first * 2 + second) * 4 + zz
+
+        return f, g, first_peer, second_peer, block
+
+    def one_copy(zz):
+        f, g, first_peer, _, block = order(zz)
+        return remote(
+            spot(block(f, g), c), spot(block(f, g), c), one_send.at[zz], one_recv.at[zz], first_peer
+        )
+
+    def two_copy(zz, j):
+        f, g, _, second_peer, block = order(zz)
+        k = block(f if j == 0 else 1 - f, g)
+        return remote(spot(k, c), spot(k, c), two_send.at[zz, j], two_recv.at[zz, j], second_peer)
+
+    for d in (1, 2, 3):
+        along_copy(d).start()
+    sib_copy(own).start()
+    one_copy(z).start()
+
+    aux_copy.wait()
+    steps = (
+        (marks.at[y, x, z, :, lanes], sibling),
+        (marks.at[y, x, z], x_peer),
+        (marks.at[y, :, z], y_peer),
+    )
+    for n, (block_ref, peer) in enumerate(steps):
+        copy = remote(block_ref, block_ref, ax_send.at[n], ax_recv.at[n], peer)
+        copy.start()
+        copy.wait()
+
+    def mark_copy(d):
+        block_ref = marks.at[:, :, z]
+        other = lax.rem(z + d, 4)
+        return remote(block_ref, block_ref, axz_send.at[d - 1], axz_recv.at[d - 1], at(x, y, other, c))
+
+    for d in (1, 2, 3):
+        mark_copy(d).start()
+    for d in (1, 2, 3):
+        mark_copy(d).wait()
+
+    def target_rows(k):
+        ypart, xpart, zpart = k // 8, lax.rem(k // 4, 2), lax.rem(k, 4)
+        target = marks[ypart, xpart, zpart, 0:1, :].astype(jnp.int32) - base
+        return jnp.where(target >= skip, target, -1)
+
+    def row_numbers(j):
+        return lax.broadcasted_iota(jnp.int32, (cut, pair), 0) + j * cut
+
+    def cut_rows(j):
+        return pl.ds(pl.multiple_of(j * cut, cut), cut)
+
+    def token_lanes(k):
+        return pl.ds(pl.multiple_of(k * pair, pair), pair)
+
+    def forward_block(k):
+        target = target_rows(k)
+        block = held[token_lanes(k), :]
+
+        def scan_logits(j, carried):
+            highest, picked = carried
+            value = lax.dot_general(
+                emb[cut_rows(j), :], block, (((1,), (1,)), ((), ())), preferred_element_type=jnp.float32
+            )
+            number = row_numbers(j)
+            value = jnp.where(number >= skip, value, NEGATIVE)
+            logit[cut_rows(j), :] = value
+            return (
+                jnp.maximum(highest, jnp.max(value, 0, keepdims=True)),
+                picked + jnp.sum(jnp.where(number == target, value, 0.0), 0, keepdims=True),
+            )
+
+        highest, picked = lax.fori_loop(
+            0,
+            VOCAB_CUTS,
+            scan_logits,
+            (jnp.full((1, pair), NEGATIVE, jnp.float32), jnp.zeros((1, pair), jnp.float32)),
+        )
+
+        def scan_exp(j, total):
+            value = jnp.exp(logit[cut_rows(j), :] - highest)
+            expo[cut_rows(j), token_lanes(k)] = value.astype(BFLOAT)
+            return total + jnp.sum(value, 0, keepdims=True)
+
+        total = lax.fori_loop(0, VOCAB_CUTS, scan_exp, jnp.zeros((1, pair), jnp.float32))
+        mine[0, 0, pl.ds(k, 1), :] = highest
+        mine[0, 1, pl.ds(k, 1), :] = total
+        mine[0, 2, pl.ds(k, 1), :] = picked
+
+    @pl.loop(0, 16)
+    def _(s):
+        phase, t = s // 4, lax.rem(s, 4)
+        zz = lax.rem(z - t + 4, 4)
+        f, g, _, _, block = order(zz)
+        k = jnp.where(
+            phase == 0,
+            block(f, g),
+            jnp.where(
+                phase == 1, block(1 - f, g), jnp.where(phase == 2, block(f, 1 - g), block(1 - f, 1 - g))
+            ),
+        )
+
+        for d in (1, 2, 3):
+            @pl.when(s == d)
+            def _():
+                along_copy(d).wait_recv()
+
+        @pl.when((s > 0) & (phase == 0))
+        def _():
+            sib_copy(k).start()
+            one_copy(zz).start()
+
+        @pl.when(phase == 1)
+        def _():
+            one_copy(zz).wait_recv()
+            sib_copy(k).start()
+            for j in range(2):
+                two_copy(zz, j).start()
+
+        for j in range(2):
+            @pl.when(phase == 2 + j)
+            def _():
+                two_copy(zz, j).wait_recv()
+                sib_copy(k).start()
+
+        sib_copy(k).wait_recv()
+        forward_block(k)
+
+    def joined(parts):
+        highest = functools.reduce(jnp.maximum, [p[0] for p in parts])
+        total = functools.reduce(jnp.add, [p[1] * jnp.exp(p[0] - highest) for p in parts])
+        picked = functools.reduce(jnp.add, [p[2] for p in parts])
+        return highest, total, picked
+
+    def rows_of(ref, n):
+        return ref[n, 0], ref[n, 1], ref[n, 2]
+
+    for n, (peer, side) in enumerate(((sibling, c), (x_peer, x), (y_peer, y))):
+        copy = remote(mine.at[n], theirs.at[n], st_send.at[n], st_recv.at[n], peer)
+        copy.start()
+        copy.wait()
+        here, there = rows_of(mine, n), rows_of(theirs, n)
+        early = tuple(jnp.where(side == 0, a, b) for a, b in zip(here, there))
+        late = tuple(jnp.where(side == 0, b, a) for a, b in zip(here, there))
+        for r, value in enumerate(joined((early, late))):
+            mine[n + 1, r] = value
+
+    def stat_copy(d):
+        other = lax.rem(z + d, 4)
+        return remote(mine.at[3], lined.at[z], stz_send.at[d - 1], stz_recv.at[d - 1], at(x, y, other, c))
+
+    for d in (1, 2, 3):
+        stat_copy(d).start()
+    for r in range(3):
+        lined[z, r] = mine[3, r]
+    for d in (1, 2, 3):
+        stat_copy(d).wait()
+    highest, total, picked = joined([rows_of(lined, n) for n in range(4)])
+    logsum = highest + jnp.log(total)
+    log_probs = picked - logsum
+    for k in range(16):
+        prior[k : k + 1, :] = marks[k // 8, (k // 4) % 2, k % 4, 1:2, :]
+        usable[k : k + 1, :] = marks[k // 8, (k // 4) % 2, k % 4, 2:3, :]
+    lane = lax.broadcasted_iota(jnp.int32, (16, pair), 1) // length
+    mean = jnp.zeros((16, pair), jnp.float32)
+    for n in range(pair // length):
+        inside = lane == n
+        slot_sum = jnp.sum(jnp.where(inside, log_probs, 0.0), 1, keepdims=True)
+        mean = jnp.where(inside, slot_sum * (1.0 / length), mean)
+    scores = prior[...] + mean
+    counted = usable[...] > 0.5
+    masked = jnp.where(counted, scores, NEGATIVE)
+    question = lax.broadcasted_iota(jnp.int32, (16, pair), 0) // 4
+    marginal = jnp.zeros((16, pair), jnp.float32)
+    loss = jnp.zeros((1, 1), jnp.float32)
+    for n in range(4):
+        inside = question == n
+        high = jnp.max(
+            jnp.max(jnp.where(inside, masked, NEGATIVE), 1, keepdims=True), 0, keepdims=True
+        )
+        terms = jnp.where(inside & counted, jnp.exp(masked - high), 0.0)
+        mass = jnp.sum(jnp.sum(terms, 1, keepdims=True), 0, keepdims=True) * (1.0 / length)
+        value = high + jnp.log(mass)
+        marginal = jnp.where(inside, value, marginal)
+        loss = loss + value
+    posterior = jnp.where(counted, jnp.exp(scores - marginal), 0.0)
+    token_weight = -float(slots) * posterior
+    weight[...] = posterior
+    scaled[...] = token_weight * jnp.exp(mine[0, 0] - logsum)
+    picked_grad[...] = token_weight * (1.0 - jnp.exp(log_probs))
+    small_out[...] = jnp.broadcast_to(loss * (-1.0 / 4), small_out.shape)
+    own_row = weight[pl.ds(own, 1), :]
+    own_row = jnp.where(c == 0, own_row[:, :size], own_row[:, size:])
+    small_out[1:2, :] = own_row * (-float(slots * length))
+
+    def backward_block(k):
+        target = target_rows(k)
+        hit = picked_grad[pl.ds(k, 1), :]
+        scale = scaled[pl.ds(k, 1), :]
+
+        def make(j, carried):
+            value = expo[cut_rows(j), token_lanes(k)].astype(jnp.float32)
+            grad = jnp.where(row_numbers(j) == target, hit, -(value * scale))
+            expo[cut_rows(j), token_lanes(k)] = grad.astype(BFLOAT)
+            return carried
+
+        lax.fori_loop(0, VOCAB_CUTS, make, 0)
+
+        def to_rows(n, carried):
+            cut_width = pl.ds(pl.multiple_of(n * 256, 256), 256)
+            value = lax.dot_general(
+                emb_t[cut_width, :],
+                expo[:, token_lanes(k)],
+                (((1,), (0,)), ((), ())),
+                preferred_element_type=jnp.float32,
+            ).astype(BFLOAT)
+            part[k, 0, cut_width, :] = value[:, :size]
+            part[k, 1, cut_width, :] = value[:, size:]
+            return carried
+
+        lax.fori_loop(0, width // 256, to_rows, 0)
+
+    def dd_copy(k):
+        return remote(part.at[k, 1 - c], sib_part.at[k], dd_send.at[k], dd_recv.at[k], sibling)
+
+    def r1_copy(zz, j):
+        f, _, first_peer, _, block = order(zz)
+        return remote(
+            sib_part.at[block(1 - f, j)], part_one.at[zz, j], r1_send.at[zz, j], r1_recv.at[zz, j],
+            first_peer,
+        )
+
+    def r2_copy(zz):
+        _, g, _, second_peer, _ = order(zz)
+        return remote(part_one.at[zz, 1 - g], part_two.at[zz], r2_send.at[zz], r2_recv.at[zz], second_peer)
+
+    def rz_copy(zz):
+        return remote(part_two.at[zz], part_z.at[z], rz_send.at[zz], rz_recv.at[z], at(x, y, zz, c))
+
+    def rz_arrival(zz):
+        return remote(part_two.at[zz], part_z.at[zz], rz_send.at[zz], rz_recv.at[zz], at(x, y, zz, c))
+
+    step = 64
+
+    def add_into(target_ref, other_ref):
+        @pl.loop(0, width // step)
+        def _(n):
+            rows_here = pl.ds(pl.multiple_of(n * step, step), step)
+            target_ref[rows_here, :] = (
+                target_ref[rows_here, :].astype(jnp.float32) + other_ref[rows_here, :].astype(jnp.float32)
+            ).astype(BFLOAT)
+
+    def group(n):
+        return lax.rem(n, 2) * 2 + n // 2
+
+    def chunk(q):
+        j, n = q // 4, lax.rem(q, 4)
+        columns = pl.ds(pl.multiple_of(n * 256, 256), 256)
+        gemb_out[cut_rows(j), columns] = lax.dot_general(
+            expo[cut_rows(j), :],
+            held[:, columns],
+            (((1,), (0,)), ((), ())),
+            preferred_element_type=jnp.float32,
+        ).astype(BFLOAT)
+
+    @pl.loop(0, 28)
+    def _(s):
+        turn = s // 4
+        edge = lax.rem(s, 4) == 0
+
+        @pl.when(edge & (turn >= 1) & (turn < 5))
+        def _():
+            zz = group(turn - 1)
+
+            @pl.loop(0, 4)
+            def _(n):
+                k = n * 4 + zz
+                dd_copy(k).wait_recv()
+                add_into(sib_part.at[k], part.at[k, c])
+
+            for j in range(2):
+                r1_copy(zz, j).start()
+
+        @pl.when(edge & (turn >= 2) & (turn < 6))
+        def _():
+            zz = group(turn - 2)
+            f, _, _, _, block = order(zz)
+            for j in range(2):
+                r1_copy(zz, j).wait_recv()
+                add_into(part_one.at[zz, j], sib_part.at[block(f, j)])
+            r2_copy(zz).start()
+
+        @pl.when(edge & (turn >= 3))
+        def _():
+            zz = group(turn - 3)
+            _, g, _, _, _ = order(zz)
+            r2_copy(zz).wait_recv()
+            add_into(part_two.at[zz], part_one.at[zz, g])
+
+            @pl.when(zz != z)
+            def _():
+                rz_copy(zz).start()
+
+        @pl.when(s < 16)
+        def _():
+            k = lax.rem(s, 4) * 4 + group(turn)
+            backward_block(k)
+            dd_copy(k).start()
+
+        @pl.when(s >= 16)
+        def _():
+            chunk(s - 16)
+
+    for d in (1, 2, 3):
+        rz_arrival(lax.rem(z + d, 4)).wait_recv()
+
+    @pl.loop(0, width // step)
+    def _(n):
+        rows_here = pl.ds(pl.multiple_of(n * step, step), step)
+        value = part_two[z, rows_here, :].astype(jnp.float32)
+        for d in (1, 2, 3):
+            value = value + part_z[lax.rem(z + d, 4), rows_here, :].astype(jnp.float32)
+        third_out[rows_here, :] = value
+
+    for d in (1, 2, 3):
+        along_copy(d).wait_send()
+        rz_copy(lax.rem(z + d, 4)).wait_send()
+
+    @pl.loop(0, 4)
+    def _(zz):
+        one_copy(zz).wait_send()
+        for j in range(2):
+            two_copy(zz, j).wait_send()
+            r1_copy(zz, j).wait_send()
+        r2_copy(zz).wait_send()
+
+    @pl.loop(0, 16)
+    def _(k):
+        sib_copy(k).wait_send()
+        dd_copy(k).wait_send()
+
+
+def vocabulary_head(third_low, targets, log_prior, usable, embedding, slots, length):
+    size, width = third_low.shape
+    vocab_here = embedding.shape[0]
+    rows = 16 * VOCAB_CUTS * -(-vocab_here // (4 * 16 * VOCAB_CUTS))
+    start = jnp.minimum(lax.axis_index("pb") * rows, vocab_here - rows)
+    emb = lax.dynamic_slice_in_dim(embedding, start, rows)
+    aux = jnp.zeros((8, size), jnp.float32)
+    aux = aux.at[0].set(targets.astype(jnp.float32))
+    aux = aux.at[1].set(jnp.repeat(log_prior, length))
+    aux = aux.at[2].set(jnp.repeat(usable.astype(jnp.float32), length))
+    dma = pltpu.SemaphoreType.DMA
+    vmem = pl.BlockSpec(memory_space=pltpu.VMEM)
+    stat = (3, 16, 2 * size)
+    f32 = jnp.float32
+    block = (width, size)
+    small, gemb, third = pl.pallas_call(
+        functools.partial(head_kernel, slots, length, vocab_here),
+        out_shape=(
+            jax.ShapeDtypeStruct((8, size), f32),
+            jax.ShapeDtypeStruct((rows, width), BFLOAT),
+            jax.ShapeDtypeStruct((width, size), f32),
+        ),
+        in_specs=[vmem] * 4,
+        out_specs=(vmem,) * 3,
+        scratch_shapes=[
+            pltpu.VMEM((32 * size, width), BFLOAT),
+            pltpu.VMEM((2, 2, 4, 8, 2 * size), f32),
+            pltpu.VMEM((rows, 2 * size), f32),
+            pltpu.VMEM((rows, 32 * size), BFLOAT),
+            pltpu.VMEM((16, 2) + block, BFLOAT),
+            pltpu.VMEM((16,) + block, BFLOAT),
+            pltpu.VMEM((4, 2) + block, BFLOAT),
+            pltpu.VMEM((4,) + block, BFLOAT),
+            pltpu.VMEM((4,) + block, BFLOAT),
+            pltpu.VMEM((4,) + stat, f32),
+            pltpu.VMEM((3,) + stat, f32),
+            pltpu.VMEM((4,) + stat, f32),
+        ]
+        + [pltpu.VMEM((16, 2 * size), f32)] * 5
+        + [dma((2,))]
+        + [dma((3,))] * 2
+        + [dma((4,))] * 2
+        + [dma((4, 2))] * 2
+        + [dma((16,))] * 2
+        + [dma((3,))] * 8
+        + [dma((16,))] * 2
+        + [dma((4, 2))] * 2
+        + [dma((4,))] * 4,
+        compiler_params=pltpu.CompilerParams(
+            collective_id=2, has_side_effects=True, vmem_limit_bytes=60 * 2**20
+        ),
+        name="vocabulary_head",
+    )(third_low, aux, emb, emb.T)
+    return small, gemb, third
 
 
 def merged(part, axis, combine):
@@ -462,9 +1398,82 @@
     )
 
 
+def per_device_kernels(
+    decoder_states,
+    encoder_memory,
+    target_tokens,
+    log_prior,
+    slot_counts,
+    slot_mask,
+    self_packed,
+    self_output,
+    cross_query,
+    cross_memory,
+    cross_output,
+    feed_expand,
+    feed_reduce,
+    embedding,
+    norm_gains,
+    norm_shifts,
+):
+    shards = (
+        self_packed,
+        self_output,
+        cross_query,
+        cross_memory,
+        cross_output,
+        feed_expand,
+        feed_reduce,
+    )
+    norm_rows = jnp.concatenate(
+        [norm_gains, norm_shifts, jnp.zeros((2, norm_gains.shape[1]), BFLOAT)]
+    ).astype(jnp.float32)
+    matrices, norms = gather_weights(shards, norm_rows)
+    weights = matrices + (norms[:3], norms[3:6])
+    _, slots_here, length, model_width = decoder_states.shape
+    slots = slots_here * lax.axis_size("pa")
+    inputs = decoder_states[0]
+    encoded = encoder_memory[0]
+    third_low, stored = layer_forward(inputs, encoded, weights)
+    slot_index = lax.axis_index("pa") * slots_here + jnp.arange(slots_here)
+    usable = (slot_mask[0] == 1) & (slot_index < slot_counts[0])
+    small, grad_embed, grad_third = vocabulary_head(
+        third_low.reshape(slots_here * length, model_width),
+        target_tokens.reshape(slots_here * length),
+        log_prior[0],
+        usable,
+        embedding,
+        slots,
+        length,
+    )
+    loss_value = small[0, 0]
+    grad_prior = small[1].reshape(1, slots_here, length)[:, :, 0]
+    pieces = lax.all_gather(grad_embed, "pb", axis=0)
+    repeated = 4 * grad_embed.shape[0] - embedding.shape[0]
+    grad_embed = jnp.concatenate(
+        [pieces[0], pieces[1], pieces[2], pieces[3][repeated:]]
+    ).astype(jnp.float32)
+    grad_third = grad_third.T.reshape(slots_here, length, model_width)
+    grad_inputs, grad_encoded, grads = layer_backward(grad_third, inputs, encoded, weights, stored)
+    low_grads = tuple(grad.astype(BFLOAT) for grad in grads[:7])
+    norm_grads = jnp.concatenate([grads[7], grads[8], jnp.zeros((2, model_width), jnp.float32)])
+    shares, norm_sums = reduce_grads(low_grads, norm_grads)
+    norm_here = norm_gains.shape[1]
+    norm_sums = lax.dynamic_slice_in_dim(
+        norm_sums, lax.axis_index("pa") * norm_here, norm_here, axis=1
+    )
+    return (
+        loss_value,
+        grad_inputs.reshape(decoder_states.shape),
+        grad_encoded.reshape(encoder_memory.shape),
+        grad_prior,
+    ) + shares + (grad_embed, norm_sums[:3], norm_sums[3:6])
+
+
 def solution(mesh):
+    own_kernels = mesh.shape["pb"] == 4 and mesh.shape["pa"] == 8
     return jax.shard_map(
-        per_device,
+        per_device_kernels if own_kernels else per_device,
         mesh=mesh,
         in_specs=(
             P("pb", "pa", None, None),

time: 1490 us -> 832 us (0.56)
  waiting for transfers between devices: 1010 us -> 0.02 us
  Pallas kernels: 0 us -> 557 us
  blocking collectives: 109 us -> 0 us
  matrix products: 186 us -> 107 us
    pallas_call x0 -> x3, Pallas kernels: none -> 557 us  [the longest x1 199 us: reduce_grads(): pl.pallas_call(reduce_kernel, out_shape=tuple((jax.ShapeDtypeStruct(shape...]
    reduce_scatter x6 -> x0, waiting for transfers between devices: 325 us -> none  [the longest x1 90.4 us: per_device(): lax.psum_scatter(grads[5].astype(BFLOAT), 'pa', scatter_dimension=0, tile...]
    psum x1 -> x0, waiting for transfers between devices: 303 us -> none  [per_device(): lax.psum((shares[0], shares[1], shares[2], shares[3], shares[4], shares[5...]
    all_gather x8 -> x1, waiting for transfers between devices: 302 us -> 0.01 us  [per_device_kernels(): pieces = lax.all_gather(grad_embed, 'pb', axis=0)]
    unnamed x23 -> x1, waiting for transfers between devices: 83.4 us -> 0.02 us
    all_gather x7 -> x0, blocking collectives: 81.7 us -> none  [the longest x3 42 us: merged(): gathered = jax.tree.map(lambda a: lax.all_gather(a, axis), part)]
    dot_general x8 -> x7, matrix products: 52.2 us -> 17.8 us  [matmul(): lax.dot_general(matrix_left, matrix_right, (((matrix_left.ndim - 1,), (0,...]
    dot_general x8 -> x7, matrix products: 61.7 us -> 31.7 us  [matmul_back(): lax.dot_general(matrix_left, matrix_right, (((matrix_left.ndim - 1,), (1,...]
  transfers between devices with their start and end apart: 19 -> 1, of which waited for: 18 -> 0; matrix products, arithmetic and copies ran while one was open for 11% -> 19% of each run, Pallas kernels for 0% -> 24%
where the time goes in v2:
time: 832 us; the launch traced here: 821 us
  Pallas kernels  557 us (67%)
  matrix products  107 us (13%)
  local copies, waits for them, and re-layouts  95.3 us (11%)
  other arithmetic  44.7 us (5%)
  between operations  15.9 us (2%)
    pallas_call x1, Pallas kernels, reduce_grads(): pl.pallas_call(reduce_kernel, out_shape=tuple((jax.ShapeDtypeStruct(shape...  199 us
    pallas_call x1, Pallas kernels, vocabulary_head(): pl.pallas_call(functools.partial(head_kernel, slots, length, vocab_here),...  183 us
    pallas_call x1, Pallas kernels, gather_weights(): pl.pallas_call(gather_kernel, out_shape=tuple((jax.ShapeDtypeStruct(shape...  176 us
    dot_general x7, matrix products, matmul_back(): lax.dot_general(matrix_left, matrix_right, (((matrix_left.ndim - 1,), (1,...  31.7 us
    dot_general x7, matrix products, outer_sum(): lax.dot_general(flat_left, flat_right, (((0,), (0,)), ((), ())), preferre...  31.5 us
    unnamed x143, local copies, waits for them, and re-layouts  20.1 us
    dot_general x7, matrix products, matmul(): lax.dot_general(matrix_left, matrix_right, (((matrix_left.ndim - 1,), (0,...  17.8 us
    convert_element_type x1, other arithmetic, per_device_kernels(): grad_embed = jnp.concatenate([pieces[0], pieces[1], pieces[2], pieces[3][...  17.5 us
  transfers between devices with their start and end apart: 1, of which 0 were waited for; matrix products, arithmetic and copies ran while one was open for 19% of the time, Pallas kernels for 24%

profile of v2, /device:TPU:0, one launch (start us, length us, event | category | flops | bytes accessed | tf_op | source)
XLA Modules:
  0.0 820.6 jit_solution(14647221416933661945)
XLA Ops:
  8.8 176.4 %gather_weights.1 = (bf16[4,2,128,3072]{3,2,1,0:T(8,128)(2,1)}, bf16[4,2,128,1024]{3,2,1,0:T(8,128)(2,1)}, bf16[4,2,128,1024]{3,2,1,0:T(8,128)(2,1)}, bf16[4,2,1...) custom-call(bf16[128,3072]{1,0:T(8,128)(2,1)} %refs_0_.1, ...), custom_call_target="tpu_custom_call" | custom-call | tf_op jit(solution)/shard_map/gather_weights/pallas_call | solution.py:182
  185.2 7.4 convert_bitcast_fusion
  218.0 5.7 fusion.43
  223.8 5.2 multiply_convert_fusion.2
  232.6 4.5 constant_dynamic-slice_fusion.1.refs_2_
  237.1 5.4 copy.109
  244.5 182.5 %vocabulary_head.1 = (f32[8,128]{1,0:T(8,128)}, bf16[1584,1024]{1,0:T(8,128)(2,1)}, f32[1024,128]{1,0:T(8,128)}) custom-call(bf16[128,1024]{1,0:T(8,128)(2,1)} %bitcast.255, f32[8,128]{1,0:T(8,128)} %copy-done.60, bf16[1584,1024]{1,0:T(8,128)(2,1)} %constant_dynamic-slice_fusion.1.refs_2_, bf16[1024,1584]{1,0:T(8,128)(2,1)} %bitcast.217), custom_call_target="tpu_custom_call" | custom-call | tf_op jit(solution)/shard_map/vocabulary_head/pallas_call | solution.py:912
  434.4 9.9 %add_convert_fusion = bf16[2,64,4096]{2,1,0:T(8,128)(2,1)S(1)} fusion(bf16[4096,1024,1]{1,0,2:T(8,128)(2,1)} %bitcast.213, f32[2,64,4096]{2,1,0:T(8,128)S(1)} %copy-done.40, f32[2,64,1024]{2,1,0:T(8,128)S(1)} %subtract_multiply_fusion.2, u8[64,4096]{1,0:T(8,128)(4,1)S(1)} %copy-done.56, u8[64,4096]{1,0:T(8,128)(4,1)S(1)} %copy-done.54), kind=kOutput, calls=%fused_computation.33 | convolution fusion | flops 1114243072 | bytes 12582912 | tf_op jit(solution)/shard_map/dot_general | solution.py:974
  452.5 4.8 multiply_reduce_fusion
  496.6 4.6 convolution_convert_fusion.5
  501.2 4.0 copy.89
  505.2 3.6 multiply_convert_fusion
  508.8 4.2 copy.88
  518.6 3.8 copy.96
  539.1 4.5 convolution_convert_fusion
  543.6 6.0 bitcast_convert_fusion
  549.6 5.9 bitcast_convert_fusion.1
  555.5 7.9 fusion.8
  563.4 198.6 %reduce_grads.1 = (bf16[128,3072]{1,0:T(8,128)(2,1)S(1)}, bf16[128,1024]{1,0:T(8,128)(2,1)S(1)}, bf16[128,1024]{1,0:T(8,128)(2,1)S(1)}, bf16[128,2048]{1,0:T(8,1...) custom-call(bf16[4,2,128,3072]{3,2,1,0:T(8,128)(2,1)} %bitcast.200, ...), custom_call_target="tpu_custom_call" | custom-call | tf_op jit(solution)/shard_map/reduce_grads/pallas_call | solution.py:464
  771.3 6.1 fusion.30
  777.4 6.2 fusion.13
  783.6 3.9 slice_bitcast_fusion
  787.5 8.6 %slice.169 = bf16[4752,1024]{1,0:T(8,128)(2,1)} slice(bf16[6336,1024]{1,0:T(8,128)(2,1)} %all-gather.3.cloned.1.call-done), slice={[0:4752], [0:1024]} | slice | bytes 19464192 | tf_op jit(solution)/shard_map/slice | solution.py:1454
  796.1 17.5 %maximum_convert_fusion = f32[6288,1024]{1,0:T(8,128)} fusion(bf16[1536,1024]{1,0:T(8,128)(2,1)} %slice_bitcast_fusion, bf16[4752,1024]{1,0:T(8,128)(2,1)} %slice.169), kind=kLoop, calls=%fused_computation.2 | loop fusion | flops 25755648 | bytes 38633472 | tf_op jit(solution)/shard_map/convert_element_type | solution.py:1455
  (253 shorter events, 117.8 us)
Async XLA Ops:
  7.2 178.0 %copy-start = (bf16[1,2,512,1024]{3,2,1,0:T(8,128)(2,1)S(1)}, bf16[1,2,512,1024]{3,2,1,0:T(8,128)(2,1)}, u32[]{:S(2)}) copy-start(bf16[1,2,512,1024]{3,2,1,0:T(8,128)(2,1)} %param.23) | copy-start | bytes 6291460
  7.2 776.4 %all-gather.3.cloned.1.call-start = ((), (), s32[]{:S(2)}) async-start(), calls=%async_computation | async-start | bytes 16220160 | tf_op jit(solution)/shard_map/all_gather | solution.py:1451
  217.8 11.2 %copy-start.3 = (f32[2,64,1024]{2,1,0:T(8,128)}, f32[2,64,1024]{2,1,0:T(8,128)S(1)}, u32[]{:S(2)}) copy-start(f32[2,64,1024]{2,1,0:T(8,128)S(1)} %get-tuple-element.120) | copy-start | bytes 1572868
  218.0 11.0 %slice-start.2 = ((s8[8388608]{0:T(1024)(128)(4,1)}), s8[4194304]{0:T(1024)(128)(4,1)S(1)}, s32[]{:S(2)}) async-start(s8[8388608]{0:T(1024)(128)(4,1)} %bitcast.214), calls=%async_computation.3 | async-start | bytes 8388608
  218.0 11.0 %slice-start.3 = ((s8[8388608]{0:T(1024)(128)(4,1)}), s8[4194304]{0:T(1024)(128)(4,1)S(1)}, s32[]{:S(2)}) async-start(s8[8388608]{0:T(1024)(128)(4,1)} %bitcast.214), calls=%async_computation.4 | async-start | bytes 8388608
  223.8 6.7 copy-start.39
  223.8 6.7 copy-start.53
  223.8 6.7 copy-start.55
  430.4 13.8 %slice-start = ((s8[8388608]{0:T(1024)(128)(4,1)}), s8[4194304]{0:T(1024)(128)(4,1)S(1)}, s32[]{:S(2)}) async-start(s8[8388608]{0:T(1024)(128)(4,1)} %bitcast.210), calls=%async_computation.1 | async-start | bytes 8388608
  434.3 9.9 %copy-start.24 = (f32[2,64,1024]{2,1,0:T(8,128)}, f32[2,64,1024]{2,1,0:T(8,128)S(1)}, u32[]{:S(2)}) copy-start(f32[2,64,1024]{2,1,0:T(8,128)S(1)} %subtract_multiply_fusion.2) | copy-start | bytes 1572868
  434.3 9.9 %copy-start.4 = (f32[2,64,1024]{2,1,0:T(8,128)S(1)}, f32[2,64,1024]{2,1,0:T(8,128)}, u32[]{:S(2)}) copy-start(f32[2,64,1024]{2,1,0:T(8,128)} %copy-done.3) | copy-start | bytes 1572868
  434.3 9.9 %slice-start.1 = ((s8[8388608]{0:T(1024)(128)(4,1)}), s8[4194304]{0:T(1024)(128)(4,1)S(1)}, s32[]{:S(2)}) async-start(s8[8388608]{0:T(1024)(128)(4,1)} %bitcast.210), calls=%async_computation.2 | async-start | bytes 8388608
  508.8 8.3 %copy-start.29 = (bf16[2,16,64,64]{3,2,1,0:T(8,128)(2,1)S(1)}, bf16[2,16,64,64]{3,2,1,0:T(8,128)(2,1)}, u32[]{:S(2)}) copy-start(bf16[2,16,64,64]{3,2,1,0:T(8,128)(2,1)} %copy-done.28) | copy-start | bytes 786436
  526.5 5.3 copy-start.38
  526.5 5.3 copy-start.51
  531.8 5.2 copy-start.36
  531.8 5.2 copy-start.52
  543.6 6.0 copy-start.5
  543.6 6.0 copy-start.23
  549.6 5.9 copy-start.44
  549.6 5.9 copy-start.45
  771.2 6.1 copy-start.42
  771.3 6.1 copy-start.43
  771.3 6.1 copy-start.64
  (47 other events, 129.5 us)
Sparse Core Ops, SparseCore 0:
  427.2 137.3 all-gather.2

commit v3 on v2

--- a/solution.py
+++ b/solution.py
@@ -63,148 +63,8 @@
 Z_FULL = (9, 14)
 
 
-def gather_kernel(*refs):
-    shards, norm, fulls, norm_full = refs[:7], refs[7], refs[8:15], refs[15]
-    (
-        local_sem, z_send, z_recv, one_send, one_recv, two_send, two_recv, d_send, d_recv,
-        norm_sem, nz_send, nz_recv, nd_send, nd_recv,
-    ) = refs[16:]
-    x, y, z, c = whereami()
-    greet(neighbours(x, y, z, c))
-    every = slice(None)
-
-    def copies(u):
-        unit = UNITS[u]
-        shard, full = shards[unit[0]], fulls[unit[0]]
-        wide = u in Z_FULL
-        a, b = (x, y) if u % 2 == 0 else (y, x)
-        first_peer = at(x, 1 - y, z, c) if u % 2 == 0 else at(1 - x, y, z, c)
-        second_peer = at(1 - x, y, z, c) if u % 2 == 0 else at(x, 1 - y, z, c)
-        quarter = pl.multiple_of(64 * a + 32 * b, 32)
-        half = pl.multiple_of(64 * a, 64)
-        rows = (0, ROWS) if wide else (quarter, 32)
-        local = pltpu.make_async_copy(
-            shard_view(shard, unit, *rows), full_view(full, unit, z, c, *rows), local_sem.at[u]
-        )
-        along = [
-            pltpu.make_async_remote_copy(
-                src_ref=shard_view(shard, unit, *rows),
-                dst_ref=full_view(full, unit, z, c, *rows),
-                send_sem=z_send.at[u, d - 1],
-                recv_sem=z_recv.at[u, d - 1],
-                device_id=at(x, y, lax.rem(z + d, 4), c),
-                device_id_type=MESH,
-            )
-            for d in (1, 2, 3)
-        ]
-
-        def cross(start, size, sends, recvs, peer):
-            part = full_view(full, unit, every, c, start, size)
-            return pltpu.make_async_remote_copy(
-                src_ref=part,
-                dst_ref=part,
-                send_sem=sends.at[u],
-                recv_sem=recvs.at[u],
-                device_id=peer,
-                device_id_type=MESH,
-            )
-
-        first = None if wide else cross(quarter, 32, one_send, one_recv, first_peer)
-        second = None if wide else cross(half, 64, two_send, two_recv, second_peer)
-        sibling = cross(0, ROWS, d_send, d_recv, at(x, y, z, 1 - c))
-        return local, along, first, second, sibling
-
-    def norm_copy(src, dst, send, recv, peer):
-        return pltpu.make_async_remote_copy(
-            src_ref=src, dst_ref=dst, send_sem=send, recv_sem=recv, device_id=peer, device_id_type=MESH
-        )
-
-    norm_local = pltpu.make_async_copy(norm, norm_full.at[z, c], norm_sem)
-    norm_along = [
-        norm_copy(
-            norm, norm_full.at[z, c], nz_send.at[d - 1], nz_recv.at[d - 1], at(x, y, lax.rem(z + d, 4), c)
-        )
-        for d in (1, 2, 3)
-    ]
-    norm_sibling = norm_copy(
-        norm_full.at[:, c], norm_full.at[:, c], nd_send, nd_recv, at(x, y, z, 1 - c)
-    )
-    norm_local.start()
-    for copy in norm_along:
-        copy.start()
-    count = len(UNITS)
-    every_copy = [copies(u) for u in range(count)]
-    for local, along, _, _, _ in every_copy:
-        local.start()
-        for copy in along:
-            copy.start()
-    norm_local.wait()
-    for copy in norm_along:
-        copy.wait()
-    norm_sibling.start()
-    norm_sibling.wait()
-    lag_two, lag_sibling = 2, 4
-    for i in range(count + lag_sibling):
-        if i < count:
-            local, along, first, _, _ = every_copy[i]
-            local.wait()
-            for copy in along:
-                copy.wait_recv()
-            if first is not None:
-                first.start()
-        if 0 <= i - lag_two < count:
-            _, _, first, second, _ = every_copy[i - lag_two]
-            if first is not None:
-                first.wait_recv()
-                second.start()
-        if 0 <= i - lag_sibling < count:
-            _, _, _, second, sibling = every_copy[i - lag_sibling]
-            if second is not None:
-                second.wait_recv()
-            sibling.start()
-    for _, along, first, second, sibling in every_copy:
-        for copy in along:
-            copy.wait_send()
-        if first is not None:
-            first.wait_send()
-            second.wait_send()
-        sibling.wait()
-
-
-def gather_weights(weights, norm):
-    count = len(UNITS)
-    shapes = []
-    for w, weight in enumerate(weights):
-        if w == REDUCE_WEIGHT:
-            shapes.append((4, 2, weight.shape[0] // ROWS, ROWS, weight.shape[1]))
-        else:
-            shapes.append((4, 2) + weight.shape)
-    *fulls, norm_full = pl.pallas_call(
-        gather_kernel,
-        out_shape=tuple(jax.ShapeDtypeStruct(shape, BFLOAT) for shape in shapes)
-        + (jax.ShapeDtypeStruct((4, 2) + norm.shape, norm.dtype),),
-        in_specs=[pl.BlockSpec(memory_space=pl.ANY)] * 8,
-        out_specs=(pl.BlockSpec(memory_space=pl.ANY),) * 8,
-        scratch_shapes=[
-            pltpu.SemaphoreType.DMA((count,)),
-            pltpu.SemaphoreType.DMA((count, 3)),
-            pltpu.SemaphoreType.DMA((count, 3)),
-        ]
-        + [pltpu.SemaphoreType.DMA((count,))] * 6
-        + [pltpu.SemaphoreType.DMA]
-        + [pltpu.SemaphoreType.DMA((3,))] * 2
-        + [pltpu.SemaphoreType.DMA] * 2,
-        compiler_params=pltpu.CompilerParams(collective_id=0, has_side_effects=True),
-        name="gather_weights",
-    )(*weights, norm)
-    norm_full = norm_full.reshape(8, norm.shape[0], norm.shape[1]).transpose(1, 0, 2)
-    return (
-        tuple(full.reshape(-1, full.shape[-1]) for full in fulls),
-        norm_full.reshape(norm.shape[0], -1),
-    )
-
-
 LAGS = (0, 2, 4, 6, 8, 10)
+SIBLING_WINDOW = 2
 
 
 def reduce_kernel(*refs):
@@ -237,7 +97,7 @@
             own_sem.at[u % 2],
         )
 
-    for u in range(count):
+    for u in range(SIBLING_WINDOW):
         sibling_copy(u).start()
     own_copy(0).start()
 
@@ -315,6 +175,11 @@
     @pl.loop(0, count + LAGS[-1])
     def _(i):
         u0 = i
+        for k in range(SIBLING_WINDOW, count):
+            @pl.when(i + SIBLING_WINDOW == k)
+            def _():
+                sibling_copy(k).start()
+
         for k in range(1, count):
             @pl.when(i + 1 == k)
             def _():
@@ -490,22 +355,375 @@
         name="reduce_grads",
     )(*views, norm)
     return tuple(share.astype(jnp.float32) for share in shares), norm_sum
+GATHER_WINDOW = 4
+LAG_TWO, LAG_SIBLING, LAG_LOAD, LAG_USE = 1, 2, 4, 5
+SLOTS_IN_FLIGHT = 3
+
+
+def dot_nn(left, right):
+    return lax.dot_general(left, right, (((1,), (0,)), ((), ())), preferred_element_type=jnp.float32)
+
+
+def dot_nt(left, right):
+    return lax.dot_general(left, right, (((1,), (1,)), ((), ())), preferred_element_type=jnp.float32)
+
+
+def dot_tn(left, right):
+    return lax.dot_general(left, right, (((0,), (0,)), ((), ())), preferred_element_type=jnp.float32)
+
+
+def stack_heads(pair):
+    lane = lax.broadcasted_iota(jnp.int32, pair.shape, 1)
+    zero = jnp.zeros_like(pair)
+    return jnp.concatenate(
+        [jnp.where(lane < HEAD_DIM, pair, zero), jnp.where(lane < HEAD_DIM, zero, pair)], 0
+    )
+
+
+def unstack_heads(stacked):
+    rows = stacked.shape[0] // 2
+    lane = lax.broadcasted_iota(jnp.int32, (rows, stacked.shape[1]), 1)
+    return jnp.where(lane < HEAD_DIM, stacked[:rows], stacked[rows:])
+
+
+def pair_scores(queries, keys, causal):
+    scores = dot_nt(queries, keys) * (1.0 / math.sqrt(HEAD_DIM))
+    if causal:
+        length = keys.shape[0]
+        row = lax.rem(lax.broadcasted_iota(jnp.int32, scores.shape, 0), length)
+        column = lax.broadcasted_iota(jnp.int32, scores.shape, 1)
+        scores = jnp.where(row >= column, scores, NEGATIVE)
+    highest = jnp.max(scores, -1, keepdims=True)
+    total = jnp.sum(jnp.exp(scores - highest), -1, keepdims=True)
+    return jnp.exp(scores - (highest + jnp.log(total)))
+
+
+def attend_pair(queries, keys, values, causal):
+    probs = pair_scores(stack_heads(queries), keys, causal).astype(BFLOAT)
+    return unstack_heads(dot_nn(probs, values)).astype(BFLOAT)
+
+
+def normalise(values, gain, shift):
+    centre = values - jnp.mean(values, -1, keepdims=True)
+    inverse = lax.rsqrt(jnp.mean(centre * centre, -1, keepdims=True) + EPSILON)
+    normed = centre * inverse
+    return normed * gain + shift, normed, inverse
+
+
+def forward_kernel(length, mem_length, *refs):
+    shards, norm, states, encoded = refs[:7], refs[7], refs[8], refs[9]
+    fulls = refs[10:17]
+    (
+        norm_full, packed, context, first_normed, first_inverse, first_low, cross_queries, pairs,
+        cross_context, second_normed, second_inverse, second_low, inner, active, third_normed,
+        third_inverse, third_low,
+    ) = refs[17:34]
+    wbuf, residual = refs[34:36]
+    (
+        local_sem, z_send, z_recv, one_send, one_recv, two_send, two_recv, d_send, d_recv,
+        norm_sem, nz_send, nz_recv, nd_send, nd_recv, load_sem,
+    ) = refs[36:]
+    x, y, z, c = whereami()
+    greet(neighbours(x, y, z, c))
+    every = slice(None)
+    tokens, width = states.shape
+    slots_here = tokens // length
+
+    def copies(u):
+        unit = UNITS[u]
+        shard, full = shards[unit[0]], fulls[unit[0]]
+        wide = u in Z_FULL
+        a, b = (x, y) if u % 2 == 0 else (y, x)
+        first_peer = at(x, 1 - y, z, c) if u % 2 == 0 else at(1 - x, y, z, c)
+        second_peer = at(1 - x, y, z, c) if u % 2 == 0 else at(x, 1 - y, z, c)
+        quarter = pl.multiple_of(64 * a + 32 * b, 32)
+        half = pl.multiple_of(64 * a, 64)
+        rows = (0, ROWS) if wide else (quarter, 32)
+        local = pltpu.make_async_copy(
+            shard_view(shard, unit, *rows), full_view(full, unit, z, c, *rows), local_sem.at[u]
+        )
+        along = [
+            pltpu.make_async_remote_copy(
+                src_ref=shard_view(shard, unit, *rows),
+                dst_ref=full_view(full, unit, z, c, *rows),
+                send_sem=z_send.at[u, d - 1],
+                recv_sem=z_recv.at[u, d - 1],
+                device_id=at(x, y, lax.rem(z + d, 4), c),
+                device_id_type=MESH,
+            )
+            for d in (1, 2, 3)
+        ]
+
+        def cross(start, size, sends, recvs, peer):
+            part = full_view(full, unit, every, c, start, size)
+            return pltpu.make_async_remote_copy(
+                src_ref=part,
+                dst_ref=part,
+                send_sem=sends.at[u],
+                recv_sem=recvs.at[u],
+                device_id=peer,
+                device_id_type=MESH,
+            )
+
+        first = None if wide else cross(quarter, 32, one_send, one_recv, first_peer)
+        second = None if wide else cross(half, 64, two_send, two_recv, second_peer)
+        sibling = cross(0, ROWS, d_send, d_recv, at(x, y, z, 1 - c))
+        load = pltpu.make_async_copy(
+            full_view(full, unit, every, every, 0, ROWS),
+            wbuf.at[u % SLOTS_IN_FLIGHT],
+            load_sem.at[u % SLOTS_IN_FLIGHT],
+        )
+        return local, along, first, second, sibling, load
+
+    def norm_copy(src, dst, send, recv, peer):
+        return pltpu.make_async_remote_copy(
+            src_ref=src, dst_ref=dst, send_sem=send, recv_sem=recv, device_id=peer, device_id_type=MESH
+        )
+
+    norm_local = pltpu.make_async_copy(norm, norm_full.at[z, c], norm_sem)
+    norm_along = [
+        norm_copy(
+            norm, norm_full.at[z, c], nz_send.at[d - 1], nz_recv.at[d - 1], at(x, y, lax.rem(z + d, 4), c)
+        )
+        for d in (1, 2, 3)
+    ]
+    norm_sibling = norm_copy(
+        norm_full.at[:, c], norm_full.at[:, c], nd_send, nd_recv, at(x, y, z, 1 - c)
+    )
+    norm_local.start()
+    for copy in norm_along:
+        copy.start()
+
+    def norm_row(n):
+        return jnp.concatenate(
+            [norm_full[p // 2, p % 2, n : n + 1, :] for p in range(8)], 1
+        )
+
+    def times(left_ref, u, write):
+        slot = u % SLOTS_IN_FLIGHT
+
+        @pl.loop(0, 4)
+        def _(n):
+            columns = pl.ds(pl.multiple_of(n * 256, 256), 256)
+            right = wbuf[slot, :, :, :, columns].reshape(TILE, 256)
+            write(columns, n, dot_nn(left_ref[...], right))
+
+    def block_columns(k, n):
+        return pl.ds(pl.multiple_of(k * TILE + n * 256, 256), 256)
+
+    def attention(queries, keys, key_start, value_start, key_length, out, causal):
+        @pl.loop(0, slots_here * (width // 128))
+        def _(n):
+            slot, group = n // (width // 128), lax.rem(n, width // 128)
+            lanes = pl.ds(pl.multiple_of(group * 128, 128), 128)
+            key_lanes = pl.ds(pl.multiple_of(key_start + group * 128, 128), 128)
+            value_lanes = pl.ds(pl.multiple_of(value_start + group * 128, 128), 128)
+            query_rows = pl.ds(pl.multiple_of(slot * length, length), length)
+            key_rows = pl.ds(pl.multiple_of(slot * key_length, key_length), key_length)
+            out[query_rows, lanes] = attend_pair(
+                queries[query_rows, lanes], keys[key_rows, key_lanes], keys[key_rows, value_lanes], causal
+            )
+
+    def finish_norm(n, value, normed_ref, inverse_ref, low_ref):
+        out, normed, inverse = normalise(value, norm_row(n), norm_row(n + 3))
+        normed_ref[...] = normed
+        inverse_ref[...] = jnp.broadcast_to(inverse, inverse_ref.shape)
+        low_ref[...] = out.astype(BFLOAT)
+        return out
+
+    def use(u):
+        weight, k = UNITS[u]
+        if weight == 0:
+            def write(columns, n, value):
+                packed[:, block_columns(k, n)] = value.astype(BFLOAT)
+
+            times(states, u, write)
+            if k == 2:
+                attention(packed, packed, width, 2 * width, length, context, True)
+        elif weight == 1:
+            def write(columns, n, value):
+                residual[:, columns] = states[:, columns].astype(jnp.float32) + value
+
+            times(context, u, write)
+            residual[...] = finish_norm(0, residual[...], first_normed, first_inverse, first_low)
+        elif weight == 2:
+            def write(columns, n, value):
+                cross_queries[:, columns] = value.astype(BFLOAT)
+
+            times(first_low, u, write)
+        elif weight == 3:
+            slot = u % SLOTS_IN_FLIGHT
+
+            @pl.loop(0, 16)
+            def _(n):
+                m, n = n // 4, lax.rem(n, 4)
+                columns = pl.ds(pl.multiple_of(n * 256, 256), 256)
+                part = encoded.shape[0] // 4
+                rows_here = pl.ds(pl.multiple_of(m * part, part), part)
+                right = wbuf[slot, :, :, :, columns].reshape(TILE, 256)
+                pairs[rows_here, block_columns(k, n)] = dot_nn(encoded[rows_here, :], right).astype(BFLOAT)
+
+            if k == 1:
+                attention(cross_queries, pairs, 0, width, mem_length, cross_context, False)
+        elif weight == 4:
+            def write(columns, n, value):
+                residual[:, columns] = residual[:, columns] + value
+
+            times(cross_context, u, write)
+            residual[...] = finish_norm(1, residual[...], second_normed, second_inverse, second_low)
+        elif weight == 5:
+            def write(columns, n, value):
+                inner[:, block_columns(k, n)] = value
+                gate = 0.5 * (1.0 + lax.erf(value * math.sqrt(0.5)))
+                active[:, block_columns(k, n)] = (value * gate).astype(BFLOAT)
+
+            times(second_low, u, write)
+        else:
+            slot = u % SLOTS_IN_FLIGHT
+            blocks = active.shape[1] // (8 * ROWS)
+            left = jnp.concatenate(
+                [active[:, (p * blocks + k) * ROWS : (p * blocks + k + 1) * ROWS] for p in range(8)], 1
+            )
+
+            @pl.loop(0, 4)
+            def _(n):
+                columns = pl.ds(pl.multiple_of(n * 256, 256), 256)
+                right = wbuf[slot, :, :, :, columns].reshape(TILE, 256)
+                residual[:, columns] = residual[:, columns] + dot_nn(left, right)
+
+            if k == blocks - 1:
+                finish_norm(2, residual[...], third_normed, third_inverse, third_low)
+
+    count = len(UNITS)
+    every_copy = [copies(u) for u in range(count)]
+    for local, along, _, _, _, _ in every_copy[:GATHER_WINDOW]:
+        local.start()
+        for copy in along:
+            copy.start()
+    for i in range(count + LAG_USE):
+        if i + GATHER_WINDOW < count:
+            local, along = every_copy[i + GATHER_WINDOW][:2]
+            local.start()
+            for copy in along:
+                copy.start()
+        if i < count:
+            local, along, first = every_copy[i][:3]
+            local.wait()
+            for copy in along:
+                copy.wait_recv()
+            if first is not None:
+                first.start()
+        if 0 <= i - LAG_TWO < count:
+            first, second = every_copy[i - LAG_TWO][2:4]
+            if first is not None:
+                first.wait_recv()
+                second.start()
+        if 0 <= i - LAG_SIBLING < count:
+            second, sibling = every_copy[i - LAG_SIBLING][3:5]
+            if second is not None:
+                second.wait_recv()
+            sibling.start()
+        if i == 2:
+            norm_local.wait()
+            for copy in norm_along:
+                copy.wait()
+            norm_sibling.start()
+        if i == 4:
+            norm_sibling.wait()
+        if 0 <= i - LAG_LOAD < count:
+            sibling, load = every_copy[i - LAG_LOAD][4:]
+            sibling.wait_recv()
+            load.start()
+        if 0 <= i - LAG_USE < count:
+            every_copy[i - LAG_USE][5].wait()
+            use(i - LAG_USE)
+    for _, along, first, second, sibling, _ in every_copy:
+        for copy in along:
+            copy.wait_send()
+        if first is not None:
+            first.wait_send()
+            second.wait_send()
+        sibling.wait_send()
+
+
+def forward_layer(weights, norm, states, encoded, length):
+    count = len(UNITS)
+    shapes = []
+    for w, weight in enumerate(weights):
+        if w == REDUCE_WEIGHT:
+            shapes.append((4, 2, weight.shape[0] // ROWS, ROWS, weight.shape[1]))
+        else:
+            shapes.append((4, 2) + weight.shape)
+    tokens, width = states.shape
+    mem_tokens = encoded.shape[0]
+    mem_length = mem_tokens // (tokens // length)
+    units = weights[5].shape[1]
+    f32 = jnp.float32
+    kept = [
+        ((4, 2) + norm.shape, f32),
+        ((tokens, 3 * width), BFLOAT),
+        ((tokens, width), BFLOAT),
+        ((tokens, width), f32),
+        ((tokens, 128), f32),
+        ((tokens, width), BFLOAT),
+        ((tokens, width), BFLOAT),
+        ((mem_tokens, 2 * width), BFLOAT),
+        ((tokens, width), BFLOAT),
+        ((tokens, width), f32),
+        ((tokens, 128), f32),
+        ((tokens, width), BFLOAT),
+        ((tokens, units), f32),
+        ((tokens, units), BFLOAT),
+        ((tokens, width), f32),
+        ((tokens, 128), f32),
+        ((tokens, width), BFLOAT),
+    ]
+    every = pl.BlockSpec(memory_space=pl.ANY)
+    vmem = pl.BlockSpec(memory_space=pltpu.VMEM)
+    dma = pltpu.SemaphoreType.DMA
+    results = pl.pallas_call(
+        functools.partial(forward_kernel, length, mem_length),
+        out_shape=tuple(jax.ShapeDtypeStruct(shape, BFLOAT) for shape in shapes)
+        + tuple(jax.ShapeDtypeStruct(shape, kind) for shape, kind in kept),
+        in_specs=[every] * 8 + [vmem] * 2,
+        out_specs=(every,) * 7 + (vmem,) * len(kept),
+        scratch_shapes=[
+            pltpu.VMEM((SLOTS_IN_FLIGHT, 4, 2, ROWS, TILE), BFLOAT),
+            pltpu.VMEM((tokens, width), f32),
+            dma((count,)),
+            dma((count, 3)),
+            dma((count, 3)),
+        ]
+        + [dma((count,))] * 6
+        + [dma]
+        + [dma((3,))] * 2
+        + [dma] * 2
+        + [dma((SLOTS_IN_FLIGHT,))],
+        compiler_params=pltpu.CompilerParams(
+            collective_id=0, has_side_effects=True, vmem_limit_bytes=48 * 2**20
+        ),
+        name="forward_layer",
+    )(*weights, norm, states, encoded)
+    fulls = tuple(full.reshape(-1, full.shape[-1]) for full in results[:7])
+    norm_full = results[7].reshape(8, norm.shape[0], norm.shape[1]).transpose(1, 0, 2)
+    return fulls, norm_full.reshape(norm.shape[0], -1), results[8:]
+
 
 VOCAB_CUTS = 3
 
 
 def head_kernel(slots, length, vocab_here, *refs):
-    hid, aux, emb, emb_t = refs[:4]
-    small_out, gemb_out, third_out = refs[4:7]
+    hid, aux, emb_all = refs[:3]
+    small_out, gemb_out, third_out = refs[3:6]
     (
-        held, marks, logit, expo, part, sib_part, part_one, part_two, part_z,
+        emb, emb_t, held, marks, logit, expo, part, sib_part, part_one, part_two, part_z,
         mine, theirs, lined, prior, usable, weight, scaled, picked_grad,
-    ) = refs[7:24]
+    ) = refs[6:25]
     (
         local_sem, z_send, z_recv, one_send, one_recv, two_send, two_recv, sib_send, sib_recv,
         ax_send, ax_recv, axz_send, axz_recv, st_send, st_recv, stz_send, stz_recv,
         dd_send, dd_recv, r1_send, r1_recv, r2_send, r2_recv, rz_send, rz_recv,
-    ) = refs[24:]
+    ) = refs[25:]
     x, y, z, c = whereami()
     pb, pa = y * 2 + x, z * 2 + c
     size = hid.shape[0]
@@ -513,8 +731,9 @@
     width = hid.shape[1]
     rows = emb.shape[0]
     cut = rows // VOCAB_CUTS
-    start = jnp.minimum(pb * rows, vocab_here - rows)
-    skip = pb * rows - start
+    start = pl.multiple_of(pb * rows, 16)
+    last = vocab_here - 3 * rows
+    valid = jnp.where(pb == 3, last, rows)
     base = pa * vocab_here + start
     own = pb * 4 + z
 
@@ -535,6 +754,16 @@
     lanes = pl.ds(pl.multiple_of(c * size, size), size)
     aux_copy = pltpu.make_async_copy(aux, marks.at[y, x, z, :, lanes], local_sem.at[1])
     aux_copy.start()
+    emb_copy = pltpu.make_async_copy(
+        emb_all.at[pl.ds(start, last), :], emb.at[pl.ds(0, last), :], local_sem.at[2]
+    )
+    rest_copy = pltpu.make_async_copy(
+        emb_all.at[pl.ds(pl.multiple_of(jnp.minimum(start + last, vocab_here - (rows - last)), 16), rows - last), :],
+        emb.at[pl.ds(last, rows - last), :],
+        local_sem.at[3],
+    )
+    emb_copy.start()
+    rest_copy.start()
     own_copy.wait()
 
     def along_copy(d):
@@ -593,10 +822,22 @@
     for d in (1, 2, 3):
         mark_copy(d).wait()
 
+    emb_copy.wait()
+    rest_copy.wait()
+    full_cuts = rows // 128
+
+    @pl.loop(0, full_cuts)
+    def _(n):
+        here = pl.ds(pl.multiple_of(n * 128, 128), 128)
+        emb_t[:, here] = emb[here, :].T
+
+    if rows % 128:
+        emb_t[:, full_cuts * 128 :] = emb[full_cuts * 128 :, :].T
+
     def target_rows(k):
         ypart, xpart, zpart = k // 8, lax.rem(k // 4, 2), lax.rem(k, 4)
         target = marks[ypart, xpart, zpart, 0:1, :].astype(jnp.int32) - base
-        return jnp.where(target >= skip, target, -1)
+        return jnp.where(target < valid, target, -1)
 
     def row_numbers(j):
         return lax.broadcasted_iota(jnp.int32, (cut, pair), 0) + j * cut
@@ -617,7 +858,7 @@
                 emb[cut_rows(j), :], block, (((1,), (1,)), ((), ())), preferred_element_type=jnp.float32
             )
             number = row_numbers(j)
-            value = jnp.where(number >= skip, value, NEGATIVE)
+            value = jnp.where(number < valid, value, NEGATIVE)
             logit[cut_rows(j), :] = value
             return (
                 jnp.maximum(highest, jnp.max(value, 0, keepdims=True)),
@@ -898,8 +1139,6 @@
     size, width = third_low.shape
     vocab_here = embedding.shape[0]
     rows = 16 * VOCAB_CUTS * -(-vocab_here // (4 * 16 * VOCAB_CUTS))
-    start = jnp.minimum(lax.axis_index("pb") * rows, vocab_here - rows)
-    emb = lax.dynamic_slice_in_dim(embedding, start, rows)
     aux = jnp.zeros((8, size), jnp.float32)
     aux = aux.at[0].set(targets.astype(jnp.float32))
     aux = aux.at[1].set(jnp.repeat(log_prior, length))
@@ -916,9 +1155,11 @@
             jax.ShapeDtypeStruct((rows, width), BFLOAT),
             jax.ShapeDtypeStruct((width, size), f32),
         ),
-        in_specs=[vmem] * 4,
+        in_specs=[vmem, vmem, pl.BlockSpec(memory_space=pl.ANY)],
         out_specs=(vmem,) * 3,
         scratch_shapes=[
+            pltpu.VMEM((rows, width), BFLOAT),
+            pltpu.VMEM((width, rows), BFLOAT),
             pltpu.VMEM((32 * size, width), BFLOAT),
             pltpu.VMEM((2, 2, 4, 8, 2 * size), f32),
             pltpu.VMEM((rows, 2 * size), f32),
@@ -933,7 +1174,7 @@
             pltpu.VMEM((4,) + stat, f32),
         ]
         + [pltpu.VMEM((16, 2 * size), f32)] * 5
-        + [dma((2,))]
+        + [dma((4,))]
         + [dma((3,))] * 2
         + [dma((4,))] * 2
         + [dma((4, 2))] * 2
@@ -946,7 +1187,7 @@
             collective_id=2, has_side_effects=True, vmem_limit_bytes=60 * 2**20
         ),
         name="vocabulary_head",
-    )(third_low, aux, emb, emb.T)
+    )(third_low, aux, embedding)
     return small, gemb, third
 
 
@@ -1398,6 +1639,12 @@
     )
 
 
+def score_logsum(queries, key_rows, causal):
+    scores = score_block(split_heads(queries), split_heads(key_rows), causal)
+    highest = jnp.max(scores, -1, keepdims=True)
+    return highest + jnp.log(jnp.sum(jnp.exp(scores - highest), -1, keepdims=True))
+
+
 def per_device_kernels(
     decoder_states,
     encoder_memory,
@@ -1428,13 +1675,30 @@
     norm_rows = jnp.concatenate(
         [norm_gains, norm_shifts, jnp.zeros((2, norm_gains.shape[1]), BFLOAT)]
     ).astype(jnp.float32)
-    matrices, norms = gather_weights(shards, norm_rows)
-    weights = matrices + (norms[:3], norms[3:6])
     _, slots_here, length, model_width = decoder_states.shape
     slots = slots_here * lax.axis_size("pa")
     inputs = decoder_states[0]
     encoded = encoder_memory[0]
-    third_low, stored = layer_forward(inputs, encoded, weights)
+    matrices, norms, kept = forward_layer(
+        shards,
+        norm_rows,
+        inputs.reshape(slots_here * length, model_width),
+        encoded.reshape(-1, model_width),
+        length,
+    )
+    weights = matrices + (norms[:3], norms[3:6])
+    (
+        packed, context, first_normed, first_inverse, first_low, cross_queries, pairs,
+        cross_context, second_normed, second_inverse, second_low, inner, active, third_normed,
+        third_inverse, third_low,
+    ) = (part.reshape(slots_here, -1, part.shape[-1]) for part in kept)
+    self_logsum = score_logsum(packed[..., :model_width], packed[..., model_width : 2 * model_width], True)
+    cross_logsum = score_logsum(cross_queries, pairs[..., :model_width], False)
+    stored = (
+        packed, context, self_logsum, first_normed, first_inverse[..., :1], first_low, cross_queries,
+        pairs, cross_context, cross_logsum, second_normed, second_inverse[..., :1], second_low, inner,
+        active, third_normed, third_inverse[..., :1],
+    )
     slot_index = lax.axis_index("pa") * slots_here + jnp.arange(slots_here)
     usable = (slot_mask[0] == 1) & (slot_index < slot_counts[0])
     small, grad_embed, grad_third = vocabulary_head(
@@ -1449,10 +1713,8 @@
     loss_value = small[0, 0]
     grad_prior = small[1].reshape(1, slots_here, length)[:, :, 0]
     pieces = lax.all_gather(grad_embed, "pb", axis=0)
-    repeated = 4 * grad_embed.shape[0] - embedding.shape[0]
-    grad_embed = jnp.concatenate(
-        [pieces[0], pieces[1], pieces[2], pieces[3][repeated:]]
-    ).astype(jnp.float32)
+    pieces = pieces.reshape(4 * grad_embed.shape[0], model_width)
+    grad_embed = pieces[: embedding.shape[0]].astype(jnp.float32)
     grad_third = grad_third.T.reshape(slots_here, length, model_width)
     grad_inputs, grad_encoded, grads = layer_backward(grad_third, inputs, encoded, weights, stored)
     low_grads = tuple(grad.astype(BFLOAT) for grad in grads[:7])

time: 832 us -> 795 us (0.956)
  matrix products: 107 us -> 79 us
  local copies, waits for them, and re-layouts: 95.3 us -> 86.1 us
    dot_general x9 -> x0, matrix products: 20.3 us -> none  [the longest x7 17.8 us: matmul(): lax.dot_general(matrix_left, matrix_right, (((matrix_left.ndim - 1,), (0,...]
    convert_element_type x4 -> x2, other arithmetic: 24.7 us -> 17 us  [the longest x1 14.5 us: per_device_kernels(): grad_embed = pieces[:embedding.shape[0]].astype(jnp.float32)]
    reshape x6 -> x5, local copies, waits for them, and re-layouts: 16.8 us -> 11.8 us  [join_heads(): return values.reshape(values.shape[0], values.shape[1], HEADS * HEAD_DIM)]
    unnamed x143 -> x115, local copies, waits for them, and re-layouts: 20.1 us -> 20.2 us
  transfers between devices with their start and end apart: 1 -> 1, of which waited for: 0 -> 0; matrix products, arithmetic and copies ran while one was open for 19% -> 22% of each run, Pallas kernels for 24% -> 25%
where the time goes in v3:
time: 795 us; the launch traced here: 784 us
  Pallas kernels  565 us (71%)
  local copies, waits for them, and re-layouts  86.1 us (11%)
  matrix products  79 us (10%)
  other arithmetic  37.9 us (5%)
  between operations  15.8 us (2%)
    pallas_call x1, Pallas kernels, reduce_grads(): pl.pallas_call(reduce_kernel, out_shape=tuple((jax.ShapeDtypeStruct(shape...  199 us
    pallas_call x1, Pallas kernels, vocabulary_head(): pl.pallas_call(functools.partial(head_kernel, slots, length, vocab_here),...  187 us
    pallas_call x1, Pallas kernels, forward_layer(): pl.pallas_call(functools.partial(forward_kernel, length, mem_length), out...  180 us
    dot_general x7, matrix products, outer_sum(): lax.dot_general(flat_left, flat_right, (((0,), (0,)), ((), ())), preferre...  30.3 us
    dot_general x7, matrix products, matmul_back(): lax.dot_general(matrix_left, matrix_right, (((matrix_left.ndim - 1,), (1,...  27.6 us
    unnamed x115, local copies, waits for them, and re-layouts  20.2 us
  transfers between devices with their start and end apart: 1, of which 0 were waited for; matrix products, arithmetic and copies ran while one was open for 22% of the time, Pallas kernels for 25%

profile of v3, /device:TPU:0, one launch (start us, length us, event | category | flops | bytes accessed | tf_op | source)
XLA Modules:
  0.0 784.3 jit_solution(15839602351198933762)
XLA Ops:
  16.0 179.7 %forward_layer.1 = (bf16[4,2,128,3072]{3,2,1,0:T(8,128)(2,1)}, bf16[4,2,128,1024]{3,2,1,0:T(8,128)(2,1)}, bf16[4,2,128,1024]{3,2,1,0:T(8,128)(2,1)}, bf16[4,2,12...) custom-call(bf16[128,3072]{1,0:T(8,128)(2,1)} %refs_0_.1, ...), custom_call_target="tpu_custom_call" | custom-call | tf_op jit(solution)/shard_map/forward_layer/pallas_call | solution.py:684
  198.4 187.1 %vocabulary_head.1 = (f32[8,128]{1,0:T(8,128)}, bf16[1584,1024]{1,0:T(8,128)(2,1)}, f32[1024,128]{1,0:T(8,128)}) custom-call(bf16[128,1024]{1,0:T(8,128)(2,1)} %copy-done.7, f32[8,128]{1,0:T(8,128)} %copy-done.46, bf16[6288,1024]{1,0:T(8,128)(2,1)} %refs_2_.3), custom_call_target="tpu_custom_call" | custom-call | tf_op jit(solution)/shard_map/vocabulary_head/pallas_call | solution.py:1151
  386.8 4.7 fusion.62
  391.5 3.9 copy.64
  404.4 2.4 multiply_reduce_fusion.3
  409.9 2.5 multiply_convert_fusion.3
  419.1 9.5 %fusion.21 = bf16[2,64,4096]{2,1,0:T(8,128)(2,1)S(1)} fusion(f32[2,64,4096]{2,1,0:T(8,128)S(1)} %bitcast.227, f32[2,64,4096]{2,1,0:T(8,128)S(1)} %bitcast.226, bf16[2,64,1024]{2,1,0:T(8,128)(2,1)S(1)} %bitcast.236, bf16[4096,1024,1]{1,0,2:T(8,128)(2,1)} %bitcast.257), kind=kOutput, calls=%fused_computation.27 | convolution fusion | flops 1109917696 | bytes 13893632 | tf_op jit(solution)/shard_map/dot_general | solution.py:1215
  428.8 3.1 fusion.60
  435.4 4.0 copy.66
  439.5 2.4 multiply_reduce_fusion.1
  461.3 2.3 convolution_convert_fusion.6
  475.0 4.6 fusion.29
  479.5 3.9 copy.85
  483.5 3.8 multiply_convert_fusion
  487.3 4.1 copy.84
  502.1 3.8 copy.91
  518.2 4.8 convolution_convert_fusion.2
  523.0 5.6 convolution_convert_fusion
  528.6 5.8 convolution_convert_fusion.1
  534.4 8.0 %fusion.8 = bf16[2048,1024]{0,1:T(8,128)(2,1)} fusion(bf16[1024,1024]{1,0:T(8,128)(2,1)S(1)} %bitcast.235, bf16[1024,1024]{0,1:T(8,128)(2,1)S(1)} %bitcast.232, bf16[1024,1024]{0,1:T(8,128)(2,1)S(1)} %bitcast.233), kind=kOutput, calls=%fused_computation.17 | convolution fusion | flops 4305453056 | bytes 10485760 | tf_op jit(solution)/shard_map/dot_general | solution.py:1226
  542.4 198.5 %reduce_grads.1 = (bf16[128,3072]{1,0:T(8,128)(2,1)S(1)}, bf16[128,1024]{1,0:T(8,128)(2,1)S(1)}, bf16[128,1024]{1,0:T(8,128)(2,1)S(1)}, bf16[128,2048]{1,0:T(8,1...) custom-call(bf16[4,2,128,3072]{3,2,1,0:T(8,128)(2,1)} %bitcast.188, ...), custom_call_target="tpu_custom_call" | custom-call | tf_op jit(solution)/shard_map/reduce_grads/pallas_call | solution.py:329
  750.2 5.9 fusion.36
  756.1 6.3 fusion.12
  762.4 14.5 %slice_convert_fusion = f32[6288,1024]{1,0:T(8,128)} fusion(bf16[6336,1024]{1,0:T(8,128)(2,1)} %all-gather.3.cloned.1.call-done), kind=kLoop, calls=%fused_computation | loop fusion | flops 6438912 | bytes 38633472 | tf_op jit(solution)/shard_map/convert_element_type | solution.py:1717
  (202 shorter events, 97.2 us)
Async XLA Ops:
  7.2 755.3 %all-gather.3.cloned.1.call-start = ((), (), s32[]{:S(2)}) async-start(), calls=%async_computation | async-start | bytes 16220160 | tf_op jit(solution)/shard_map/all_gather | solution.py:1715
  10.4 185.4 %copy-start.46 = (f32[8,128]{1,0:T(8,128)}, f32[8,128]{1,0:T(8,128)S(1)}, u32[]{:S(2)}) copy-start(f32[8,128]{1,0:T(8,128)S(1)} %scatter.14.refs_1_) | copy-start | bytes 12292
  416.9 11.8 %slice-start = ((s8[8388608]{0:T(1024)(128)(4,1)}), s8[4194304]{0:T(1024)(128)(4,1)S(1)}, s32[]{:S(2)}) async-start(s8[8388608]{0:T(1024)(128)(4,1)} %bitcast.195), calls=%async_computation.1 | async-start | bytes 8388608
  419.1 9.6 %slice-start.1 = ((s8[8388608]{0:T(1024)(128)(4,1)}), s8[4194304]{0:T(1024)(128)(4,1)S(1)}, s32[]{:S(2)}) async-start(s8[8388608]{0:T(1024)(128)(4,1)} %bitcast.195), calls=%async_computation.2 | async-start | bytes 8388608
  419.1 9.6 %copy-start.31 = (f32[128,1024]{1,0:T(8,128)S(1)}, f32[128,1024]{1,0:T(8,128)}, u32[]{:S(2)}) copy-start(f32[128,1024]{1,0:T(8,128)} %copy.60) | copy-start | bytes 1572868
  419.1 9.6 %copy-start.49 = (f32[2,64,1]{1,0,2:T(2,128)S(1)}, f32[2,64,1]{1,0,2:T(2,128)}, u32[]{:S(2)}) copy-start(f32[2,64,1]{1,0,2:T(2,128)} %copy-done.48) | copy-start | bytes 1540
  419.1 9.6 %copy-start.50 = (f32[2,64]{1,0:T(2,128)S(1)}, f32[2,64]{1,0:T(2,128)}, u32[]{:S(2)}) copy-start(f32[2,64]{1,0:T(2,128)} %div.25) | copy-start | bytes 1540
  419.1 9.6 %copy-start.51 = (f32[2,64]{1,0:T(2,128)S(1)}, f32[2,64]{1,0:T(2,128)}, u32[]{:S(2)}) copy-start(f32[2,64]{1,0:T(2,128)} %div.23) | copy-start | bytes 1540
  428.8 4.8 copy-start.28
  441.9 4.9 copy-start.10
  512.0 4.1 copy-start.26
  514.1 4.1 copy-start.1
  514.1 4.1 copy-start.38
  514.1 4.1 copy-start.39
  514.1 4.1 copy-start.40
  518.2 4.8 copy-start.23
  518.2 4.8 copy-start.24
  523.0 5.6 copy-start.16
  528.6 5.8 copy-start.35
  528.6 5.8 copy-start.36
  528.6 5.8 copy-start.37
  750.1 6.0 copy-start.33
  750.1 6.0 copy-start.34
  750.1 6.0 copy-start.52
  (32 other events, 57.9 us)
Sparse Core Ops, SparseCore 0:
  385.7 137.8 all-gather.2

commit v4 on v3

--- a/solution.py
+++ b/solution.py
@@ -63,298 +63,6 @@
 Z_FULL = (9, 14)
 
 
-LAGS = (0, 2, 4, 6, 8, 10)
-SIBLING_WINDOW = 2
-
-
-def reduce_kernel(*refs):
-    grads, norm, outs, norm_out = refs[:7], refs[7], refs[8:15], refs[15]
-    (
-        own, got, one, two, line, done, norm_here, norm_there, norm_line,
-        own_sem, d_send, d_recv, one_send, one_recv, two_send, two_recv,
-        z_send, z_recv, ag_send, ag_recv, ah_send, ah_recv, out_sem,
-        n_send, n_recv, nz_send, nz_recv,
-    ) = refs[16:]
-    x, y, z, c = whereami()
-    greet(neighbours(x, y, z, c))
-    count = len(UNITS)
-    every = slice(None)
-
-    def sibling_copy(u):
-        return pltpu.make_async_remote_copy(
-            src_ref=full_view(grads[UNITS[u][0]], UNITS[u], every, 1 - c, 0, ROWS),
-            dst_ref=got.at[u],
-            send_sem=d_send.at[u],
-            recv_sem=d_recv.at[u],
-            device_id=at(x, y, z, 1 - c),
-            device_id_type=MESH,
-        )
-
-    def own_copy(u):
-        return pltpu.make_async_copy(
-            full_view(grads[UNITS[u][0]], UNITS[u], every, c, 0, ROWS),
-            own.at[u % 2],
-            own_sem.at[u % 2],
-        )
-
-    for u in range(SIBLING_WINDOW):
-        sibling_copy(u).start()
-    own_copy(0).start()
-
-    def place(u):
-        even = lax.rem(u, 2) == 0
-        a = jnp.where(even, x, y)
-        b = jnp.where(even, y, x)
-        x_peer = y * 2 + (1 - x)
-        y_peer = (1 - y) * 2 + x
-        a_peer = (jnp.where(even, x_peer, y_peer), z * 2 + c)
-        b_peer = (jnp.where(even, y_peer, x_peer), z * 2 + c)
-        return a, b, a_peer, b_peer
-
-    def remote(src, dst, send, recv, peer):
-        return pltpu.make_async_remote_copy(
-            src_ref=src, dst_ref=dst, send_sem=send, recv_sem=recv, device_id=peer, device_id_type=MESH
-        )
-
-    def one_copy(u):
-        a, _, a_peer, _ = place(u)
-        return remote(
-            got.at[u, :, pl.ds(pl.multiple_of(64 * (1 - a), 64), 64), :],
-            one.at[u], one_send.at[u], one_recv.at[u], a_peer,
-        )
-
-    def two_copy(u):
-        _, b, _, b_peer = place(u)
-        return remote(
-            one.at[u, :, pl.ds(pl.multiple_of(32 * (1 - b), 32), 32), :],
-            two.at[u], two_send.at[u], two_recv.at[u], b_peer,
-        )
-
-    def line_copy(u, d):
-        other = lax.rem(z + d, 4)
-        return remote(
-            two.at[u, other], line.at[u, d - 1], z_send.at[u, d - 1], z_recv.at[u, d - 1],
-            at(x, y, other, c),
-        )
-
-    def ag_copy(u):
-        a, b, _, b_peer = place(u)
-        part = done.at[u, pl.ds(pl.multiple_of(64 * a + 32 * b, 32), 32), :]
-        return remote(part, part, ag_send.at[u], ag_recv.at[u], b_peer)
-
-    def ah_copy(u):
-        a, _, a_peer, _ = place(u)
-        part = done.at[u, pl.ds(pl.multiple_of(64 * a, 64), 64), :]
-        return remote(part, part, ah_send.at[u], ah_recv.at[u], a_peer)
-
-    norm_peers = (at(x, y, z, 1 - c), at(1 - x, y, z, c), at(x, 1 - y, z, c))
-
-    def norm_copy(n):
-        return remote(norm_here.at[n], norm_there.at[n], n_send.at[n], n_recv.at[n], norm_peers[n])
-
-    def norm_line_copy(d):
-        return remote(
-            norm_here.at[3], norm_line.at[d - 1], nz_send.at[d - 1], nz_recv.at[d - 1],
-            at(x, y, lax.rem(z + d, 4), c),
-        )
-
-    norm_here[0] = norm[...]
-    norm_copy(0).start()
-
-    def out_copy(u):
-        return pltpu.make_async_copy(
-            done.at[u], shard_view(outs[UNITS[u][0]], UNITS[u], 0, ROWS), out_sem.at[u]
-        )
-
-    def total(*parts):
-        out = parts[0].astype(jnp.float32)
-        for part in parts[1:]:
-            out = out + part.astype(jnp.float32)
-        return out.astype(BFLOAT)
-
-    @pl.loop(0, count + LAGS[-1])
-    def _(i):
-        u0 = i
-        for k in range(SIBLING_WINDOW, count):
-            @pl.when(i + SIBLING_WINDOW == k)
-            def _():
-                sibling_copy(k).start()
-
-        for k in range(1, count):
-            @pl.when(i + 1 == k)
-            def _():
-                own_copy(k).start()
-
-        @pl.when(i < count)
-        def _():
-            for k in range(count):
-                @pl.when(i == k)
-                def _():
-                    own_copy(k).wait()
-                    sibling_copy(k).wait_recv()
-
-            slot = lax.rem(u0, 2)
-
-            @pl.loop(0, 32)
-            def _(j):
-                zz, r = j // 8, pl.multiple_of(lax.rem(j, 8) * 16, 16)
-                got[u0, zz, pl.ds(r, 16), :] = total(
-                    got[u0, zz, pl.ds(r, 16), :], own[slot, zz, pl.ds(r, 16), :]
-                )
-
-            one_copy(u0).start()
-
-        for n in range(3):
-            @pl.when(i == 2 + 2 * n)
-            def _():
-                norm_copy(n).wait_recv()
-                norm_here[n + 1] = norm_here[n] + norm_there[n]
-                if n < 2:
-                    norm_copy(n + 1).start()
-                else:
-                    for d in (1, 2, 3):
-                        norm_line_copy(d).start()
-
-        @pl.when(i == 9)
-        def _():
-            for d in (1, 2, 3):
-                norm_line_copy(d).wait_recv()
-            norm_out[...] = ((norm_here[3] + norm_line[0]) + norm_line[1]) + norm_line[2]
-
-        u1 = i - LAGS[1]
-
-        @pl.when((u1 >= 0) & (u1 < count))
-        def _():
-            one_copy(u1).wait_recv()
-            a, _, _, _ = place(u1)
-
-            @pl.loop(0, 16)
-            def _(j):
-                zz, r = j // 4, pl.multiple_of(lax.rem(j, 4) * 16, 16)
-                one[u1, zz, pl.ds(r, 16), :] = total(
-                    one[u1, zz, pl.ds(r, 16), :],
-                    got[u1, zz, pl.ds(pl.multiple_of(64 * a + r, 16), 16), :],
-                )
-
-            two_copy(u1).start()
-
-        u2 = i - LAGS[2]
-
-        @pl.when((u2 >= 0) & (u2 < count))
-        def _():
-            two_copy(u2).wait_recv()
-            _, b, _, _ = place(u2)
-
-            @pl.loop(0, 8)
-            def _(j):
-                zz, r = j // 2, pl.multiple_of(lax.rem(j, 2) * 16, 16)
-                two[u2, zz, pl.ds(r, 16), :] = total(
-                    two[u2, zz, pl.ds(r, 16), :],
-                    one[u2, zz, pl.ds(pl.multiple_of(32 * b + r, 16), 16), :],
-                )
-
-            for d in (1, 2, 3):
-                line_copy(u2, d).start()
-
-        u3 = i - LAGS[3]
-
-        @pl.when((u3 >= 0) & (u3 < count))
-        def _():
-            for d in (1, 2, 3):
-                line_copy(u3, d).wait_recv()
-            a, b, _, _ = place(u3)
-
-            @pl.loop(0, 2)
-            def _(j):
-                r = pl.multiple_of(j * 16, 16)
-                done[u3, pl.ds(pl.multiple_of(64 * a + 32 * b + r, 16), 16), :] = total(
-                    two[u3, z, pl.ds(r, 16), :],
-                    line[u3, 0, pl.ds(r, 16), :],
-                    line[u3, 1, pl.ds(r, 16), :],
-                    line[u3, 2, pl.ds(r, 16), :],
-                )
-
-            ag_copy(u3).start()
-
-        u4 = i - LAGS[4]
-
-        @pl.when((u4 >= 0) & (u4 < count))
-        def _():
-            ag_copy(u4).wait_recv()
-            ah_copy(u4).start()
-
-        u5 = i - LAGS[5]
-
-        @pl.when((u5 >= 0) & (u5 < count))
-        def _():
-            ah_copy(u5).wait_recv()
-            for k in range(count):
-                @pl.when(u5 == k)
-                def _():
-                    out_copy(k).start()
-
-    for u in range(count):
-        sibling_copy(u).wait_send()
-
-    @pl.loop(0, count)
-    def _(u):
-        one_copy(u).wait_send()
-        two_copy(u).wait_send()
-        for d in (1, 2, 3):
-            line_copy(u, d).wait_send()
-        ag_copy(u).wait_send()
-        ah_copy(u).wait_send()
-
-    for u in range(count):
-        out_copy(u).wait()
-    for n in range(3):
-        norm_copy(n).wait_send()
-        norm_line_copy(n + 1).wait_send()
-
-
-def reduce_grads(grads, norm):
-    count = len(UNITS)
-    views = []
-    shapes = []
-    for w, grad in enumerate(grads):
-        rows, columns = grad.shape[0] // 8, grad.shape[1]
-        shapes.append((rows, columns))
-        if w == REDUCE_WEIGHT:
-            views.append(grad.reshape(4, 2, rows // ROWS, ROWS, columns))
-        else:
-            views.append(grad.reshape(4, 2, rows, columns))
-    sems = pltpu.SemaphoreType.DMA((count,))
-    every = pl.BlockSpec(memory_space=pl.ANY)
-    vmem = pl.BlockSpec(memory_space=pltpu.VMEM)
-    *shares, norm_sum = pl.pallas_call(
-        reduce_kernel,
-        out_shape=tuple(jax.ShapeDtypeStruct(shape, BFLOAT) for shape in shapes)
-        + (jax.ShapeDtypeStruct(norm.shape, norm.dtype),),
-        in_specs=[every] * 7 + [vmem],
-        out_specs=(every,) * 7 + (vmem,),
-        scratch_shapes=[
-            pltpu.VMEM((2, 4, ROWS, TILE), BFLOAT),
-            pltpu.VMEM((count, 4, ROWS, TILE), BFLOAT),
-            pltpu.VMEM((count, 4, 64, TILE), BFLOAT),
-            pltpu.VMEM((count, 4, 32, TILE), BFLOAT),
-            pltpu.VMEM((count, 3, 32, TILE), BFLOAT),
-            pltpu.VMEM((count, ROWS, TILE), BFLOAT),
-            pltpu.VMEM((4,) + norm.shape, norm.dtype),
-            pltpu.VMEM((3,) + norm.shape, norm.dtype),
-            pltpu.VMEM((3,) + norm.shape, norm.dtype),
-            pltpu.SemaphoreType.DMA((2,)),
-            sems, sems, sems, sems, sems, sems,
-            pltpu.SemaphoreType.DMA((count, 3)),
-            pltpu.SemaphoreType.DMA((count, 3)),
-            sems, sems, sems, sems, sems,
-        ]
-        + [pltpu.SemaphoreType.DMA((3,))] * 4,
-        compiler_params=pltpu.CompilerParams(
-            collective_id=1, has_side_effects=True, vmem_limit_bytes=48 * 2**20
-        ),
-        name="reduce_grads",
-    )(*views, norm)
-    return tuple(share.astype(jnp.float32) for share in shares), norm_sum
 GATHER_WINDOW = 4
 LAG_TWO, LAG_SIBLING, LAG_LOAD, LAG_USE = 1, 2, 4, 5
 SLOTS_IN_FLIGHT = 3
@@ -705,8 +413,627 @@
         name="forward_layer",
     )(*weights, norm, states, encoded)
     fulls = tuple(full.reshape(-1, full.shape[-1]) for full in results[:7])
-    norm_full = results[7].reshape(8, norm.shape[0], norm.shape[1]).transpose(1, 0, 2)
-    return fulls, norm_full.reshape(norm.shape[0], -1), results[8:]
+    return fulls, results[7], results[8:]
+
+
+SEQUENCE = tuple((6, k) for k in range(4)) + tuple((5, k) for k in range(4)) + (
+    (4, 0), (2, 0), (3, 0), (3, 1), (1, 0), (0, 0), (0, 1), (0, 2),
+)
+LINE_FIRST = 5
+LINE_LAGS = (12, 14, 16, 18, 20)
+CROSS_LAGS = (2, 4, 6, 8, 10)
+TURNS = 27
+READS = tuple(read for k in range(4) for read in ((6, k), (5, k))) + (
+    (4, 0), (2, 0), (1, 0), (0, 0), (0, 1), (0, 2), (3, 0), (3, 1),
+)
+
+
+def norm_back(upstream, normed, inverse, gain):
+    scaled = upstream * gain
+    mean_scaled = jnp.mean(scaled, -1, keepdims=True)
+    along = jnp.mean(scaled * normed, -1, keepdims=True)
+    return (
+        inverse * (scaled - mean_scaled - normed * along),
+        jnp.sum(upstream * normed, 0, keepdims=True),
+        jnp.sum(upstream, 0, keepdims=True),
+    )
+
+
+def attend_pair_back(grad, queries, keys, values, causal):
+    scale = 1.0 / math.sqrt(HEAD_DIM)
+    queries, grad = stack_heads(queries), stack_heads(grad)
+    probs = pair_scores(queries, keys, causal)
+    grad_probs = dot_nt(grad, values)
+    grad_values = dot_tn(probs.astype(BFLOAT), grad).astype(BFLOAT)
+    grad_scores = (
+        probs * (grad_probs - jnp.sum(probs * grad_probs, -1, keepdims=True))
+    ).astype(BFLOAT)
+    grad_queries = unstack_heads(dot_nn(grad_scores, keys) * scale).astype(BFLOAT)
+    grad_keys = (dot_tn(grad_scores, queries) * scale).astype(BFLOAT)
+    return grad_queries, grad_keys, grad_values
+
+
+def backward_kernel(length, mem_length, *refs):
+    weights = refs[:7]
+    kept_hbm = refs[7:23]
+    inner_hbm = refs[23]
+    norm_full, grad_third = refs[24:26]
+    outs = refs[26:33]
+    norm_out, grad_states, grad_memory, landing = refs[33:37]
+    kept = refs[37:53]
+    (
+        wbuf, inner, stage, got, zload, one_line, two_line, one, two, line, fin,
+        resid, low, grad_low, grad_context, grad_queries, grad_packed, memory_part,
+        norm_here, norm_there, norm_line,
+    ) = refs[53:74]
+    (
+        kept_sem, w_sem, inner_sem, dd_send, dd_recv, z_send, z_recv, zload_sem,
+        ra_send, ra_recv, rb_send, rb_recv, rz_send, rz_recv, ag_send, ag_recv, ah_send, ah_recv,
+        fin_sem, memory_sem, n_send, n_recv, nz_send, nz_recv,
+    ) = refs[74:]
+    (
+        packed, context, first_normed, first_inverse, first_low, cross_queries, pairs, cross_context,
+        second_normed, second_inverse, second_low, active, third_normed, third_inverse, states, encoded,
+    ) = kept
+    x, y, z, c = whereami()
+    greet(neighbours(x, y, z, c))
+    tokens, width = states.shape
+    slots_here = tokens // length
+    count = len(SEQUENCE)
+    blocks = active.shape[1] // (8 * ROWS)
+
+    def keep_copy(n):
+        return pltpu.make_async_copy(kept_hbm[n], kept[n], kept_sem.at[n])
+
+    first_needed = (12, 13, 11, 10)
+    for n in first_needed:
+        keep_copy(n).start()
+    for n in range(16):
+        if n not in first_needed:
+            keep_copy(n).start()
+
+    def need(*names):
+        for n in names:
+            keep_copy(n).wait()
+
+    def read_copy(n):
+        weight, k = READS[n]
+        if weight == REDUCE_WEIGHT:
+            source = weights[weight].at[pl.ds(k * TILE, TILE), :]
+        else:
+            source = weights[weight].at[:, pl.ds(k * TILE, TILE)]
+        return pltpu.make_async_copy(source, wbuf.at[n % 2], w_sem.at[n % 2])
+
+    def inner_copy(k):
+        return pltpu.make_async_copy(
+            inner_hbm.at[:, pl.ds(k * TILE, TILE)], inner.at[k % 2], inner_sem.at[k % 2]
+        )
+
+    read_copy(0).start()
+    read_copy(1).start()
+    inner_copy(0).start()
+    inner_copy(1).start()
+
+    def remote(src, dst, send, recv, peer):
+        return pltpu.make_async_remote_copy(
+            src_ref=src, dst_ref=dst, send_sem=send, recv_sem=recv, device_id=peer, device_id_type=MESH
+        )
+
+    def norm_row(n):
+        return jnp.concatenate([norm_full[p // 2, p % 2, n : n + 1, :] for p in range(8)], 1)
+
+    def place(q):
+        even = lax.rem(q, 2) == 0
+        a = jnp.where(even, x, y)
+        b = jnp.where(even, y, x)
+        x_peer = y * 2 + (1 - x)
+        y_peer = (1 - y) * 2 + x
+        a_peer = (jnp.where(even, x_peer, y_peer), z * 2 + c)
+        b_peer = (jnp.where(even, y_peer, x_peer), z * 2 + c)
+        return a, b, a_peer, b_peer
+
+    def piece(index, size):
+        return pl.ds(pl.multiple_of(index * size, size), size)
+
+    def total(*parts):
+        out = parts[0].astype(jnp.float32)
+        for part in parts[1:]:
+            out = out + part.astype(jnp.float32)
+        return out.astype(BFLOAT)
+
+    def dd_copy(q):
+        return remote(
+            stage.at[lax.rem(q, 2), 1 - c], got.at[q], dd_send.at[q], dd_recv.at[q], at(x, y, z, 1 - c)
+        )
+
+    def line_copy(q, d):
+        other = lax.rem(z + d, 4)
+        return remote(
+            got.at[q, other], landing.at[q, d - 1], z_send.at[q, d - 1], z_recv.at[q, d - 1],
+            at(x, y, other, c),
+        )
+
+    def ra_line(q):
+        a, _, a_peer, _ = place(q)
+        return remote(got.at[q, z, piece(1 - a, 64), :], one_line.at[q], ra_send.at[q], ra_recv.at[q], a_peer)
+
+    def rb_line(q):
+        _, b, _, b_peer = place(q)
+        return remote(one_line.at[q, piece(1 - b, 32), :], two_line.at[q], rb_send.at[q], rb_recv.at[q], b_peer)
+
+    def ra_cross(q):
+        a, _, a_peer, _ = place(q)
+        return remote(
+            got.at[q, :, piece(1 - a, 64), :], one.at[q - LINE_FIRST], ra_send.at[q], ra_recv.at[q], a_peer
+        )
+
+    def rb_cross(q):
+        _, b, _, b_peer = place(q)
+        return remote(
+            one.at[q - LINE_FIRST, :, piece(1 - b, 32), :], two.at[q - LINE_FIRST],
+            rb_send.at[q], rb_recv.at[q], b_peer,
+        )
+
+    def rz_cross(q, d):
+        other = lax.rem(z + d, 4)
+        n = q - LINE_FIRST
+        return remote(
+            two.at[n, other], line.at[n, d - 1], rz_send.at[n, d - 1], rz_recv.at[n, d - 1],
+            at(x, y, other, c),
+        )
+
+    def out_view(q, start, size):
+        return shard_view(outs[SEQUENCE[q][0]], SEQUENCE[q], start, size)
+
+    def quarter_start(q):
+        a, b, _, _ = place(q)
+        return pl.multiple_of(64 * a + 32 * b, 32)
+
+    def fin_copy(q):
+        return pltpu.make_async_copy(fin.at[q], out_view(q, quarter_start(q), 32), fin_sem.at[q])
+
+    def ag_copy(q):
+        return remote(
+            fin.at[q], out_view(q, quarter_start(q), 32), ag_send.at[q], ag_recv.at[q], place(q)[3]
+        )
+
+    def ah_copy(q):
+        a, _, a_peer, _ = place(q)
+        part = out_view(q, pl.multiple_of(64 * a, 64), 64)
+        return remote(part, part, ah_send.at[q], ah_recv.at[q], a_peer)
+
+    norm_peers = (at(x, y, z, 1 - c), at(1 - x, y, z, c), at(x, 1 - y, z, c))
+
+    def norm_copy(n):
+        return remote(norm_here.at[n], norm_there.at[n], n_send.at[n], n_recv.at[n], norm_peers[n])
+
+    def norm_line_copy(d):
+        return remote(
+            norm_here.at[3], norm_line.at[d - 1], nz_send.at[d - 1], nz_recv.at[d - 1],
+            at(x, y, lax.rem(z + d, 4), c),
+        )
+
+    def outer(q, left, start, step, right):
+        slot = q % 2
+
+        @pl.loop(0, 8)
+        def _(p):
+            lanes = pl.ds(pl.multiple_of(start + p * step, 128), 128)
+            stage[slot, lax.rem(p, 2), p // 2] = dot_tn(left[:, lanes], right()).astype(BFLOAT)
+
+    def back_times(left, n, write):
+        slot = n % 2
+        read_copy(n).wait()
+
+        @pl.loop(0, 4)
+        def _(m):
+            write(piece(m, 256), dot_nt(left[...], wbuf[slot, piece(m, 256), :]))
+
+        if n + 2 < len(READS):
+            read_copy(n + 2).start()
+
+    def add_resid(columns, value):
+        resid[:, columns] = resid[:, columns] + value
+
+    def finish_norm(n, normed, inverse):
+        value, gain, shift = norm_back(resid[...], normed[...], inverse[:, 0:1], norm_row(n))
+        resid[...] = value
+        low[...] = value.astype(BFLOAT)
+        norm_here[0, n : n + 1, :] = gain
+        norm_here[0, n + 3 : n + 4, :] = shift
+
+    def attention_back(queries, keys, key_start, value_start, key_length, out, out_keys, causal):
+        @pl.loop(0, slots_here * (width // 128))
+        def _(n):
+            slot, group = n // (width // 128), lax.rem(n, width // 128)
+            lanes = piece(group, 128)
+            key_lanes = pl.ds(pl.multiple_of(key_start + group * 128, 128), 128)
+            value_lanes = pl.ds(pl.multiple_of(value_start + group * 128, 128), 128)
+            query_rows = piece(slot, length)
+            key_rows = piece(slot, key_length)
+            grad_query, grad_key, grad_value = attend_pair_back(
+                grad_context[query_rows, lanes],
+                queries[query_rows, lanes],
+                keys[key_rows, key_lanes],
+                keys[key_rows, value_lanes],
+                causal,
+            )
+            out[query_rows, lanes] = grad_query
+            out_keys[key_rows, key_lanes] = grad_key
+            out_keys[key_rows, value_lanes] = grad_value
+
+    def produce(q):
+        weight, k = SEQUENCE[q]
+        if q == 0:
+            norm_here[0] = jnp.zeros_like(norm_here[0])
+            for p in range(8):
+                resid[:, p * 128 : (p + 1) * 128] = grad_third[p * 128 : (p + 1) * 128, :].T
+            need(12, 13, 11)
+            finish_norm(2, third_normed, third_inverse)
+        if weight == 6:
+            outer(q, active, k * ROWS, blocks * ROWS, lambda: low[...])
+        elif weight == 5:
+            if k == 0:
+                need(10)
+            inner_copy(k).wait()
+
+            def write(columns, value):
+                pre = inner[k % 2, :, columns]
+                slope = 0.5 * (1.0 + lax.erf(pre * math.sqrt(0.5))) + pre * jnp.exp(
+                    -0.5 * pre * pre
+                ) * (1.0 / math.sqrt(2.0 * math.pi))
+                grad_low[:, columns] = (value * slope).astype(BFLOAT)
+
+            back_times(low, 2 * k, write)
+            if k + 2 < 4:
+                inner_copy(k + 2).start()
+            outer(q, second_low, 0, ROWS, lambda: grad_low[...])
+            back_times(grad_low, 2 * k + 1, add_resid)
+        elif weight == 4:
+            need(8, 9, 7)
+            finish_norm(1, second_normed, second_inverse)
+            outer(q, cross_context, 0, ROWS, lambda: low[...])
+
+            def write(columns, value):
+                grad_context[:, columns] = value.astype(BFLOAT)
+
+            back_times(low, 8, write)
+        elif weight == 2:
+            need(5, 6, 4, 2, 3)
+            attention_back(cross_queries, pairs, 0, width, mem_length, grad_queries, pairs, False)
+            outer(q, first_low, 0, ROWS, lambda: grad_queries[...])
+            back_times(grad_queries, 9, add_resid)
+            finish_norm(0, first_normed, first_inverse)
+        elif weight == 3:
+            if k == 0:
+                need(15)
+            outer(q, encoded, 0, ROWS, lambda: pairs[:, pl.ds(k * TILE, TILE)])
+        elif weight == 1:
+            need(1, 0, 14)
+            outer(q, context, 0, ROWS, lambda: low[...])
+
+            def write(columns, value):
+                grad_context[:, columns] = value.astype(BFLOAT)
+
+            back_times(low, 10, write)
+            attention_back(packed, packed, width, 2 * width, length, grad_packed, grad_packed, True)
+        else:
+            def part():
+                return grad_packed[:, pl.ds(k * TILE, TILE)]
+
+            outer(q, states, 0, ROWS, part)
+            back_times(grad_packed.at[:, pl.ds(k * TILE, TILE)], 11 + k, add_resid)
+            if k == 2:
+                grad_states[...] = resid[...]
+
+    memory_rows = encoded.shape[0] // 8
+
+    def memory_copy(m):
+        return pltpu.make_async_copy(
+            memory_part.at[m % 2], grad_memory.at[pl.ds(m * memory_rows, memory_rows), :], memory_sem.at[m % 2]
+        )
+
+    def memory_chunk(m):
+        if m == 0:
+            read_copy(14).wait()
+            read_copy(15).wait()
+        if m >= 2:
+            memory_copy(m - 2).wait()
+        rows_here = pl.ds(m * memory_rows, memory_rows)
+
+        @pl.loop(0, 4)
+        def _(n):
+            memory_part[m % 2, :, piece(n, 256)] = dot_nt(
+                pairs[rows_here, :width], wbuf[0, piece(n, 256), :]
+            ) + dot_nt(pairs[rows_here, width:], wbuf[1, piece(n, 256), :])
+
+        memory_copy(m).start()
+
+    def each(q, action):
+        for k in range(count):
+            @pl.when(q == k)
+            def _():
+                action(k)
+
+    def finish_block(q):
+        def action(k):
+            fin_copy(k).start()
+            ag_copy(k).start()
+
+        each(q, action)
+
+    step = 16
+
+    @pl.loop(0, TURNS)
+    def _(i):
+        for q in range(count):
+            @pl.when(i == q)
+            def _():
+                if q >= 2:
+                    dd_copy(q - 2).wait_send()
+                produce(q)
+                dd_copy(q).start()
+
+        for m in range(8):
+            @pl.when(i == count + 1 + m)
+            def _():
+                memory_chunk(m)
+
+        qs = i - 1
+
+        @pl.when((qs >= 0) & (qs < count))
+        def _():
+            dd_copy(qs).wait_recv()
+            slot = lax.rem(qs, 2)
+
+            @pl.loop(0, 32)
+            def _(j):
+                zz, rows_here = j // 8, piece(lax.rem(j, 8), step)
+                got[qs, zz, rows_here, :] = total(got[qs, zz, rows_here, :], stage[slot, c, zz, rows_here, :])
+
+            @pl.when(qs < LINE_FIRST)
+            def _():
+                for d in (1, 2, 3):
+                    line_copy(qs, d).start()
+
+            @pl.when(qs >= LINE_FIRST)
+            def _():
+                ra_cross(qs).start()
+
+        q0 = i - LINE_LAGS[0]
+
+        @pl.when((q0 >= 0) & (q0 < LINE_FIRST))
+        def _():
+            for d in (1, 2, 3):
+                line_copy(q0, d).wait_recv()
+            load = pltpu.make_async_copy(landing.at[q0], zload, zload_sem)
+            load.start()
+            load.wait()
+
+            @pl.loop(0, 8)
+            def _(j):
+                rows_here = piece(j, step)
+                got[q0, z, rows_here, :] = total(
+                    got[q0, z, rows_here, :], zload[0, rows_here, :], zload[1, rows_here, :],
+                    zload[2, rows_here, :],
+                )
+
+            ra_line(q0).start()
+
+        q1 = i - LINE_LAGS[1]
+
+        @pl.when((q1 >= 0) & (q1 < LINE_FIRST))
+        def _():
+            ra_line(q1).wait_recv()
+            a = place(q1)[0]
+
+            @pl.loop(0, 4)
+            def _(j):
+                rows_here = piece(j, step)
+                one_line[q1, rows_here, :] = total(
+                    one_line[q1, rows_here, :],
+                    got[q1, z, pl.ds(pl.multiple_of(64 * a + j * step, step), step), :],
+                )
+
+            rb_line(q1).start()
+
+        q2 = i - LINE_LAGS[2]
+
+        @pl.when((q2 >= 0) & (q2 < LINE_FIRST))
+        def _():
+            rb_line(q2).wait_recv()
+            b = place(q2)[1]
+
+            @pl.loop(0, 2)
+            def _(j):
+                rows_here = piece(j, step)
+                fin[q2, rows_here, :] = total(
+                    two_line[q2, rows_here, :],
+                    one_line[q2, pl.ds(pl.multiple_of(32 * b + j * step, step), step), :],
+                )
+
+            finish_block(q2)
+
+        p0 = i - CROSS_LAGS[0]
+
+        @pl.when((p0 >= LINE_FIRST) & (p0 < count))
+        def _():
+            ra_cross(p0).wait_recv()
+            a = place(p0)[0]
+
+            @pl.loop(0, 16)
+            def _(j):
+                zz, r = j // 4, lax.rem(j, 4)
+                rows_here = piece(r, step)
+                one[p0 - LINE_FIRST, zz, rows_here, :] = total(
+                    one[p0 - LINE_FIRST, zz, rows_here, :],
+                    got[p0, zz, pl.ds(pl.multiple_of(64 * a + r * step, step), step), :],
+                )
+
+            rb_cross(p0).start()
+
+        p1 = i - CROSS_LAGS[1]
+
+        @pl.when((p1 >= LINE_FIRST) & (p1 < count))
+        def _():
+            rb_cross(p1).wait_recv()
+            b = place(p1)[1]
+
+            @pl.loop(0, 8)
+            def _(j):
+                zz, r = j // 2, lax.rem(j, 2)
+                rows_here = piece(r, step)
+                two[p1 - LINE_FIRST, zz, rows_here, :] = total(
+                    two[p1 - LINE_FIRST, zz, rows_here, :],
+                    one[p1 - LINE_FIRST, zz, pl.ds(pl.multiple_of(32 * b + r * step, step), step), :],
+                )
+
+            for d in (1, 2, 3):
+                rz_cross(p1, d).start()
+
+        p2 = i - CROSS_LAGS[2]
+
+        @pl.when((p2 >= LINE_FIRST) & (p2 < count))
+        def _():
+            for d in (1, 2, 3):
+                rz_cross(p2, d).wait_recv()
+            n = p2 - LINE_FIRST
+
+            @pl.loop(0, 2)
+            def _(j):
+                rows_here = piece(j, step)
+                fin[p2, rows_here, :] = total(
+                    two[n, z, rows_here, :], line[n, 0, rows_here, :], line[n, 1, rows_here, :],
+                    line[n, 2, rows_here, :],
+                )
+
+            finish_block(p2)
+
+        def pass_on(k):
+            ag_copy(k).wait_recv()
+            fin_copy(k).wait()
+            ah_copy(k).start()
+
+        for lags, low_q, high_q in ((LINE_LAGS, 0, LINE_FIRST), (CROSS_LAGS, LINE_FIRST, count)):
+            q3 = i - lags[3]
+
+            @pl.when((q3 >= low_q) & (q3 < high_q))
+            def _():
+                each(q3, pass_on)
+
+            q4 = i - lags[4]
+
+            @pl.when((q4 >= low_q) & (q4 < high_q))
+            def _():
+                each(q4, lambda k: ah_copy(k).wait_recv())
+
+        @pl.when(i == count)
+        def _():
+            norm_copy(0).start()
+
+        for n in range(3):
+            @pl.when(i == count + 2 * (n + 1))
+            def _():
+                norm_copy(n).wait_recv()
+                norm_here[n + 1] = norm_here[n] + norm_there[n]
+                if n < 2:
+                    norm_copy(n + 1).start()
+                else:
+                    for d in (1, 2, 3):
+                        norm_line_copy(d).start()
+
+        @pl.when(i == count + 8)
+        def _():
+            for d in (1, 2, 3):
+                norm_line_copy(d).wait_recv()
+            norm_out[...] = ((norm_here[3] + norm_line[0]) + norm_line[1]) + norm_line[2]
+
+    memory_copy(6).wait()
+    memory_copy(7).wait()
+    dd_copy(count - 2).wait_send()
+    dd_copy(count - 1).wait_send()
+
+    @pl.loop(0, LINE_FIRST)
+    def _(q):
+        for d in (1, 2, 3):
+            line_copy(q, d).wait_send()
+        ra_line(q).wait_send()
+        rb_line(q).wait_send()
+
+    @pl.loop(LINE_FIRST, count)
+    def _(q):
+        ra_cross(q).wait_send()
+        rb_cross(q).wait_send()
+        for d in (1, 2, 3):
+            rz_cross(q, d).wait_send()
+
+    for q in range(count):
+        ag_copy(q).wait_send()
+        ah_copy(q).wait_send()
+    for n in range(3):
+        norm_copy(n).wait_send()
+        norm_line_copy(n + 1).wait_send()
+
+
+def backward_layer(weights, kept, inner, norm_full, grad_third, length):
+    count = len(SEQUENCE)
+    f32 = jnp.float32
+    tokens, width = kept[14].shape
+    mem_tokens = kept[15].shape[0]
+    mem_length = mem_tokens // (tokens // length)
+    shapes = [(weight.shape[0] // 8, weight.shape[1]) for weight in weights]
+    every = pl.BlockSpec(memory_space=pl.ANY)
+    vmem = pl.BlockSpec(memory_space=pltpu.VMEM)
+    dma = pltpu.SemaphoreType.DMA
+    sems = dma((count,))
+    crossed = count - LINE_FIRST
+    *shares, norm_sum, grad_states, grad_memory, _ = pl.pallas_call(
+        functools.partial(backward_kernel, length, mem_length),
+        out_shape=tuple(jax.ShapeDtypeStruct(shape, BFLOAT) for shape in shapes)
+        + (
+            jax.ShapeDtypeStruct((8, width), f32),
+            jax.ShapeDtypeStruct((tokens, width), f32),
+            jax.ShapeDtypeStruct((mem_tokens, width), f32),
+            jax.ShapeDtypeStruct((LINE_FIRST, 3, ROWS, TILE), BFLOAT),
+        ),
+        in_specs=[every] * 24 + [vmem] * 2,
+        out_specs=(every,) * 7 + (vmem, vmem, every, every),
+        scratch_shapes=[pltpu.VMEM(part.shape, part.dtype) for part in kept]
+        + [
+            pltpu.VMEM((2, TILE, TILE), BFLOAT),
+            pltpu.VMEM((2, tokens, TILE), f32),
+            pltpu.VMEM((2, 2, 4, ROWS, TILE), BFLOAT),
+            pltpu.VMEM((count, 4, ROWS, TILE), BFLOAT),
+            pltpu.VMEM((3, ROWS, TILE), BFLOAT),
+            pltpu.VMEM((LINE_FIRST, 64, TILE), BFLOAT),
+            pltpu.VMEM((LINE_FIRST, 32, TILE), BFLOAT),
+            pltpu.VMEM((crossed, 4, 64, TILE), BFLOAT),
+            pltpu.VMEM((crossed, 4, 32, TILE), BFLOAT),
+            pltpu.VMEM((crossed, 3, 32, TILE), BFLOAT),
+            pltpu.VMEM((count, 32, TILE), BFLOAT),
+            pltpu.VMEM((tokens, width), f32),
+            pltpu.VMEM((tokens, width), BFLOAT),
+            pltpu.VMEM((tokens, TILE), BFLOAT),
+            pltpu.VMEM((tokens, width), BFLOAT),
+            pltpu.VMEM((tokens, width), BFLOAT),
+            pltpu.VMEM((tokens, 3 * width), BFLOAT),
+            pltpu.VMEM((2, mem_tokens // 8, width), f32),
+            pltpu.VMEM((4, 8, width), f32),
+            pltpu.VMEM((3, 8, width), f32),
+            pltpu.VMEM((3, 8, width), f32),
+            dma((16,)), dma((2,)), dma((2,)), sems, sems,
+            dma((LINE_FIRST, 3)), dma((LINE_FIRST, 3)), dma,
+            sems, sems, sems, sems,
+            dma((crossed, 3)), dma((crossed, 3)),
+            sems, sems, sems, sems, sems, dma((2,)),
+            dma((3,)), dma((3,)), dma((3,)), dma((3,)),
+        ],
+        compiler_params=pltpu.CompilerParams(
+            collective_id=1, has_side_effects=True, vmem_limit_bytes=62 * 2**20
+        ),
+        name="backward_layer",
+    )(*weights, *kept, inner, norm_full, grad_third)
+    return tuple(share.astype(f32) for share in shares), norm_sum, grad_states, grad_memory
 
 
 VOCAB_CUTS = 3
@@ -1639,12 +1966,6 @@
     )
 
 
-def score_logsum(queries, key_rows, causal):
-    scores = score_block(split_heads(queries), split_heads(key_rows), causal)
-    highest = jnp.max(scores, -1, keepdims=True)
-    return highest + jnp.log(jnp.sum(jnp.exp(scores - highest), -1, keepdims=True))
-
-
 def per_device_kernels(
     decoder_states,
     encoder_memory,
@@ -1677,32 +1998,13 @@
     ).astype(jnp.float32)
     _, slots_here, length, model_width = decoder_states.shape
     slots = slots_here * lax.axis_size("pa")
-    inputs = decoder_states[0]
-    encoded = encoder_memory[0]
-    matrices, norms, kept = forward_layer(
-        shards,
-        norm_rows,
-        inputs.reshape(slots_here * length, model_width),
-        encoded.reshape(-1, model_width),
-        length,
-    )
-    weights = matrices + (norms[:3], norms[3:6])
-    (
-        packed, context, first_normed, first_inverse, first_low, cross_queries, pairs,
-        cross_context, second_normed, second_inverse, second_low, inner, active, third_normed,
-        third_inverse, third_low,
-    ) = (part.reshape(slots_here, -1, part.shape[-1]) for part in kept)
-    self_logsum = score_logsum(packed[..., :model_width], packed[..., model_width : 2 * model_width], True)
-    cross_logsum = score_logsum(cross_queries, pairs[..., :model_width], False)
-    stored = (
-        packed, context, self_logsum, first_normed, first_inverse[..., :1], first_low, cross_queries,
-        pairs, cross_context, cross_logsum, second_normed, second_inverse[..., :1], second_low, inner,
-        active, third_normed, third_inverse[..., :1],
-    )
+    states = decoder_states.reshape(slots_here * length, model_width)
+    memory = encoder_memory.reshape(-1, model_width)
+    matrices, norms, kept = forward_layer(shards, norm_rows, states, memory, length)
     slot_index = lax.axis_index("pa") * slots_here + jnp.arange(slots_here)
     usable = (slot_mask[0] == 1) & (slot_index < slot_counts[0])
     small, grad_embed, grad_third = vocabulary_head(
-        third_low.reshape(slots_here * length, model_width),
+        kept[-1],
         target_tokens.reshape(slots_here * length),
         log_prior[0],
         usable,
@@ -1715,11 +2017,14 @@
     pieces = lax.all_gather(grad_embed, "pb", axis=0)
     pieces = pieces.reshape(4 * grad_embed.shape[0], model_width)
     grad_embed = pieces[: embedding.shape[0]].astype(jnp.float32)
-    grad_third = grad_third.T.reshape(slots_here, length, model_width)
-    grad_inputs, grad_encoded, grads = layer_backward(grad_third, inputs, encoded, weights, stored)
-    low_grads = tuple(grad.astype(BFLOAT) for grad in grads[:7])
-    norm_grads = jnp.concatenate([grads[7], grads[8], jnp.zeros((2, model_width), jnp.float32)])
-    shares, norm_sums = reduce_grads(low_grads, norm_grads)
+    shares, norm_sums, grad_inputs, grad_encoded = backward_layer(
+        matrices,
+        kept[:11] + kept[12:15] + (states, memory),
+        kept[11],
+        norms,
+        grad_third,
+        length,
+    )
     norm_here = norm_gains.shape[1]
     norm_sums = lax.dynamic_slice_in_dim(
         norm_sums, lax.axis_index("pa") * norm_here, norm_here, axis=1

time: 795 us -> 712 us (0.90); the launches traced: 784 us -> 711 us
  Pallas kernels: 565 us -> 646 us
  matrix products: 79 us -> 0 us
  local copies, waits for them, and re-layouts: 86.1 us -> 22.6 us
  other arithmetic: 37.9 us -> 28.2 us
    pallas_call x1, Pallas kernels: 199 us -> 279 us  [backward_layer(): pl.pallas_call(functools.partial(backward_kernel, length, mem_length), ou...]
    dot_general x24 -> x0, matrix products: 79 us -> none  [the longest x7 30.3 us: outer_sum(): lax.dot_general(flat_left, flat_right, (((0,), (0,)), ((), ())), preferre...]
    reshape x10 -> x0, local copies, waits for them, and re-layouts: 18.9 us -> none  [the longest x5 11.8 us: join_heads(): return values.reshape(values.shape[0], values.shape[1], HEADS * HEAD_DIM)]
    slice x5 -> x0, local copies, waits for them, and re-layouts: 14.3 us -> none  [the longest x2 8.66 us: layer_backward(): memory_pairs[..., model_width:]]
    convert_element_type x7 -> x0, local copies, waits for them, and re-layouts: 12 us -> none  [the longest x2 5.99 us: attend_back(): grad_values = jnp.einsum('nhqk,nqhd->nkhd', probs_full.astype(BFLOAT), gr...]
    unnamed x115 -> x56, local copies, waits for them, and re-layouts: 20.2 us -> 17.6 us
  transfers between devices with their start and end apart: 1 -> 1, of which waited for: 0 -> 0; matrix products, arithmetic and copies ran while one was open for 22% -> 2% of each run, Pallas kernels for 25% -> 39%
where the time goes in v4:
time: 712 us; the launch traced here: 711 us
  Pallas kernels  646 us (91%)
  other arithmetic  28.2 us (4%)
  local copies, waits for them, and re-layouts  22.6 us (3%)
  between operations  14.8 us (2%)
    pallas_call x1, Pallas kernels, backward_layer(): pl.pallas_call(functools.partial(backward_kernel, length, mem_length), ou...  279 us
    pallas_call x1, Pallas kernels, vocabulary_head(): pl.pallas_call(functools.partial(head_kernel, slots, length, vocab_here),...  187 us
    pallas_call x1, Pallas kernels, forward_layer(): pl.pallas_call(functools.partial(forward_kernel, length, mem_length), out...  180 us
    unnamed x56, local copies, waits for them, and re-layouts  17.6 us
    convert_element_type x1, other arithmetic, per_device_kernels(): grad_embed = pieces[:embedding.shape[0]].astype(jnp.float32)  15.5 us
  transfers between devices with their start and end apart: 1, of which 0 were waited for; matrix products, arithmetic and copies ran while one was open for 2% of the time, Pallas kernels for 39%

profile of v4, /device:TPU:0, one launch (start us, length us, event | category | flops | bytes accessed | tf_op | source)
XLA Modules:
  0.0 711.2 jit_solution(4043120329131948086)
XLA Ops:
  10.4 0.8 maximum_convert_fusion.refs_7_
  11.2 0.9 copy-done
  12.1 1.0 copy-done.5
  13.2 0.9 copy-done.11
  14.1 0.9 copy-done.12
  15.1 0.9 copy-done.13
  16.0 179.7 %forward_layer.1 = (bf16[4,2,128,3072]{3,2,1,0:T(8,128)(2,1)}, bf16[4,2,128,1024]{3,2,1,0:T(8,128)(2,1)}, bf16[4,2,128,1024]{3,2,1,0:T(8,128)(2,1)}, bf16[4,2,12...) custom-call(bf16[128,3072]{1,0:T(8,128)(2,1)} %refs_0_.1, ...), custom_call_target="tpu_custom_call" | custom-call | tf_op jit(solution)/shard_map/forward_layer/pallas_call | solution.py:392
  195.7 0.9 copy-done.1
  196.6 0.8 copy-done.2
  197.4 0.8 copy-done.3
  198.2 0.8 copy-done.4
  205.7 187.0 %vocabulary_head.1 = (f32[8,128]{1,0:T(8,128)}, bf16[1584,1024]{1,0:T(8,128)(2,1)}, f32[1024,128]{1,0:T(8,128)}) custom-call(bf16[128,1024]{1,0:T(8,128)(2,1)} %copy-done.14, f32[8,128]{1,0:T(8,128)} %copy-done.26, bf16[6288,1024]{1,0:T(8,128)(2,1)} %refs_2_.3), custom_call_target="tpu_custom_call" | custom-call | tf_op jit(solution)/shard_map/vocabulary_head/pallas_call | solution.py:1478
  392.7 278.9 %backward_layer.1 = (bf16[128,3072]{1,0:T(8,128)(2,1)}, bf16[128,1024]{1,0:T(8,128)(2,1)}, bf16[128,1024]{1,0:T(8,128)(2,1)}, bf16[128,2048]{1,0:T(8,128)(2,1)},...) custom-call(bf16[1024,3072]{1,0:T(8,128)(2,1)} %bitcast.26, ...), custom_call_target="tpu_custom_call" | custom-call | tf_op jit(solution)/shard_map/backward_layer/pallas_call | solution.py:990
  671.6 2.9 convert_element_type.50
  674.5 2.9 convert_element_type.51
  677.3 1.3 convert_element_type.45
  678.6 1.1 convert_element_type.48
  679.7 0.8 convert_element_type.46
  680.5 0.8 convert_element_type.47
  681.4 0.8 convert_element_type.49
  682.2 1.2 slice.62
  686.1 15.5 %slice_convert_fusion = f32[6288,1024]{1,0:T(8,128)} fusion(bf16[6336,1024]{1,0:T(8,128)(2,1)} %all-gather.3.cloned.1.call-done), kind=kLoop, calls=%fused_computation | loop fusion | flops 6438912 | bytes 38633472 | tf_op jit(solution)/shard_map/convert_element_type | solution.py:2019
  701.5 0.8 copy.35
  702.3 2.0 copy.36
  (65 shorter events, 12.0 us)
Async XLA Ops:
  7.2 678.9 %all-gather.3.cloned.1.call-start = ((), (), s32[]{:S(2)}) async-start(), calls=%async_computation | async-start | bytes 16220160 | tf_op jit(solution)/shard_map/all_gather | solution.py:2017
  10.4 195.2 %copy-start.26 = (f32[8,128]{1,0:T(8,128)}, f32[8,128]{1,0:T(8,128)S(1)}, u32[]{:S(2)}) copy-start(f32[8,128]{1,0:T(8,128)S(1)} %scatter.14.refs_1_) | copy-start | bytes 12292
  11.2 0.9 copy-start
  12.1 1.0 copy-start.5
  13.2 0.9 copy-start.11
  14.1 0.9 copy-start.12
  15.1 0.9 copy-start.13
  195.7 0.9 copy-start.1
  196.6 0.8 copy-start.2
  197.4 0.8 copy-start.3
  198.2 0.8 copy-start.4
  199.0 0.7 copy-start.6
  199.7 0.7 copy-start.7
  200.4 0.7 copy-start.8
  201.1 0.7 copy-start.9
  201.8 0.7 copy-start.10
  202.5 0.7 copy-start.14
  671.6 5.7 copy-start.20
  671.6 7.0 copy-start.21
  674.4 5.2 copy-start.25
  674.4 6.1 copy-start.24
  674.5 6.9 copy-start.23
  686.1 15.5 %copy-start.22 = (f32[128,1024]{1,0:T(8,128)S(1)}, f32[128,1024]{1,0:T(8,128)}, u32[]{:S(2)}) copy-start(f32[128,1024]{1,0:T(8,128)} %get-tuple-element.113) | copy-start | bytes 1572868
  686.1 16.3 %copy-start.19 = (f32[1024,1024]{1,0:T(8,128)S(1)}, f32[1024,1024]{1,0:T(8,128)}, u32[]{:S(2)}) copy-start(f32[1024,1024]{1,0:T(8,128)} %get-tuple-element.114) | copy-start | bytes 12582916
  (4 other events, 2.5 us)
Sparse Core Ops, SparseCore 0:
  392.8 202.6 all-gather.2

commit v5 on v4

--- a/solution.py
+++ b/solution.py
@@ -119,22 +119,23 @@
 
 
 def forward_kernel(length, mem_length, *refs):
-    shards, norm, states, encoded = refs[:7], refs[7], refs[8], refs[9]
-    fulls = refs[10:17]
+    shards, norm, aux, states_hbm, encoded_hbm = refs[:7], refs[7], refs[8], refs[9], refs[10]
+    fulls, marks, kept_hbm = refs[11:18], refs[18], refs[19:36]
     (
         norm_full, packed, context, first_normed, first_inverse, first_low, cross_queries, pairs,
         cross_context, second_normed, second_inverse, second_low, inner, active, third_normed,
         third_inverse, third_low,
-    ) = refs[17:34]
-    wbuf, residual = refs[34:36]
+    ) = refs[36:53]
+    wbuf, residual, states, encoded = refs[53:57]
     (
         local_sem, z_send, z_recv, one_send, one_recv, two_send, two_recv, d_send, d_recv,
-        norm_sem, nz_send, nz_recv, nd_send, nd_recv, load_sem,
-    ) = refs[36:]
+        norm_sem, nz_send, nz_recv, nd_send, nd_recv, load_sem, ax_sem, ax_send, ax_recv,
+        axz_send, axz_recv, kept_sem, input_sem,
+    ) = refs[57:]
     x, y, z, c = whereami()
     greet(neighbours(x, y, z, c))
     every = slice(None)
-    tokens, width = states.shape
+    tokens, width = states_hbm.shape
     slots_here = tokens // length
 
     def copies(u):
@@ -202,6 +203,42 @@
     for copy in norm_along:
         copy.start()
 
+    lanes = pl.ds(pl.multiple_of(c * tokens, tokens), tokens)
+    aux_local = pltpu.make_async_copy(aux, marks.at[y, x, z, :, lanes], ax_sem)
+    aux_local.start()
+    aux_steps = [
+        norm_copy(part, part, ax_send.at[n], ax_recv.at[n], peer)
+        for n, (part, peer) in enumerate(
+            (
+                (marks.at[y, x, z, :, lanes], at(x, y, z, 1 - c)),
+                (marks.at[y, x, z], at(1 - x, y, z, c)),
+                (marks.at[y, :, z], at(x, 1 - y, z, c)),
+            )
+        )
+    ]
+    aux_along = [
+        norm_copy(
+            marks.at[:, :, z], marks.at[:, :, z], axz_send.at[d - 1], axz_recv.at[d - 1],
+            at(x, y, lax.rem(z + d, 4), c),
+        )
+        for d in (1, 2, 3)
+    ]
+
+    kept = (
+        norm_full, packed, context, first_normed, first_inverse, first_low, cross_queries, pairs,
+        cross_context, second_normed, second_inverse, second_low, inner, active, third_normed,
+        third_inverse, third_low,
+    )
+
+    def keep(*numbers):
+        for n in numbers:
+            pltpu.make_async_copy(kept[n], kept_hbm[n], kept_sem.at[n]).start()
+
+    states_copy = pltpu.make_async_copy(states_hbm, states, input_sem.at[0])
+    encoded_copy = pltpu.make_async_copy(encoded_hbm, encoded, input_sem.at[1])
+    states_copy.start()
+    encoded_copy.start()
+
     def norm_row(n):
         return jnp.concatenate(
             [norm_full[p // 2, p % 2, n : n + 1, :] for p in range(8)], 1
@@ -248,12 +285,14 @@
             times(states, u, write)
             if k == 2:
                 attention(packed, packed, width, 2 * width, length, context, True)
+                keep(1, 2)
         elif weight == 1:
             def write(columns, n, value):
                 residual[:, columns] = states[:, columns].astype(jnp.float32) + value
 
             times(context, u, write)
             residual[...] = finish_norm(0, residual[...], first_normed, first_inverse, first_low)
+            keep(3, 4, 5)
         elif weight == 2:
             def write(columns, n, value):
                 cross_queries[:, columns] = value.astype(BFLOAT)
@@ -273,12 +312,14 @@
 
             if k == 1:
                 attention(cross_queries, pairs, 0, width, mem_length, cross_context, False)
+                keep(6, 7, 8)
         elif weight == 4:
             def write(columns, n, value):
                 residual[:, columns] = residual[:, columns] + value
 
             times(cross_context, u, write)
             residual[...] = finish_norm(1, residual[...], second_normed, second_inverse, second_low)
+            keep(9, 10, 11)
         elif weight == 5:
             def write(columns, n, value):
                 inner[:, block_columns(k, n)] = value
@@ -286,6 +327,8 @@
                 active[:, block_columns(k, n)] = (value * gate).astype(BFLOAT)
 
             times(second_low, u, write)
+            if k == 3:
+                keep(12, 13)
         else:
             slot = u % SLOTS_IN_FLIGHT
             blocks = active.shape[1] // (8 * ROWS)
@@ -301,6 +344,7 @@
 
             if k == blocks - 1:
                 finish_norm(2, residual[...], third_normed, third_inverse, third_low)
+                keep(14, 15, 16)
 
     count = len(UNITS)
     every_copy = [copies(u) for u in range(count)]
@@ -338,6 +382,19 @@
             norm_sibling.start()
         if i == 4:
             norm_sibling.wait()
+            keep(0)
+            states_copy.wait()
+            encoded_copy.wait()
+        if 5 <= i < 9:
+            if i == 5:
+                aux_local.wait()
+            else:
+                aux_steps[i - 6].wait()
+            for copy in aux_steps[i - 5 : i - 4] if i < 8 else aux_along:
+                copy.start()
+        if i == 9:
+            for copy in aux_along:
+                copy.wait()
         if 0 <= i - LAG_LOAD < count:
             sibling, load = every_copy[i - LAG_LOAD][4:]
             sibling.wait_recv()
@@ -352,9 +409,11 @@
             first.wait_send()
             second.wait_send()
         sibling.wait_send()
-
-
-def forward_layer(weights, norm, states, encoded, length):
+    for n in range(len(kept)):
+        pltpu.make_async_copy(kept[n], kept_hbm[n], kept_sem.at[n]).wait()
+
+
+def forward_layer(weights, norm, aux, states, encoded, length):
     count = len(UNITS)
     shapes = []
     for w, weight in enumerate(weights):
@@ -387,17 +446,20 @@
         ((tokens, width), BFLOAT),
     ]
     every = pl.BlockSpec(memory_space=pl.ANY)
-    vmem = pl.BlockSpec(memory_space=pltpu.VMEM)
     dma = pltpu.SemaphoreType.DMA
     results = pl.pallas_call(
         functools.partial(forward_kernel, length, mem_length),
         out_shape=tuple(jax.ShapeDtypeStruct(shape, BFLOAT) for shape in shapes)
+        + (jax.ShapeDtypeStruct((2, 2, 4, aux.shape[0], 2 * tokens), f32),)
         + tuple(jax.ShapeDtypeStruct(shape, kind) for shape, kind in kept),
-        in_specs=[every] * 8 + [vmem] * 2,
-        out_specs=(every,) * 7 + (vmem,) * len(kept),
-        scratch_shapes=[
+        in_specs=[every] * 11,
+        out_specs=(every,) * (8 + len(kept)),
+        scratch_shapes=[pltpu.VMEM(shape, kind) for shape, kind in kept]
+        + [
             pltpu.VMEM((SLOTS_IN_FLIGHT, 4, 2, ROWS, TILE), BFLOAT),
             pltpu.VMEM((tokens, width), f32),
+            pltpu.VMEM((tokens, width), BFLOAT),
+            pltpu.VMEM((mem_tokens, width), BFLOAT),
             dma((count,)),
             dma((count, 3)),
             dma((count, 3)),
@@ -406,14 +468,17 @@
         + [dma]
         + [dma((3,))] * 2
         + [dma] * 2
-        + [dma((SLOTS_IN_FLIGHT,))],
+        + [dma((SLOTS_IN_FLIGHT,))]
+        + [dma]
+        + [dma((3,))] * 4
+        + [dma((len(kept),)), dma((2,))],
         compiler_params=pltpu.CompilerParams(
-            collective_id=0, has_side_effects=True, vmem_limit_bytes=48 * 2**20
+            collective_id=0, has_side_effects=True, vmem_limit_bytes=62 * 2**20
         ),
         name="forward_layer",
-    )(*weights, norm, states, encoded)
+    )(*weights, norm, aux, states, encoded)
     fulls = tuple(full.reshape(-1, full.shape[-1]) for full in results[:7])
-    return fulls, results[7], results[8:]
+    return fulls, results[7], results[8], results[9:]
 
 
 SEQUENCE = tuple((6, k) for k in range(4)) + tuple((5, k) for k in range(4)) + (
@@ -1037,20 +1102,23 @@
 
 
 VOCAB_CUTS = 3
+ARRIVAL_PHASES = (0, 0, 1, 0, 1, 2, 3, 0, 1, 2, 3, 1, 2, 3, 2, 3)
+ARRIVAL_TURNS = (0, 1, 0, 2, 1, 0, 0, 3, 2, 1, 1, 3, 2, 2, 3, 3)
+NEAREST = ((0, 1, 2, 3), (1, 0, 1, 2), (2, 2, 3, 1), (3, 3, 0, 0))
 
 
 def head_kernel(slots, length, vocab_here, *refs):
-    hid, aux, emb_all = refs[:3]
+    hid, marks, emb_all = refs[:3]
     small_out, gemb_out, third_out = refs[3:6]
     (
-        emb, emb_t, held, marks, logit, expo, part, sib_part, part_one, part_two, part_z,
+        emb, emb_t, held, logit, expo, part, sib_part, part_one, part_two, part_z,
         mine, theirs, lined, prior, usable, weight, scaled, picked_grad,
-    ) = refs[6:25]
+    ) = refs[6:24]
     (
         local_sem, z_send, z_recv, one_send, one_recv, two_send, two_recv, sib_send, sib_recv,
-        ax_send, ax_recv, axz_send, axz_recv, st_send, st_recv, stz_send, stz_recv,
+        st_send, st_recv, stz_send, stz_recv,
         dd_send, dd_recv, r1_send, r1_recv, r2_send, r2_recv, rz_send, rz_recv,
-    ) = refs[25:]
+    ) = refs[24:]
     x, y, z, c = whereami()
     pb, pa = y * 2 + x, z * 2 + c
     size = hid.shape[0]
@@ -1078,9 +1146,6 @@
     greet(neighbours(x, y, z, c))
     own_copy = pltpu.make_async_copy(hid, spot(own, c), local_sem.at[0])
     own_copy.start()
-    lanes = pl.ds(pl.multiple_of(c * size, size), size)
-    aux_copy = pltpu.make_async_copy(aux, marks.at[y, x, z, :, lanes], local_sem.at[1])
-    aux_copy.start()
     emb_copy = pltpu.make_async_copy(
         emb_all.at[pl.ds(start, last), :], emb.at[pl.ds(0, last), :], local_sem.at[2]
     )
@@ -1093,9 +1158,22 @@
     rest_copy.start()
     own_copy.wait()
 
-    def along_copy(d):
-        other = lax.rem(z + d, 4)
-        return remote(hid, spot(own, c), z_send.at[d - 1], z_recv.at[d - 1], at(x, y, other, c))
+    def up_copy(origin):
+        block = spot(pb * 4 + origin, c)
+        return remote(block, block, z_send.at[0, origin], z_recv.at[origin], at(x, y, z + 1, c))
+
+    def down_copy(origin):
+        block = spot(pb * 4 + origin, c)
+        return remote(block, block, z_send.at[1, origin], z_recv.at[origin], at(x, y, z - 1, c))
+
+    def pass_along(origin, action):
+        @pl.when((origin <= z) & (z < 3))
+        def _():
+            action(up_copy(origin))
+
+        @pl.when((origin >= z) & (z > 0))
+        def _():
+            action(down_copy(origin))
 
     def sib_copy(k):
         return remote(spot(k, c), spot(k, c), sib_send.at[k], sib_recv.at[k], sibling)
@@ -1123,43 +1201,13 @@
         k = block(f if j == 0 else 1 - f, g)
         return remote(spot(k, c), spot(k, c), two_send.at[zz, j], two_recv.at[zz, j], second_peer)
 
-    for d in (1, 2, 3):
-        along_copy(d).start()
+    pass_along(z, lambda copy: copy.start())
     sib_copy(own).start()
     one_copy(z).start()
-
-    aux_copy.wait()
-    steps = (
-        (marks.at[y, x, z, :, lanes], sibling),
-        (marks.at[y, x, z], x_peer),
-        (marks.at[y, :, z], y_peer),
-    )
-    for n, (block_ref, peer) in enumerate(steps):
-        copy = remote(block_ref, block_ref, ax_send.at[n], ax_recv.at[n], peer)
-        copy.start()
-        copy.wait()
-
-    def mark_copy(d):
-        block_ref = marks.at[:, :, z]
-        other = lax.rem(z + d, 4)
-        return remote(block_ref, block_ref, axz_send.at[d - 1], axz_recv.at[d - 1], at(x, y, other, c))
-
-    for d in (1, 2, 3):
-        mark_copy(d).start()
-    for d in (1, 2, 3):
-        mark_copy(d).wait()
 
     emb_copy.wait()
     rest_copy.wait()
     full_cuts = rows // 128
-
-    @pl.loop(0, full_cuts)
-    def _(n):
-        here = pl.ds(pl.multiple_of(n * 128, 128), 128)
-        emb_t[:, here] = emb[here, :].T
-
-    if rows % 128:
-        emb_t[:, full_cuts * 128 :] = emb[full_cuts * 128 :, :].T
 
     def target_rows(k):
         ypart, xpart, zpart = k // 8, lax.rem(k // 4, 2), lax.rem(k, 4)
@@ -1209,30 +1257,42 @@
         mine[0, 1, pl.ds(k, 1), :] = total
         mine[0, 2, pl.ds(k, 1), :] = picked
 
-    @pl.loop(0, 16)
+    def listed(values, index):
+        out = values[0]
+        for n in range(1, len(values)):
+            out = jnp.where(index == n, values[n], out)
+        return out
+
+    def step_block(s):
+        phase = listed(ARRIVAL_PHASES, s)
+        t = listed(ARRIVAL_TURNS, s)
+        zz = listed([listed(row, z) for row in NEAREST], t)
+        f, g, _, _, block = order(zz)
+        k = listed((block(f, g), block(1 - f, g), block(f, 1 - g), block(1 - f, 1 - g)), phase)
+        return phase, zz, k
+
+    @pl.loop(0, 17)
     def _(s):
-        phase, t = s // 4, lax.rem(s, 4)
-        zz = lax.rem(z - t + 4, 4)
-        f, g, _, _, block = order(zz)
-        k = jnp.where(
-            phase == 0,
-            block(f, g),
-            jnp.where(
-                phase == 1, block(1 - f, g), jnp.where(phase == 2, block(f, 1 - g), block(1 - f, 1 - g))
-            ),
-        )
-
-        for d in (1, 2, 3):
-            @pl.when(s == d)
+        phase, zz, k = step_block(s)
+
+        @pl.when(s < full_cuts)
+        def _():
+            here = pl.ds(pl.multiple_of(s * 128, 128), 128)
+            emb_t[:, here] = emb[here, :].T
+
+        if rows % 128:
+            @pl.when(s == full_cuts)
             def _():
-                along_copy(d).wait_recv()
-
-        @pl.when((s > 0) & (phase == 0))
+                emb_t[:, full_cuts * 128 :] = emb[full_cuts * 128 :, :].T
+
+        @pl.when((s > 0) & (s < 16) & (phase == 0))
         def _():
+            up_copy(zz).wait_recv()
+            pass_along(zz, lambda copy: copy.start())
             sib_copy(k).start()
             one_copy(zz).start()
 
-        @pl.when(phase == 1)
+        @pl.when((s < 16) & (phase == 1))
         def _():
             one_copy(zz).wait_recv()
             sib_copy(k).start()
@@ -1240,13 +1300,16 @@
                 two_copy(zz, j).start()
 
         for j in range(2):
-            @pl.when(phase == 2 + j)
+            @pl.when((s < 16) & (phase == 2 + j))
             def _():
                 two_copy(zz, j).wait_recv()
                 sib_copy(k).start()
 
-        sib_copy(k).wait_recv()
-        forward_block(k)
+        @pl.when(s > 0)
+        def _():
+            former = step_block(s - 1)[2]
+            sib_copy(former).wait_recv()
+            forward_block(former)
 
     def joined(parts):
         highest = functools.reduce(jnp.maximum, [p[0] for p in parts])
@@ -1362,7 +1425,7 @@
     def rz_arrival(zz):
         return remote(part_two.at[zz], part_z.at[zz], rz_send.at[zz], rz_recv.at[zz], at(x, y, zz, c))
 
-    step = 64
+    step = 128
 
     def add_into(target_ref, other_ref):
         @pl.loop(0, width // step)
@@ -1385,36 +1448,37 @@
             preferred_element_type=jnp.float32,
         ).astype(BFLOAT)
 
+    def grad_block(s):
+        leaves = s < 8
+        zz = group(lax.rem(s, 8) // 2)
+        j = lax.rem(s, 2)
+        f, _, _, _, block = order(zz)
+        return leaves, zz, j, block(jnp.where(leaves, 1 - f, f), j)
+
     @pl.loop(0, 28)
     def _(s):
-        turn = s // 4
-        edge = lax.rem(s, 4) == 0
-
-        @pl.when(edge & (turn >= 1) & (turn < 5))
+        @pl.when((s >= 2) & (s < 18))
         def _():
-            zz = group(turn - 1)
-
-            @pl.loop(0, 4)
-            def _(n):
-                k = n * 4 + zz
-                dd_copy(k).wait_recv()
-                add_into(sib_part.at[k], part.at[k, c])
-
+            leaves, zz, turn, k = grad_block(s - 2)
+            dd_copy(k).wait_recv()
+            add_into(sib_part.at[k], part.at[k, c])
             for j in range(2):
-                r1_copy(zz, j).start()
-
-        @pl.when(edge & (turn >= 2) & (turn < 6))
+                @pl.when(leaves & (turn == j))
+                def _():
+                    r1_copy(zz, j).start()
+
+        @pl.when((lax.rem(s, 2) == 1) & (s >= 11) & (s < 18))
         def _():
-            zz = group(turn - 2)
+            zz = group((s - 11) // 2)
             f, _, _, _, block = order(zz)
             for j in range(2):
                 r1_copy(zz, j).wait_recv()
                 add_into(part_one.at[zz, j], sib_part.at[block(f, j)])
             r2_copy(zz).start()
 
-        @pl.when(edge & (turn >= 3))
+        @pl.when((lax.rem(s, 2) == 0) & (s >= 16) & (s < 24))
         def _():
-            zz = group(turn - 3)
+            zz = group((s - 16) // 2)
             _, g, _, _, _ = order(zz)
             r2_copy(zz).wait_recv()
             add_into(part_two.at[zz], part_one.at[zz, g])
@@ -1425,7 +1489,7 @@
 
         @pl.when(s < 16)
         def _():
-            k = lax.rem(s, 4) * 4 + group(turn)
+            k = grad_block(s)[3]
             backward_block(k)
             dd_copy(k).start()
 
@@ -1445,11 +1509,11 @@
         third_out[rows_here, :] = value
 
     for d in (1, 2, 3):
-        along_copy(d).wait_send()
         rz_copy(lax.rem(z + d, 4)).wait_send()
 
     @pl.loop(0, 4)
     def _(zz):
+        pass_along(zz, lambda copy: copy.wait_send())
         one_copy(zz).wait_send()
         for j in range(2):
             two_copy(zz, j).wait_send()
@@ -1462,14 +1526,10 @@
         dd_copy(k).wait_send()
 
 
-def vocabulary_head(third_low, targets, log_prior, usable, embedding, slots, length):
+def vocabulary_head(third_low, marks, embedding, slots, length):
     size, width = third_low.shape
     vocab_here = embedding.shape[0]
     rows = 16 * VOCAB_CUTS * -(-vocab_here // (4 * 16 * VOCAB_CUTS))
-    aux = jnp.zeros((8, size), jnp.float32)
-    aux = aux.at[0].set(targets.astype(jnp.float32))
-    aux = aux.at[1].set(jnp.repeat(log_prior, length))
-    aux = aux.at[2].set(jnp.repeat(usable.astype(jnp.float32), length))
     dma = pltpu.SemaphoreType.DMA
     vmem = pl.BlockSpec(memory_space=pltpu.VMEM)
     stat = (3, 16, 2 * size)
@@ -1488,7 +1548,6 @@
             pltpu.VMEM((rows, width), BFLOAT),
             pltpu.VMEM((width, rows), BFLOAT),
             pltpu.VMEM((32 * size, width), BFLOAT),
-            pltpu.VMEM((2, 2, 4, 8, 2 * size), f32),
             pltpu.VMEM((rows, 2 * size), f32),
             pltpu.VMEM((rows, 32 * size), BFLOAT),
             pltpu.VMEM((16, 2) + block, BFLOAT),
@@ -1502,11 +1561,11 @@
         ]
         + [pltpu.VMEM((16, 2 * size), f32)] * 5
         + [dma((4,))]
-        + [dma((3,))] * 2
+        + [dma((2, 4)), dma((4,))]
         + [dma((4,))] * 2
         + [dma((4, 2))] * 2
         + [dma((16,))] * 2
-        + [dma((3,))] * 8
+        + [dma((3,))] * 4
         + [dma((16,))] * 2
         + [dma((4, 2))] * 2
         + [dma((4,))] * 4,
@@ -1514,7 +1573,7 @@
             collective_id=2, has_side_effects=True, vmem_limit_bytes=60 * 2**20
         ),
         name="vocabulary_head",
-    )(third_low, aux, embedding)
+    )(third_low, marks, embedding)
     return small, gemb, third
 
 
@@ -2000,17 +2059,21 @@
     slots = slots_here * lax.axis_size("pa")
     states = decoder_states.reshape(slots_here * length, model_width)
     memory = encoder_memory.reshape(-1, model_width)
-    matrices, norms, kept = forward_layer(shards, norm_rows, states, memory, length)
     slot_index = lax.axis_index("pa") * slots_here + jnp.arange(slots_here)
     usable = (slot_mask[0] == 1) & (slot_index < slot_counts[0])
+    marks = jnp.concatenate(
+        [
+            target_tokens.reshape(1, slots_here * length).astype(jnp.float32),
+            jnp.repeat(log_prior, length, axis=1),
+            jnp.repeat(usable[None].astype(jnp.float32), length, axis=1),
+            jnp.zeros((5, slots_here * length), jnp.float32),
+        ]
+    )
+    matrices, marks, norms, kept = forward_layer(
+        shards, norm_rows, marks, states, memory, length
+    )
     small, grad_embed, grad_third = vocabulary_head(
-        kept[-1],
-        target_tokens.reshape(slots_here * length),
-        log_prior[0],
-        usable,
-        embedding,
-        slots,
-        length,
+        kept[-1], marks, embedding, slots, length
     )
     loss_value = small[0, 0]
     grad_prior = small[1].reshape(1, slots_here, length)[:, :, 0]

time: 712 us -> 645 us (0.906)
  Pallas kernels: 646 us -> 592 us
  local copies, waits for them, and re-layouts: 22.6 us -> 7.87 us
    pallas_call x1, Pallas kernels: 187 us -> 146 us  [vocabulary_head(): pl.pallas_call(functools.partial(head_kernel, slots, length, vocab_here),...]
    unnamed x56 -> x16, local copies, waits for them, and re-layouts: 17.6 us -> 2.83 us
    pallas_call x1, Pallas kernels: 180 us -> 172 us  [forward_layer(): pl.pallas_call(functools.partial(forward_kernel, length, mem_length), out...]
  transfers between devices with their start and end apart: 1 -> 1, of which waited for: 0 -> 0; matrix products, arithmetic and copies ran while one was open for 2% -> 2% of each run, Pallas kernels for 39% -> 43%
where the time goes in v5:
time: 645 us; the launch traced here: 644 us
  Pallas kernels  592 us (92%)
  other arithmetic  29.4 us (5%)
  between operations  14.8 us (2%)
  local copies, waits for them, and re-layouts  7.87 us (1%)
    pallas_call x1, Pallas kernels, backward_layer(): pl.pallas_call(functools.partial(backward_kernel, length, mem_length), ou...  274 us
    pallas_call x1, Pallas kernels, forward_layer(): pl.pallas_call(functools.partial(forward_kernel, length, mem_length), out...  172 us
    pallas_call x1, Pallas kernels, vocabulary_head(): pl.pallas_call(functools.partial(head_kernel, slots, length, vocab_here),...  146 us
    convert_element_type x1, other arithmetic, per_device_kernels(): grad_embed = pieces[:embedding.shape[0]].astype(jnp.float32)  15.5 us
  transfers between devices with their start and end apart: 1, of which 0 were waited for; matrix products, arithmetic and copies ran while one was open for 2% of the time, Pallas kernels for 43%

profile of v5, /device:TPU:0, one launch (start us, length us, event | category | flops | bytes accessed | tf_op | source)
XLA Modules:
  0.0 644.2 jit_solution(4395881319344706058)
XLA Ops:
  7.9 0.7 fusion
  8.6 0.1 broadcast_in_dim.21
  8.7 0.7 broadcast_in_dim.18
  9.5 0.7 convert_element_type.49
  10.4 1.4 maximum_convert_fusion.refs_7_
  11.8 0.7 maximum_maximum_fusion.refs_8_
  12.4 171.8 %forward_layer.1 = (bf16[4,2,128,3072]{3,2,1,0:T(8,128)(2,1)}, bf16[4,2,128,1024]{3,2,1,0:T(8,128)(2,1)}, bf16[4,2,128,1024]{3,2,1,0:T(8,128)(2,1)}, bf16[4,2,12...) custom-call(bf16[128,3072]{1,0:T(8,128)(2,1)} %refs_0_.1, ...), custom_call_target="tpu_custom_call" | custom-call | tf_op jit(solution)/shard_map/forward_layer/pallas_call | solution.py:450
  184.3 146.2 %vocabulary_head.1 = (f32[8,128]{1,0:T(8,128)}, bf16[1584,1024]{1,0:T(8,128)(2,1)}, f32[1024,128]{1,0:T(8,128)}) custom-call(bf16[128,1024]{1,0:T(8,128)(2,1)} %get-tuple-element.52.refs_0_, f32[2,2,4,8,256]{4,3,2,1,0:T(8,128)} %get-tuple-element.53.refs_1_, bf16[6288,1024]{1,0:T(8,128)(2,1)} %refs_2_.3), custom_call_target="tpu_custom_call" | custom-call | tf_op jit(solution)/shard_map/vocabulary_head/pallas_call | solution.py:1538
  330.5 274.1 %backward_layer.1 = (bf16[128,3072]{1,0:T(8,128)(2,1)}, bf16[128,1024]{1,0:T(8,128)(2,1)}, bf16[128,1024]{1,0:T(8,128)(2,1)}, bf16[128,2048]{1,0:T(8,128)(2,1)},...) custom-call(bf16[1024,3072]{1,0:T(8,128)(2,1)} %bitcast.22, ...), custom_call_target="tpu_custom_call" | custom-call | tf_op jit(solution)/shard_map/backward_layer/pallas_call | solution.py:1055
  604.6 2.9 convert_element_type.58
  607.5 2.9 convert_element_type.59
  610.4 1.3 convert_element_type.53
  611.7 1.1 convert_element_type.56
  612.7 0.8 convert_element_type.54
  613.6 0.8 convert_element_type.55
  614.4 0.8 convert_element_type.57
  615.3 1.2 slice.18
  616.4 0.7 slice_reduce_fusion.1
  617.2 0.6 slice_reduce_fusion
  617.9 0.7 constant_dynamic-slice_fusion
  618.5 0.6 fusion.1
  619.1 15.5 %slice_convert_fusion = f32[6288,1024]{1,0:T(8,128)} fusion(bf16[6336,1024]{1,0:T(8,128)(2,1)} %all-gather.3.cloned.1.call-done), kind=kLoop, calls=%fused_computation | loop fusion | flops 6438912 | bytes 38633472 | tf_op jit(solution)/shard_map/convert_element_type | solution.py:2082
  634.6 0.8 copy.33
  635.4 2.0 copy.34
  (25 shorter events, 0.6 us)
Async XLA Ops:
  7.2 611.9 %all-gather.3.cloned.1.call-start = ((), (), s32[]{:S(2)}) async-start(), calls=%async_computation | async-start | bytes 16220160 | tf_op jit(solution)/shard_map/all_gather | solution.py:2080
  604.6 5.7 copy-start.1
  604.6 7.0 %copy-start.2 = (bf16[128,2048]{1,0:T(8,128)(2,1)S(1)}, bf16[128,2048]{1,0:T(8,128)(2,1)}, u32[]{:S(2)}) copy-start(bf16[128,2048]{1,0:T(8,128)(2,1)} %get-tuple-element.84) | copy-start | bytes 1572868
  607.5 5.2 copy-start.6
  607.5 6.1 copy-start.5
  607.5 6.9 %copy-start.4 = (bf16[128,1024]{1,0:T(8,128)(2,1)S(1)}, bf16[128,1024]{1,0:T(8,128)(2,1)}, u32[]{:S(2)}) copy-start(bf16[128,1024]{1,0:T(8,128)(2,1)} %get-tuple-element.85) | copy-start | bytes 786436
  619.1 15.5 %copy-start.3 = (f32[128,1024]{1,0:T(8,128)S(1)}, f32[128,1024]{1,0:T(8,128)}, u32[]{:S(2)}) copy-start(f32[128,1024]{1,0:T(8,128)} %get-tuple-element.79) | copy-start | bytes 1572868
  619.1 16.3 %copy-start = (f32[1024,1024]{1,0:T(8,128)S(1)}, f32[1024,1024]{1,0:T(8,128)}, u32[]{:S(2)}) copy-start(f32[1024,1024]{1,0:T(8,128)} %get-tuple-element.80) | copy-start | bytes 12582916
Sparse Core Ops, SparseCore 0:
  330.7 198.0 all-gather.2

commit v6 on v5

--- a/solution.py
+++ b/solution.py
@@ -63,8 +63,8 @@
 Z_FULL = (9, 14)
 
 
-GATHER_WINDOW = 4
-LAG_TWO, LAG_SIBLING, LAG_LOAD, LAG_USE = 1, 2, 4, 5
+HOP_LAG = 1
+LAG_TWO, LAG_SIBLING, LAG_LOAD, LAG_USE = 3, 6, 8, 9
 SLOTS_IN_FLIGHT = 3
 
 
@@ -151,17 +151,16 @@
         local = pltpu.make_async_copy(
             shard_view(shard, unit, *rows), full_view(full, unit, z, c, *rows), local_sem.at[u]
         )
-        along = [
-            pltpu.make_async_remote_copy(
-                src_ref=shard_view(shard, unit, *rows),
-                dst_ref=full_view(full, unit, z, c, *rows),
-                send_sem=z_send.at[u, d - 1],
-                recv_sem=z_recv.at[u, d - 1],
-                device_id=at(x, y, lax.rem(z + d, 4), c),
+        def along(origin, direction):
+            block = full_view(full, unit, origin, c, *rows)
+            return pltpu.make_async_remote_copy(
+                src_ref=block,
+                dst_ref=block,
+                send_sem=z_send.at[u, (direction + 1) // 2, origin],
+                recv_sem=z_recv.at[u, origin],
+                device_id=at(x, y, z + direction, c),
                 device_id_type=MESH,
             )
-            for d in (1, 2, 3)
-        ]
 
         def cross(start, size, sends, recvs, peer):
             part = full_view(full, unit, every, c, start, size)
@@ -247,7 +246,7 @@
     def times(left_ref, u, write):
         slot = u % SLOTS_IN_FLIGHT
 
-        @pl.loop(0, 4)
+        @pl.loop(0, 4, unroll=True)
         def _(n):
             columns = pl.ds(pl.multiple_of(n * 256, 256), 256)
             right = wbuf[slot, :, :, :, columns].reshape(TILE, 256)
@@ -257,7 +256,7 @@
         return pl.ds(pl.multiple_of(k * TILE + n * 256, 256), 256)
 
     def attention(queries, keys, key_start, value_start, key_length, out, causal):
-        @pl.loop(0, slots_here * (width // 128))
+        @pl.loop(0, slots_here * (width // 128), unroll=2)
         def _(n):
             slot, group = n // (width // 128), lax.rem(n, width // 128)
             lanes = pl.ds(pl.multiple_of(group * 128, 128), 128)
@@ -301,11 +300,11 @@
         elif weight == 3:
             slot = u % SLOTS_IN_FLIGHT
 
-            @pl.loop(0, 16)
+            @pl.loop(0, 8)
             def _(n):
                 m, n = n // 4, lax.rem(n, 4)
                 columns = pl.ds(pl.multiple_of(n * 256, 256), 256)
-                part = encoded.shape[0] // 4
+                part = encoded.shape[0] // 2
                 rows_here = pl.ds(pl.multiple_of(m * part, part), part)
                 right = wbuf[slot, :, :, :, columns].reshape(TILE, 256)
                 pairs[rows_here, block_columns(k, n)] = dot_nn(encoded[rows_here, :], right).astype(BFLOAT)
@@ -336,7 +335,7 @@
                 [active[:, (p * blocks + k) * ROWS : (p * blocks + k + 1) * ROWS] for p in range(8)], 1
             )
 
-            @pl.loop(0, 4)
+            @pl.loop(0, 4, unroll=True)
             def _(n):
                 columns = pl.ds(pl.multiple_of(n * 256, 256), 256)
                 right = wbuf[slot, :, :, :, columns].reshape(TILE, 256)
@@ -348,21 +347,36 @@
 
     count = len(UNITS)
     every_copy = [copies(u) for u in range(count)]
-    for local, along, _, _, _, _ in every_copy[:GATHER_WINDOW]:
-        local.start()
-        for copy in along:
-            copy.start()
+
+    def hop(u, h):
+        local, along = every_copy[u][:2]
+        if h == 1:
+            local.wait()
+        for origin, there, edge, direction in (
+            (z - (h - 1), z >= h - 1, z < 3, 1),
+            (z + (h - 1), z + (h - 1) <= 3, z > 0, -1),
+        ):
+            @pl.when(there)
+            def _():
+                if h > 1:
+                    along(origin, direction).wait_recv()
+                if h < 4:
+                    @pl.when(edge)
+                    def _():
+                        along(origin, direction).start()
+
+    for copies_here in every_copy:
+        copies_here[0].start()
+    for h in range(1, 4):
+        for u in range(HOP_LAG * (4 - h)):
+            hop(u, h)
     for i in range(count + LAG_USE):
-        if i + GATHER_WINDOW < count:
-            local, along = every_copy[i + GATHER_WINDOW][:2]
-            local.start()
-            for copy in along:
-                copy.start()
+        for h in range(1, 5):
+            u = i + HOP_LAG * (4 - h)
+            if u < count:
+                hop(u, h)
         if i < count:
-            local, along, first = every_copy[i][:3]
-            local.wait()
-            for copy in along:
-                copy.wait_recv()
+            first = every_copy[i][2]
             if first is not None:
                 first.start()
         if 0 <= i - LAG_TWO < count:
@@ -403,8 +417,15 @@
             every_copy[i - LAG_USE][5].wait()
             use(i - LAG_USE)
     for _, along, first, second, sibling, _ in every_copy:
-        for copy in along:
-            copy.wait_send()
+        for origin in range(4):
+            @pl.when((origin <= z) & (z < 3))
+            def _():
+                along(origin, 1).wait_send()
+
+            @pl.when((origin >= z) & (z > 0))
+            def _():
+                along(origin, -1).wait_send()
+
         if first is not None:
             first.wait_send()
             second.wait_send()
@@ -461,8 +482,8 @@
             pltpu.VMEM((tokens, width), BFLOAT),
             pltpu.VMEM((mem_tokens, width), BFLOAT),
             dma((count,)),
-            dma((count, 3)),
-            dma((count, 3)),
+            dma((count, 2, 4)),
+            dma((count, 4)),
         ]
         + [dma((count,))] * 6
         + [dma]
@@ -484,8 +505,9 @@
 SEQUENCE = tuple((6, k) for k in range(4)) + tuple((5, k) for k in range(4)) + (
     (4, 0), (2, 0), (3, 0), (3, 1), (1, 0), (0, 0), (0, 1), (0, 2),
 )
-LINE_FIRST = 5
-LINE_LAGS = (12, 14, 16, 18, 20)
+LINE_FIRST = 9
+HOP_LAGS = (4, 7, 10)
+LINE_LAGS = (10, 12, 14, 16, 18)
 CROSS_LAGS = (2, 4, 6, 8, 10)
 TURNS = 27
 READS = tuple(read for k in range(4) for read in ((6, k), (5, k))) + (
@@ -611,12 +633,46 @@
             stage.at[lax.rem(q, 2), 1 - c], got.at[q], dd_send.at[q], dd_recv.at[q], at(x, y, z, 1 - c)
         )
 
-    def line_copy(q, d):
-        other = lax.rem(z + d, 4)
+    def line_copy(q, side, h, dest, step):
         return remote(
-            got.at[q, other], landing.at[q, d - 1], z_send.at[q, d - 1], z_recv.at[q, d - 1],
-            at(x, y, other, c),
-        )
+            got.at[q, dest], landing.at[q, side, h - 1], z_send.at[q, side, h - 1],
+            z_recv.at[q, side, h - 1], at(x, y, z + step, c),
+        )
+
+    def line_sides(h):
+        return (
+            (0, z + 4 - h, z <= h - 1, z >= 1, 1),
+            (1, z - 4 + h, z >= 4 - h, z <= 2, -1),
+        )
+
+    def line_load(q, side, h):
+        return pltpu.make_async_copy(landing.at[q, side, h - 2], zload.at[side], zload_sem.at[side])
+
+    def line_hop(q, h):
+        if h > 1:
+            for side, dest, there, fed, step in line_sides(h):
+                @pl.when(there & fed)
+                def _():
+                    line_copy(q, side, h - 1, dest, step).wait_recv()
+                    line_load(q, side, h).start()
+
+        for side, dest, there, fed, step in line_sides(h):
+            if h > 1:
+                @pl.when(there & fed)
+                def _():
+                    line_load(q, side, h).wait()
+
+                    @pl.loop(0, 8)
+                    def _(j):
+                        rows_here = piece(j, 16)
+                        got[q, dest, rows_here, :] = total(
+                            got[q, dest, rows_here, :], zload[side, rows_here, :]
+                        )
+
+            if h < 4:
+                @pl.when(there)
+                def _():
+                    line_copy(q, side, h, dest, step).start()
 
     def ra_line(q):
         a, _, a_peer, _ = place(q)
@@ -681,7 +737,7 @@
     def outer(q, left, start, step, right):
         slot = q % 2
 
-        @pl.loop(0, 8)
+        @pl.loop(0, 8, unroll=4)
         def _(p):
             lanes = pl.ds(pl.multiple_of(start + p * step, 128), 128)
             stage[slot, lax.rem(p, 2), p // 2] = dot_tn(left[:, lanes], right()).astype(BFLOAT)
@@ -690,7 +746,7 @@
         slot = n % 2
         read_copy(n).wait()
 
-        @pl.loop(0, 4)
+        @pl.loop(0, 4, unroll=True)
         def _(m):
             write(piece(m, 256), dot_nt(left[...], wbuf[slot, piece(m, 256), :]))
 
@@ -708,7 +764,7 @@
         norm_here[0, n + 3 : n + 4, :] = shift
 
     def attention_back(queries, keys, key_start, value_start, key_length, out, out_keys, causal):
-        @pl.loop(0, slots_here * (width // 128))
+        @pl.loop(0, slots_here * (width // 128), unroll=2)
         def _(n):
             slot, group = n // (width // 128), lax.rem(n, width // 128)
             lanes = piece(group, 128)
@@ -791,11 +847,13 @@
             if k == 2:
                 grad_states[...] = resid[...]
 
-    memory_rows = encoded.shape[0] // 8
+    half = encoded.shape[0] // 2
 
     def memory_copy(m):
         return pltpu.make_async_copy(
-            memory_part.at[m % 2], grad_memory.at[pl.ds(m * memory_rows, memory_rows), :], memory_sem.at[m % 2]
+            memory_part.at[m % 2],
+            grad_memory.at[pl.ds(m // 4 * half, half), pl.ds(m % 4 * 256, 256)],
+            memory_sem.at[m % 2],
         )
 
     def memory_chunk(m):
@@ -804,14 +862,10 @@
             read_copy(15).wait()
         if m >= 2:
             memory_copy(m - 2).wait()
-        rows_here = pl.ds(m * memory_rows, memory_rows)
-
-        @pl.loop(0, 4)
-        def _(n):
-            memory_part[m % 2, :, piece(n, 256)] = dot_nt(
-                pairs[rows_here, :width], wbuf[0, piece(n, 256), :]
-            ) + dot_nt(pairs[rows_here, width:], wbuf[1, piece(n, 256), :])
-
+        rows_here, columns = pl.ds(m // 4 * half, half), pl.ds(m % 4 * 256, 256)
+        memory_part[m % 2] = dot_nt(pairs[rows_here, :width], wbuf[0, columns, :]) + dot_nt(
+            pairs[rows_here, width:], wbuf[1, columns, :]
+        )
         memory_copy(m).start()
 
     def each(q, action):
@@ -858,32 +912,20 @@
 
             @pl.when(qs < LINE_FIRST)
             def _():
-                for d in (1, 2, 3):
-                    line_copy(qs, d).start()
+                line_hop(qs, 1)
 
             @pl.when(qs >= LINE_FIRST)
             def _():
                 ra_cross(qs).start()
 
-        q0 = i - LINE_LAGS[0]
-
-        @pl.when((q0 >= 0) & (q0 < LINE_FIRST))
-        def _():
-            for d in (1, 2, 3):
-                line_copy(q0, d).wait_recv()
-            load = pltpu.make_async_copy(landing.at[q0], zload, zload_sem)
-            load.start()
-            load.wait()
-
-            @pl.loop(0, 8)
-            def _(j):
-                rows_here = piece(j, step)
-                got[q0, z, rows_here, :] = total(
-                    got[q0, z, rows_here, :], zload[0, rows_here, :], zload[1, rows_here, :],
-                    zload[2, rows_here, :],
-                )
-
-            ra_line(q0).start()
+        for h in (2, 3, 4):
+            qh = i - HOP_LAGS[h - 2]
+
+            @pl.when((qh >= 0) & (qh < LINE_FIRST))
+            def _():
+                line_hop(qh, h)
+                if h == 4:
+                    ra_line(qh).start()
 
         q1 = i - LINE_LAGS[1]
 
@@ -1020,8 +1062,12 @@
 
     @pl.loop(0, LINE_FIRST)
     def _(q):
-        for d in (1, 2, 3):
-            line_copy(q, d).wait_send()
+        for h in (1, 2, 3):
+            for side, dest, there, _, step in line_sides(h):
+                @pl.when(there)
+                def _():
+                    line_copy(q, side, h, dest, step).wait_send()
+
         ra_line(q).wait_send()
         rb_line(q).wait_send()
 
@@ -1059,7 +1105,7 @@
             jax.ShapeDtypeStruct((8, width), f32),
             jax.ShapeDtypeStruct((tokens, width), f32),
             jax.ShapeDtypeStruct((mem_tokens, width), f32),
-            jax.ShapeDtypeStruct((LINE_FIRST, 3, ROWS, TILE), BFLOAT),
+            jax.ShapeDtypeStruct((LINE_FIRST, 2, 3, ROWS, TILE), BFLOAT),
         ),
         in_specs=[every] * 24 + [vmem] * 2,
         out_specs=(every,) * 7 + (vmem, vmem, every, every),
@@ -1069,7 +1115,7 @@
             pltpu.VMEM((2, tokens, TILE), f32),
             pltpu.VMEM((2, 2, 4, ROWS, TILE), BFLOAT),
             pltpu.VMEM((count, 4, ROWS, TILE), BFLOAT),
-            pltpu.VMEM((3, ROWS, TILE), BFLOAT),
+            pltpu.VMEM((2, ROWS, TILE), BFLOAT),
             pltpu.VMEM((LINE_FIRST, 64, TILE), BFLOAT),
             pltpu.VMEM((LINE_FIRST, 32, TILE), BFLOAT),
             pltpu.VMEM((crossed, 4, 64, TILE), BFLOAT),
@@ -1082,12 +1128,12 @@
             pltpu.VMEM((tokens, width), BFLOAT),
             pltpu.VMEM((tokens, width), BFLOAT),
             pltpu.VMEM((tokens, 3 * width), BFLOAT),
-            pltpu.VMEM((2, mem_tokens // 8, width), f32),
+            pltpu.VMEM((2, mem_tokens // 2, 256), f32),
             pltpu.VMEM((4, 8, width), f32),
             pltpu.VMEM((3, 8, width), f32),
             pltpu.VMEM((3, 8, width), f32),
             dma((16,)), dma((2,)), dma((2,)), sems, sems,
-            dma((LINE_FIRST, 3)), dma((LINE_FIRST, 3)), dma,
+            dma((LINE_FIRST, 2, 3)), dma((LINE_FIRST, 2, 3)), dma((2,)),
             sems, sems, sems, sems,
             dma((crossed, 3)), dma((crossed, 3)),
             sems, sems, sems, sems, sems, dma((2,)),

time: 645 us -> 612 us (0.949); the launches traced: 644 us -> 601 us
  Pallas kernels: 592 us -> 549 us
    pallas_call x1, Pallas kernels: 274 us -> 250 us  [backward_layer(): pl.pallas_call(functools.partial(backward_kernel, length, mem_length), ou...]
    pallas_call x1, Pallas kernels: 172 us -> 158 us  [forward_layer(): pl.pallas_call(functools.partial(forward_kernel, length, mem_length), out...]
  transfers between devices with their start and end apart: 1 -> 1, of which waited for: 0 -> 0; matrix products, arithmetic and copies ran while one was open for 2% -> 2% of each run, Pallas kernels for 43% -> 42%
where the time goes in v6:
time: 612 us; the launch traced here: 601 us
  Pallas kernels  549 us (90%)
  other arithmetic  29.4 us (5%)
  between operations  15.1 us (2%)
  local copies, waits for them, and re-layouts  7.9 us (1%)
    pallas_call x1, Pallas kernels, backward_layer(): pl.pallas_call(functools.partial(backward_kernel, length, mem_length), ou...  250 us
    pallas_call x1, Pallas kernels, forward_layer(): pl.pallas_call(functools.partial(forward_kernel, length, mem_length), out...  158 us
    pallas_call x1, Pallas kernels, vocabulary_head(): pl.pallas_call(functools.partial(head_kernel, slots, length, vocab_here),...  141 us
    convert_element_type x1, other arithmetic, per_device_kernels(): grad_embed = pieces[:embedding.shape[0]].astype(jnp.float32)  15.5 us
  transfers between devices with their start and end apart: 1, of which 0 were waited for; matrix products, arithmetic and copies ran while one was open for 2% of the time, Pallas kernels for 42%

profile of v6, /device:TPU:0, one launch (start us, length us, event | category | flops | bytes accessed | tf_op | source)
XLA Modules:
  0.0 601.2 jit_solution(13246529153747049452)
XLA Ops:
  7.9 0.7 fusion
  8.7 0.7 broadcast_in_dim.18
  9.5 0.7 convert_element_type.49
  10.4 1.4 maximum_convert_fusion.refs_7_
  11.8 0.7 maximum_maximum_fusion.refs_8_
  12.4 157.9 %forward_layer.1 = (bf16[4,2,128,3072]{3,2,1,0:T(8,128)(2,1)}, bf16[4,2,128,1024]{3,2,1,0:T(8,128)(2,1)}, bf16[4,2,128,1024]{3,2,1,0:T(8,128)(2,1)}, bf16[4,2,12...) custom-call(bf16[128,3072]{1,0:T(8,128)(2,1)} %refs_0_.1, ...), custom_call_target="tpu_custom_call" | custom-call | tf_op jit(solution)/shard_map/forward_layer/pallas_call | solution.py:471
  170.4 140.8 %vocabulary_head.1 = (f32[8,128]{1,0:T(8,128)}, bf16[1584,1024]{1,0:T(8,128)(2,1)}, f32[1024,128]{1,0:T(8,128)}) custom-call(bf16[128,1024]{1,0:T(8,128)(2,1)} %get-tuple-element.52.refs_0_, f32[2,2,4,8,256]{4,3,2,1,0:T(8,128)} %get-tuple-element.53.refs_1_, bf16[6288,1024]{1,0:T(8,128)(2,1)} %refs_2_.3), custom_call_target="tpu_custom_call" | custom-call | tf_op jit(solution)/shard_map/vocabulary_head/pallas_call | solution.py:1584
  311.2 250.0 %backward_layer.1 = (bf16[128,3072]{1,0:T(8,128)(2,1)}, bf16[128,1024]{1,0:T(8,128)(2,1)}, bf16[128,1024]{1,0:T(8,128)(2,1)}, bf16[128,2048]{1,0:T(8,128)(2,1)},...) custom-call(bf16[1024,3072]{1,0:T(8,128)(2,1)} %bitcast.22, ...), custom_call_target="tpu_custom_call" | custom-call | tf_op jit(solution)/shard_map/backward_layer/pallas_call | solution.py:1101
  561.2 2.9 convert_element_type.58
  564.1 2.9 convert_element_type.59
  567.0 1.3 convert_element_type.53
  568.3 1.1 convert_element_type.56
  569.3 0.8 convert_element_type.54
  570.2 0.8 convert_element_type.55
  571.0 0.8 convert_element_type.57
  571.9 1.2 slice.18
  573.0 0.7 slice_reduce_fusion.1
  573.7 0.1 reshape_squeeze.3
  573.8 0.6 slice_reduce_fusion
  574.5 0.7 constant_dynamic-slice_fusion
  575.1 0.6 fusion.1
  575.7 15.5 %slice_convert_fusion = f32[6288,1024]{1,0:T(8,128)} fusion(bf16[6336,1024]{1,0:T(8,128)(2,1)} %all-gather.3.cloned.1.call-done), kind=kLoop, calls=%fused_computation | loop fusion | flops 6438912 | bytes 38633472 | tf_op jit(solution)/shard_map/convert_element_type | solution.py:2128
  591.2 0.8 copy.33
  592.0 2.0 copy.34
  (25 shorter events, 0.6 us)
Async XLA Ops:
  7.2 568.5 %all-gather.3.cloned.1.call-start = ((), (), s32[]{:S(2)}) async-start(), calls=%async_computation | async-start | bytes 16220160 | tf_op jit(solution)/shard_map/all_gather | solution.py:2126
  561.2 5.7 copy-start.1
  561.2 7.0 %copy-start.2 = (bf16[128,2048]{1,0:T(8,128)(2,1)S(1)}, bf16[128,2048]{1,0:T(8,128)(2,1)}, u32[]{:S(2)}) copy-start(bf16[128,2048]{1,0:T(8,128)(2,1)} %get-tuple-element.84) | copy-start | bytes 1572868
  564.1 5.2 copy-start.6
  564.1 6.1 %copy-start.5 = (bf16[128,1024]{1,0:T(8,128)(2,1)S(1)}, bf16[128,1024]{1,0:T(8,128)(2,1)}, u32[]{:S(2)}) copy-start(bf16[128,1024]{1,0:T(8,128)(2,1)} %get-tuple-element.83) | copy-start | bytes 786436
  564.1 6.9 %copy-start.4 = (bf16[128,1024]{1,0:T(8,128)(2,1)S(1)}, bf16[128,1024]{1,0:T(8,128)(2,1)}, u32[]{:S(2)}) copy-start(bf16[128,1024]{1,0:T(8,128)(2,1)} %get-tuple-element.85) | copy-start | bytes 786436
  575.7 15.5 %copy-start.3 = (f32[128,1024]{1,0:T(8,128)S(1)}, f32[128,1024]{1,0:T(8,128)}, u32[]{:S(2)}) copy-start(f32[128,1024]{1,0:T(8,128)} %get-tuple-element.79) | copy-start | bytes 1572868
  575.7 16.3 %copy-start = (f32[1024,1024]{1,0:T(8,128)S(1)}, f32[1024,1024]{1,0:T(8,128)}, u32[]{:S(2)}) copy-start(f32[1024,1024]{1,0:T(8,128)} %get-tuple-element.80) | copy-start | bytes 12582916
Sparse Core Ops, SparseCore 0:
  311.4 186.2 all-gather.2

commit v7 on v6

--- a/solution.py
+++ b/solution.py
@@ -60,7 +60,7 @@
     return ref.at[place, core, pl.ds(start, size), pl.ds(block * TILE, TILE)]
 
 
-Z_FULL = (9, 14)
+Z_FULL = (13, 14, 15)
 
 
 HOP_LAG = 1
@@ -510,6 +510,7 @@
 LINE_LAGS = (10, 12, 14, 16, 18)
 CROSS_LAGS = (2, 4, 6, 8, 10)
 TURNS = 27
+GATHER_TURNS = (4, 8)
 READS = tuple(read for k in range(4) for read in ((6, k), (5, k))) + (
     (4, 0), (2, 0), (1, 0), (0, 0), (0, 1), (0, 2), (3, 0), (3, 1),
 )
@@ -544,20 +545,21 @@
     weights = refs[:7]
     kept_hbm = refs[7:23]
     inner_hbm = refs[23]
-    norm_full, grad_third = refs[24:26]
-    outs = refs[26:33]
-    norm_out, grad_states, grad_memory, landing = refs[33:37]
-    kept = refs[37:53]
+    norm_full, grad_third, gemb = refs[24:27]
+    outs = refs[27:34]
+    norm_out, grad_states, grad_memory, pieces, landing = refs[34:39]
+    kept = refs[39:55]
     (
         wbuf, inner, stage, got, zload, one_line, two_line, one, two, line, fin,
         resid, low, grad_low, grad_context, grad_queries, grad_packed, memory_part,
         norm_here, norm_there, norm_line,
-    ) = refs[53:74]
+    ) = refs[55:76]
     (
         kept_sem, w_sem, inner_sem, dd_send, dd_recv, z_send, z_recv, zload_sem,
         ra_send, ra_recv, rb_send, rb_recv, rz_send, rz_recv, ag_send, ag_recv, ah_send, ah_recv,
-        fin_sem, memory_sem, n_send, n_recv, nz_send, nz_recv,
-    ) = refs[74:]
+        fin_sem, memory_sem, n_send, n_recv, nz_send, nz_recv, gemb_sem, ga_send, ga_recv,
+        gb_send, gb_recv,
+    ) = refs[76:]
     (
         packed, context, first_normed, first_inverse, first_low, cross_queries, pairs, cross_context,
         second_normed, second_inverse, second_low, active, third_normed, third_inverse, states, encoded,
@@ -627,6 +629,29 @@
         for part in parts[1:]:
             out = out + part.astype(jnp.float32)
         return out.astype(BFLOAT)
+
+    pb = y * 2 + x
+    pb_x, pb_y = y * 2 + 1 - x, (1 - y) * 2 + x
+    vocab_rows = gemb.shape[0]
+    cut = 16 * (vocab_rows // 64)
+    cuts = [(n * cut, cut if n < 3 else vocab_rows - 3 * cut) for n in range(4)]
+
+    def gather_one(n):
+        rows_here = pl.ds(*cuts[n])
+        peer = at(1 - x, y, z, c) if n < 2 else at(x, 1 - y, z, c)
+        return remote(gemb.at[rows_here, :], pieces.at[pb, rows_here, :], ga_send.at[n], ga_recv.at[n], peer)
+
+    def gather_two(n, j):
+        rows_here = pl.ds(*cuts[n])
+        peer = at(x, 1 - y, z, c) if n < 2 else at(1 - x, y, z, c)
+        origin = pb if j == 0 else (pb_x if n < 2 else pb_y)
+        source = gemb.at[rows_here, :] if j == 0 else pieces.at[origin, rows_here, :]
+        return remote(source, pieces.at[origin, rows_here, :], gb_send.at[n, j], gb_recv.at[n, j], peer)
+
+    gemb_copy = pltpu.make_async_copy(gemb, pieces.at[pb], gemb_sem)
+    for n in (0, 2, 1, 3):
+        gather_one(n).start()
+    gemb_copy.start()
 
     def dd_copy(q):
         return remote(
@@ -893,6 +918,14 @@
                 produce(q)
                 dd_copy(q).start()
 
+        for n, turn in enumerate(GATHER_TURNS):
+            @pl.when(i == turn)
+            def _():
+                for part in (n, n + 2):
+                    gather_two(part, 0).start()
+                    gather_one(part).wait_recv()
+                    gather_two(part, 1).start()
+
         for m in range(8):
             @pl.when(i == count + 1 + m)
             def _():
@@ -1055,6 +1088,11 @@
                 norm_line_copy(d).wait_recv()
             norm_out[...] = ((norm_here[3] + norm_line[0]) + norm_line[1]) + norm_line[2]
 
+    gemb_copy.wait()
+    for n in range(4):
+        gather_one(n).wait_send()
+        for j in range(2):
+            gather_two(n, j).wait()
     memory_copy(6).wait()
     memory_copy(7).wait()
     dd_copy(count - 2).wait_send()
@@ -1086,7 +1124,7 @@
         norm_line_copy(n + 1).wait_send()
 
 
-def backward_layer(weights, kept, inner, norm_full, grad_third, length):
+def backward_layer(weights, kept, inner, norm_full, grad_third, gemb, length):
     count = len(SEQUENCE)
     f32 = jnp.float32
     tokens, width = kept[14].shape
@@ -1098,17 +1136,18 @@
     dma = pltpu.SemaphoreType.DMA
     sems = dma((count,))
     crossed = count - LINE_FIRST
-    *shares, norm_sum, grad_states, grad_memory, _ = pl.pallas_call(
+    *shares, norm_sum, grad_states, grad_memory, pieces, _ = pl.pallas_call(
         functools.partial(backward_kernel, length, mem_length),
         out_shape=tuple(jax.ShapeDtypeStruct(shape, BFLOAT) for shape in shapes)
         + (
             jax.ShapeDtypeStruct((8, width), f32),
             jax.ShapeDtypeStruct((tokens, width), f32),
             jax.ShapeDtypeStruct((mem_tokens, width), f32),
+            jax.ShapeDtypeStruct((4,) + gemb.shape, BFLOAT),
             jax.ShapeDtypeStruct((LINE_FIRST, 2, 3, ROWS, TILE), BFLOAT),
         ),
-        in_specs=[every] * 24 + [vmem] * 2,
-        out_specs=(every,) * 7 + (vmem, vmem, every, every),
+        in_specs=[every] * 24 + [vmem] * 2 + [every],
+        out_specs=(every,) * 7 + (vmem, vmem, every, every, every),
         scratch_shapes=[pltpu.VMEM(part.shape, part.dtype) for part in kept]
         + [
             pltpu.VMEM((2, TILE, TILE), BFLOAT),
@@ -1138,13 +1177,113 @@
             dma((crossed, 3)), dma((crossed, 3)),
             sems, sems, sems, sems, sems, dma((2,)),
             dma((3,)), dma((3,)), dma((3,)), dma((3,)),
+            dma, dma((4,)), dma((4,)), dma((4, 2)), dma((4, 2)),
         ],
         compiler_params=pltpu.CompilerParams(
             collective_id=1, has_side_effects=True, vmem_limit_bytes=62 * 2**20
         ),
         name="backward_layer",
-    )(*weights, *kept, inner, norm_full, grad_third)
-    return tuple(share.astype(f32) for share in shares), norm_sum, grad_states, grad_memory
+    )(*weights, *kept, inner, norm_full, grad_third, gemb)
+    return shares, norm_sum, grad_states, grad_memory, pieces
+
+
+WIDE_ROWS = 512
+WIDE_SLOTS = 4
+
+
+def widen_kernel(embed_rows, *refs):
+    parts, pieces, norms = refs[:7], refs[7], refs[8]
+    outs, embed_out, gains_out, shifts_out = refs[9:16], refs[16], refs[17], refs[18]
+    low, wide = refs[19:26], refs[26:33]
+    embed_low, embed_wide, norm_here = refs[33:36]
+    in_sem, out_sem, embed_in, embed_out_sem, norm_sem = refs[36:]
+    here = norm_here.shape[1]
+    norm_copy = pltpu.make_async_copy(
+        norms.at[:, pl.ds(pl.multiple_of(lax.axis_index("pa") * here, here), here)], norm_here, norm_sem
+    )
+    norm_copy.start()
+    full = embed_rows // WIDE_ROWS
+    rest = embed_rows - full * WIDE_ROWS
+
+    def load(n, rows):
+        return pltpu.make_async_copy(
+            pieces.at[pl.ds(n * WIDE_ROWS, rows), :],
+            embed_low.at[n % WIDE_SLOTS, pl.ds(0, rows), :],
+            embed_in.at[n % WIDE_SLOTS],
+        )
+
+    def store(n, rows):
+        return pltpu.make_async_copy(
+            embed_wide.at[n % WIDE_SLOTS, pl.ds(0, rows), :],
+            embed_out.at[pl.ds(n * WIDE_ROWS, rows), :],
+            embed_out_sem.at[n % WIDE_SLOTS],
+        )
+
+    sizes = [WIDE_ROWS] * full + [rest] * (rest > 0)
+    for n in range(WIDE_SLOTS):
+        load(n, sizes[n]).start()
+    for n in range(7):
+        pltpu.make_async_copy(parts[n], low[n], in_sem.at[n]).start()
+    for n, rows in enumerate(sizes):
+        load(n, rows).wait()
+        if n >= WIDE_SLOTS:
+            store(n - WIDE_SLOTS, sizes[n - WIDE_SLOTS]).wait()
+
+        @pl.loop(0, rows // 16, unroll=4)
+        def _(j):
+            part = pl.ds(pl.multiple_of(j * 16, 16), 16)
+            embed_wide[n % WIDE_SLOTS, part, :] = embed_low[n % WIDE_SLOTS, part, :].astype(jnp.float32)
+
+        store(n, rows).start()
+        if n + WIDE_SLOTS < len(sizes):
+            load(n + WIDE_SLOTS, sizes[n + WIDE_SLOTS]).start()
+    for n in range(7):
+        pltpu.make_async_copy(parts[n], low[n], in_sem.at[n]).wait()
+
+        @pl.loop(0, low[n].shape[0] // 16)
+        def _(j):
+            part = pl.ds(pl.multiple_of(j * 16, 16), 16)
+            wide[n][part, :] = low[n][part, :].astype(jnp.float32)
+
+        pltpu.make_async_copy(wide[n], outs[n], out_sem.at[n]).start()
+    norm_copy.wait()
+    gains_out[...] = norm_here[0:3, :]
+    shifts_out[...] = norm_here[3:6, :]
+    for n in range(len(sizes) - WIDE_SLOTS, len(sizes)):
+        store(n, sizes[n]).wait()
+    for n in range(7):
+        pltpu.make_async_copy(wide[n], outs[n], out_sem.at[n]).wait()
+
+
+def widen(parts, pieces, norms, embed_rows, norm_here):
+    every = pl.BlockSpec(memory_space=pl.ANY)
+    vmem = pl.BlockSpec(memory_space=pltpu.VMEM)
+    f32 = jnp.float32
+    width = pieces.shape[1]
+    dma = pltpu.SemaphoreType.DMA
+    results = pl.pallas_call(
+        functools.partial(widen_kernel, embed_rows),
+        out_shape=tuple(jax.ShapeDtypeStruct(part.shape, f32) for part in parts)
+        + (jax.ShapeDtypeStruct((embed_rows, width), f32),)
+        + (jax.ShapeDtypeStruct((3, norm_here), f32),) * 2,
+        in_specs=[every] * 9,
+        out_specs=(every,) * 8 + (vmem,) * 2,
+        scratch_shapes=[pltpu.VMEM(part.shape, BFLOAT) for part in parts]
+        + [pltpu.VMEM(part.shape, f32) for part in parts]
+        + [
+            pltpu.VMEM((WIDE_SLOTS, WIDE_ROWS, width), BFLOAT),
+            pltpu.VMEM((WIDE_SLOTS, WIDE_ROWS, width), f32),
+            pltpu.VMEM((8, norm_here), f32),
+            dma((7,)),
+            dma((7,)),
+            dma((WIDE_SLOTS,)),
+            dma((WIDE_SLOTS,)),
+            dma,
+        ],
+        compiler_params=pltpu.CompilerParams(vmem_limit_bytes=60 * 2**20),
+        name="widen",
+    )(*parts, pieces, norms)
+    return results[:7], results[7], results[8], results[9]
 
 
 VOCAB_CUTS = 3
@@ -1291,6 +1430,7 @@
             VOCAB_CUTS,
             scan_logits,
             (jnp.full((1, pair), NEGATIVE, jnp.float32), jnp.zeros((1, pair), jnp.float32)),
+            unroll=True,
         )
 
         def scan_exp(j, total):
@@ -1298,7 +1438,9 @@
             expo[cut_rows(j), token_lanes(k)] = value.astype(BFLOAT)
             return total + jnp.sum(value, 0, keepdims=True)
 
-        total = lax.fori_loop(0, VOCAB_CUTS, scan_exp, jnp.zeros((1, pair), jnp.float32))
+        total = lax.fori_loop(
+            0, VOCAB_CUTS, scan_exp, jnp.zeros((1, pair), jnp.float32), unroll=True
+        )
         mine[0, 0, pl.ds(k, 1), :] = highest
         mine[0, 1, pl.ds(k, 1), :] = total
         mine[0, 2, pl.ds(k, 1), :] = picked
@@ -1435,7 +1577,7 @@
             expo[cut_rows(j), token_lanes(k)] = grad.astype(BFLOAT)
             return carried
 
-        lax.fori_loop(0, VOCAB_CUTS, make, 0)
+        lax.fori_loop(0, VOCAB_CUTS, make, 0, unroll=True)
 
         def to_rows(n, carried):
             cut_width = pl.ds(pl.multiple_of(n * 256, 256), 256)
@@ -1449,7 +1591,7 @@
             part[k, 1, cut_width, :] = value[:, size:]
             return carried
 
-        lax.fori_loop(0, width // 256, to_rows, 0)
+        lax.fori_loop(0, width // 256, to_rows, 0, unroll=True)
 
     def dd_copy(k):
         return remote(part.at[k, 1 - c], sib_part.at[k], dd_send.at[k], dd_recv.at[k], sibling)
@@ -2123,27 +2265,25 @@
     )
     loss_value = small[0, 0]
     grad_prior = small[1].reshape(1, slots_here, length)[:, :, 0]
-    pieces = lax.all_gather(grad_embed, "pb", axis=0)
-    pieces = pieces.reshape(4 * grad_embed.shape[0], model_width)
-    grad_embed = pieces[: embedding.shape[0]].astype(jnp.float32)
-    shares, norm_sums, grad_inputs, grad_encoded = backward_layer(
+    shares, norm_sums, grad_inputs, grad_encoded, pieces = backward_layer(
         matrices,
         kept[:11] + kept[12:15] + (states, memory),
         kept[11],
         norms,
         grad_third,
+        grad_embed,
         length,
     )
-    norm_here = norm_gains.shape[1]
-    norm_sums = lax.dynamic_slice_in_dim(
-        norm_sums, lax.axis_index("pa") * norm_here, norm_here, axis=1
+    pieces = pieces.reshape(4 * grad_embed.shape[0], model_width)
+    shares, grad_embed, grad_gains, grad_shifts = widen(
+        shares, pieces, norm_sums, embedding.shape[0], norm_gains.shape[1]
     )
     return (
         loss_value,
         grad_inputs.reshape(decoder_states.shape),
         grad_encoded.reshape(encoder_memory.shape),
         grad_prior,
-    ) + shares + (grad_embed, norm_sums[:3], norm_sums[3:6])
+    ) + tuple(shares) + (grad_embed, grad_gains, grad_shifts)
 
 
 def solution(mesh):

time: 612 us -> 576 us (0.941); the launches traced: 601 us -> 572 us
  other arithmetic: 29.4 us -> 3.37 us
  between operations: 15.1 us -> 1.53 us
  Pallas kernels: 549 us -> 557 us
    convert_element_type x8 -> x0, other arithmetic: 26.1 us -> none  [the longest x1 15.5 us: per_device_kernels(): grad_embed = pieces[:embedding.shape[0]].astype(jnp.float32)]
    pallas_call x0 -> x1, Pallas kernels: none -> 17.7 us  [widen(): pl.pallas_call(functools.partial(widen_kernel, embed_rows), out_shape=tup...]
  transfers between devices with their start and end apart: 1 -> 0, of which waited for: 0 -> 0; matrix products, arithmetic and copies ran while one was open for 2% -> 0% of each run, Pallas kernels for 42% -> 0%
where the time goes in v7:
time: 576 us; the launch traced here: 572 us
  Pallas kernels  557 us (97%)
  local copies, waits for them, and re-layouts  9.39 us (2%)
    pallas_call x1, Pallas kernels, backward_layer(): pl.pallas_call(functools.partial(backward_kernel, length, mem_length), ou...  244 us
    pallas_call x1, Pallas kernels, forward_layer(): pl.pallas_call(functools.partial(forward_kernel, length, mem_length), out...  158 us
    pallas_call x1, Pallas kernels, vocabulary_head(): pl.pallas_call(functools.partial(head_kernel, slots, length, vocab_here),...  138 us
    pallas_call x1, Pallas kernels, widen(): pl.pallas_call(functools.partial(widen_kernel, embed_rows), out_shape=tup...  17.7 us

profile of v7, /device:TPU:0, one launch (start us, length us, event | category | flops | bytes accessed | tf_op | source)
XLA Modules:
  0.0 571.7 jit_solution(13932216535423840961)
XLA Ops:
  1.3 0.7 fusion
  2.0 0.1 broadcast_in_dim.20
  2.0 0.1 broadcast_in_dim.21
  2.1 0.7 broadcast_in_dim.18
  2.8 0.1 broadcast_in_dim.19
  2.9 0.7 convert_element_type.25
  3.6 0.1 convert_element_type.26
  3.7 0.1 pad.3.clone
  3.8 0.7 maximum_maximum_fusion.refs_8_
  4.4 0.1 pad.6.clone
  4.5 1.4 maximum_convert_fusion.refs_7_
  5.9 157.7 %forward_layer.1 = (bf16[4,2,128,3072]{3,2,1,0:T(8,128)(2,1)}, bf16[4,2,128,1024]{3,2,1,0:T(8,128)(2,1)}, bf16[4,2,128,1024]{3,2,1,0:T(8,128)(2,1)}, bf16[4,2,12...) custom-call(bf16[128,3072]{1,0:T(8,128)(2,1)} %refs_0_.1, ...), custom_call_target="tpu_custom_call" | custom-call | tf_op jit(solution)/shard_map/forward_layer/pallas_call | solution.py:471
  163.6 137.8 %vocabulary_head.1 = (f32[8,128]{1,0:T(8,128)}, bf16[1584,1024]{1,0:T(8,128)(2,1)}, f32[1024,128]{1,0:T(8,128)}) custom-call(bf16[128,1024]{1,0:T(8,128)(2,1)} %get-tuple-element.63.refs_0_, f32[2,2,4,8,256]{4,3,2,1,0:T(8,128)} %get-tuple-element.64.refs_1_, bf16[6288,1024]{1,0:T(8,128)(2,1)} %refs_2_.3), custom_call_target="tpu_custom_call" | custom-call | tf_op jit(solution)/shard_map/vocabulary_head/pallas_call | solution.py:1726
  301.3 244.3 %backward_layer.1 = (bf16[128,3072]{1,0:T(8,128)(2,1)}, bf16[128,1024]{1,0:T(8,128)(2,1)}, bf16[128,1024]{1,0:T(8,128)(2,1)}, bf16[128,2048]{1,0:T(8,128)(2,1)},...) custom-call(bf16[1024,3072]{1,0:T(8,128)(2,1)} %bitcast.24, ...), custom_call_target="tpu_custom_call" | custom-call | tf_op jit(solution)/shard_map/backward_layer/pallas_call | solution.py:1139
  545.6 0.0 copy-start
  545.6 17.7 %widen.1 = (f32[128,3072]{1,0:T(8,128)}, f32[128,1024]{1,0:T(8,128)}, f32[128,1024]{1,0:T(8,128)}, f32[128,2048]{1,0:T(8,128)}, f32[128,1024]{1,0:T(8,128)}, /*i...) custom-call(bf16[128,3072]{1,0:T(8,128)(2,1)} %get-tuple-element.93.r, ...), custom_call_target="tpu_custom_call" | custom-call | tf_op jit(solution)/shard_map/widen/pallas_call | solution.py:1264
  563.3 0.7 slice_reduce_fusion.1
  564.0 0.1 reshape_squeeze.3
  564.1 0.6 slice_reduce_fusion
  564.7 1.2 slice.9
  565.9 0.0 copy-done
  565.9 0.8 copy.33
  566.7 4.8 copy.34
  (2 shorter events, 0.0 us)
Async XLA Ops:
  545.6 20.3 %copy-start = (f32[128,1024]{1,0:T(8,128)S(1)}, f32[128,1024]{1,0:T(8,128)}, u32[]{:S(2)}) copy-start(f32[128,1024]{1,0:T(8,128)} %get-tuple-element.91) | copy-start | bytes 1572868

commit v8 on v7

--- a/solution.py
+++ b/solution.py
@@ -651,6 +651,8 @@
     gemb_copy = pltpu.make_async_copy(gemb, pieces.at[pb], gemb_sem)
     for n in (0, 2, 1, 3):
         gather_one(n).start()
+    for n in (2, 0, 3, 1):
+        gather_two(n, 0).start()
     gemb_copy.start()
 
     def dd_copy(q):
@@ -922,7 +924,6 @@
             @pl.when(i == turn)
             def _():
                 for part in (n, n + 2):
-                    gather_two(part, 0).start()
                     gather_one(part).wait_recv()
                     gather_two(part, 1).start()
 
@@ -1287,8 +1288,8 @@
 
 
 VOCAB_CUTS = 3
-ARRIVAL_PHASES = (0, 0, 1, 0, 1, 2, 3, 0, 1, 2, 3, 1, 2, 3, 2, 3)
-ARRIVAL_TURNS = (0, 1, 0, 2, 1, 0, 0, 3, 2, 1, 1, 3, 2, 2, 3, 3)
+ARRIVAL_PHASES = (0, 0, 1, 2, 0, 1, 2, 3, 0, 1, 2, 3, 1, 2, 3, 3)
+ARRIVAL_TURNS = (0, 1, 0, 0, 2, 1, 1, 0, 3, 2, 2, 1, 3, 3, 2, 3)
 NEAREST = ((0, 1, 2, 3), (1, 0, 1, 2), (2, 2, 3, 1), (3, 3, 0, 0))
 
 
@@ -1325,8 +1326,10 @@
     sibling = at(x, y, z, 1 - c)
     x_peer, y_peer = at(1 - x, y, z, c), at(x, 1 - y, z, c)
 
-    def spot(k, core):
-        return held.at[pl.ds(pl.multiple_of((k * 2 + core) * size, size), size), :]
+    def spot(k, core, n=None):
+        rows_here = size if n is None else size // 2
+        first = (k * 2 + core) * size + (0 if n is None else n * rows_here)
+        return held.at[pl.ds(pl.multiple_of(first, rows_here), rows_here), :]
 
     greet(neighbours(x, y, z, c))
     own_copy = pltpu.make_async_copy(hid, spot(own, c), local_sem.at[0])
@@ -1343,25 +1346,25 @@
     rest_copy.start()
     own_copy.wait()
 
-    def up_copy(origin):
-        block = spot(pb * 4 + origin, c)
-        return remote(block, block, z_send.at[0, origin], z_recv.at[origin], at(x, y, z + 1, c))
-
-    def down_copy(origin):
-        block = spot(pb * 4 + origin, c)
-        return remote(block, block, z_send.at[1, origin], z_recv.at[origin], at(x, y, z - 1, c))
-
-    def pass_along(origin, action):
+    def up_copy(origin, n):
+        block = spot(pb * 4 + origin, c, n)
+        return remote(block, block, z_send.at[0, origin, n], z_recv.at[origin, n], at(x, y, z + 1, c))
+
+    def down_copy(origin, n):
+        block = spot(pb * 4 + origin, c, n)
+        return remote(block, block, z_send.at[1, origin, n], z_recv.at[origin, n], at(x, y, z - 1, c))
+
+    def pass_along(origin, n, action):
         @pl.when((origin <= z) & (z < 3))
         def _():
-            action(up_copy(origin))
+            action(up_copy(origin, n))
 
         @pl.when((origin >= z) & (z > 0))
         def _():
-            action(down_copy(origin))
-
-    def sib_copy(k):
-        return remote(spot(k, c), spot(k, c), sib_send.at[k], sib_recv.at[k], sibling)
+            action(down_copy(origin, n))
+
+    def sib_copy(k, n):
+        return remote(spot(k, c, n), spot(k, c, n), sib_send.at[k, n], sib_recv.at[k, n], sibling)
 
     def order(zz):
         x_first = zz < 2
@@ -1375,20 +1378,21 @@
 
         return f, g, first_peer, second_peer, block
 
-    def one_copy(zz):
+    def one_copy(zz, n):
         f, g, first_peer, _, block = order(zz)
-        return remote(
-            spot(block(f, g), c), spot(block(f, g), c), one_send.at[zz], one_recv.at[zz], first_peer
-        )
-
-    def two_copy(zz, j):
+        part = spot(block(f, g), c, n)
+        return remote(part, part, one_send.at[zz, n], one_recv.at[zz, n], first_peer)
+
+    def two_copy(zz, j, n):
         f, g, _, second_peer, block = order(zz)
-        k = block(f if j == 0 else 1 - f, g)
-        return remote(spot(k, c), spot(k, c), two_send.at[zz, j], two_recv.at[zz, j], second_peer)
-
-    pass_along(z, lambda copy: copy.start())
-    sib_copy(own).start()
-    one_copy(z).start()
+        part = spot(block(f if j == 0 else 1 - f, g), c, n)
+        return remote(part, part, two_send.at[zz, j, n], two_recv.at[zz, j, n], second_peer)
+
+    for n in range(2):
+        pass_along(z, n, lambda copy: copy.start())
+        one_copy(z, n).start()
+        two_copy(z, 0, n).start()
+        sib_copy(own, n).start()
 
     emb_copy.wait()
     rest_copy.wait()
@@ -1475,28 +1479,32 @@
 
         @pl.when((s > 0) & (s < 16) & (phase == 0))
         def _():
-            up_copy(zz).wait_recv()
-            pass_along(zz, lambda copy: copy.start())
-            sib_copy(k).start()
-            one_copy(zz).start()
+            for n in range(2):
+                up_copy(zz, n).wait_recv()
+                pass_along(zz, n, lambda copy: copy.start())
+                one_copy(zz, n).start()
+                two_copy(zz, 0, n).start()
+                sib_copy(k, n).start()
 
         @pl.when((s < 16) & (phase == 1))
         def _():
-            one_copy(zz).wait_recv()
-            sib_copy(k).start()
-            for j in range(2):
-                two_copy(zz, j).start()
+            for n in range(2):
+                one_copy(zz, n).wait_recv()
+                two_copy(zz, 1, n).start()
+                sib_copy(k, n).start()
 
         for j in range(2):
             @pl.when((s < 16) & (phase == 2 + j))
             def _():
-                two_copy(zz, j).wait_recv()
-                sib_copy(k).start()
+                for n in range(2):
+                    two_copy(zz, j, n).wait_recv()
+                    sib_copy(k, n).start()
 
         @pl.when(s > 0)
         def _():
             former = step_block(s - 1)[2]
-            sib_copy(former).wait_recv()
+            for n in range(2):
+                sib_copy(former, n).wait_recv()
             forward_block(former)
 
     def joined(parts):
@@ -1701,16 +1709,19 @@
 
     @pl.loop(0, 4)
     def _(zz):
-        pass_along(zz, lambda copy: copy.wait_send())
-        one_copy(zz).wait_send()
+        for n in range(2):
+            pass_along(zz, n, lambda copy: copy.wait_send())
+            one_copy(zz, n).wait_send()
+            for j in range(2):
+                two_copy(zz, j, n).wait_send()
         for j in range(2):
-            two_copy(zz, j).wait_send()
             r1_copy(zz, j).wait_send()
         r2_copy(zz).wait_send()
 
     @pl.loop(0, 16)
     def _(k):
-        sib_copy(k).wait_send()
+        for n in range(2):
+            sib_copy(k, n).wait_send()
         dd_copy(k).wait_send()
 
 
@@ -1749,10 +1760,10 @@
         ]
         + [pltpu.VMEM((16, 2 * size), f32)] * 5
         + [dma((4,))]
-        + [dma((2, 4)), dma((4,))]
-        + [dma((4,))] * 2
+        + [dma((2, 4, 2)), dma((4, 2))]
         + [dma((4, 2))] * 2
-        + [dma((16,))] * 2
+        + [dma((4, 2, 2))] * 2
+        + [dma((16, 2))] * 2
         + [dma((3,))] * 4
         + [dma((16,))] * 2
         + [dma((4, 2))] * 2

time: 576 us -> 562 us (0.976)
  Pallas kernels: 557 us -> 544 us
    pallas_call x1, Pallas kernels: 138 us -> 124 us  [vocabulary_head(): pl.pallas_call(functools.partial(head_kernel, slots, length, vocab_here),...]
where the time goes in v8:
time: 562 us; the launch traced here: 558 us
  Pallas kernels  544 us (97%)
  local copies, waits for them, and re-layouts  9.39 us (2%)
    pallas_call x1, Pallas kernels, backward_layer(): pl.pallas_call(functools.partial(backward_kernel, length, mem_length), ou...  245 us
    pallas_call x1, Pallas kernels, forward_layer(): pl.pallas_call(functools.partial(forward_kernel, length, mem_length), out...  158 us
    pallas_call x1, Pallas kernels, vocabulary_head(): pl.pallas_call(functools.partial(head_kernel, slots, length, vocab_here),...  124 us
    pallas_call x1, Pallas kernels, widen(): pl.pallas_call(functools.partial(widen_kernel, embed_rows), out_shape=tup...  17.7 us

profile of v8, /device:TPU:0, one launch (start us, length us, event | category | flops | bytes accessed | tf_op | source)
XLA Modules:
  0.0 558.3 jit_solution(2418743848879452108)
XLA Ops:
  1.3 0.7 fusion
  2.0 0.1 broadcast_in_dim.20
  2.0 0.1 broadcast_in_dim.21
  2.1 0.7 broadcast_in_dim.18
  2.8 0.1 broadcast_in_dim.19
  2.9 0.7 convert_element_type.25
  3.6 0.1 convert_element_type.26
  3.7 0.1 pad.3.clone
  3.8 0.7 maximum_maximum_fusion.refs_8_
  4.4 0.1 pad.6.clone
  4.5 1.4 maximum_convert_fusion.refs_7_
  5.9 157.7 %forward_layer.1 = (bf16[4,2,128,3072]{3,2,1,0:T(8,128)(2,1)}, bf16[4,2,128,1024]{3,2,1,0:T(8,128)(2,1)}, bf16[4,2,128,1024]{3,2,1,0:T(8,128)(2,1)}, bf16[4,2,12...) custom-call(bf16[128,3072]{1,0:T(8,128)(2,1)} %refs_0_.1, ...), custom_call_target="tpu_custom_call" | custom-call | tf_op jit(solution)/shard_map/forward_layer/pallas_call | solution.py:471
  163.6 123.7 %vocabulary_head.1 = (f32[8,128]{1,0:T(8,128)}, bf16[1584,1024]{1,0:T(8,128)(2,1)}, f32[1024,128]{1,0:T(8,128)}) custom-call(bf16[128,1024]{1,0:T(8,128)(2,1)} %get-tuple-element.63.refs_0_, f32[2,2,4,8,256]{4,3,2,1,0:T(8,128)} %get-tuple-element.64.refs_1_, bf16[6288,1024]{1,0:T(8,128)(2,1)} %refs_2_.3), custom_call_target="tpu_custom_call" | custom-call | tf_op jit(solution)/shard_map/vocabulary_head/pallas_call | solution.py:1737
  287.3 245.0 %backward_layer.1 = (bf16[128,3072]{1,0:T(8,128)(2,1)}, bf16[128,1024]{1,0:T(8,128)(2,1)}, bf16[128,1024]{1,0:T(8,128)(2,1)}, bf16[128,2048]{1,0:T(8,128)(2,1)},...) custom-call(bf16[1024,3072]{1,0:T(8,128)(2,1)} %bitcast.24, ...), custom_call_target="tpu_custom_call" | custom-call | tf_op jit(solution)/shard_map/backward_layer/pallas_call | solution.py:1140
  532.3 0.0 copy-start
  532.3 17.7 %widen.1 = (f32[128,3072]{1,0:T(8,128)}, f32[128,1024]{1,0:T(8,128)}, f32[128,1024]{1,0:T(8,128)}, f32[128,2048]{1,0:T(8,128)}, f32[128,1024]{1,0:T(8,128)}, /*i...) custom-call(bf16[128,3072]{1,0:T(8,128)(2,1)} %get-tuple-element.93.r, ...), custom_call_target="tpu_custom_call" | custom-call | tf_op jit(solution)/shard_map/widen/pallas_call | solution.py:1265
  550.0 0.7 slice_reduce_fusion.1
  550.7 0.1 reshape_squeeze.3
  550.7 0.6 slice_reduce_fusion
  551.4 1.2 slice.9
  552.6 0.0 copy-done
  552.6 0.8 copy.33
  553.4 4.8 copy.34
  (2 shorter events, 0.0 us)
Async XLA Ops:
  532.3 20.3 %copy-start = (f32[128,1024]{1,0:T(8,128)S(1)}, f32[128,1024]{1,0:T(8,128)}, u32[]{:S(2)}) copy-start(f32[128,1024]{1,0:T(8,128)} %get-tuple-element.91) | copy-start | bytes 1572868

commit v9 on v8

--- a/solution.py
+++ b/solution.py
@@ -126,12 +126,12 @@
         cross_context, second_normed, second_inverse, second_low, inner, active, third_normed,
         third_inverse, third_low,
     ) = refs[36:53]
-    wbuf, residual, states, encoded = refs[53:57]
+    wbuf, residual, states, encoded, held = refs[53:58]
     (
         local_sem, z_send, z_recv, one_send, one_recv, two_send, two_recv, d_send, d_recv,
         norm_sem, nz_send, nz_recv, nd_send, nd_recv, load_sem, ax_sem, ax_send, ax_recv,
-        axz_send, axz_recv, kept_sem, input_sem,
-    ) = refs[57:]
+        axz_send, axz_recv, kept_sem, input_sem, take_sem,
+    ) = refs[58:]
     x, y, z, c = whereami()
     greet(neighbours(x, y, z, c))
     every = slice(None)
@@ -148,13 +148,13 @@
         quarter = pl.multiple_of(64 * a + 32 * b, 32)
         half = pl.multiple_of(64 * a, 64)
         rows = (0, ROWS) if wide else (quarter, 32)
-        local = pltpu.make_async_copy(
-            shard_view(shard, unit, *rows), full_view(full, unit, z, c, *rows), local_sem.at[u]
-        )
-        def along(origin, direction):
+        place = held.at[pl.ds(sum(ROWS if n in Z_FULL else 32 for n in range(u)), rows[1]), :]
+        take = pltpu.make_async_copy(shard_view(shard, unit, *rows), place, take_sem.at[u])
+        local = pltpu.make_async_copy(place, full_view(full, unit, z, c, *rows), local_sem.at[u])
+        def along(origin, direction, own=False):
             block = full_view(full, unit, origin, c, *rows)
             return pltpu.make_async_remote_copy(
-                src_ref=block,
+                src_ref=place if own else block,
                 dst_ref=block,
                 send_sem=z_send.at[u, (direction + 1) // 2, origin],
                 recv_sem=z_recv.at[u, origin],
@@ -181,7 +181,7 @@
             wbuf.at[u % SLOTS_IN_FLIGHT],
             load_sem.at[u % SLOTS_IN_FLIGHT],
         )
-        return local, along, first, second, sibling, load
+        return (take, local), along, first, second, sibling, load
 
     def norm_copy(src, dst, send, recv, peer):
         return pltpu.make_async_remote_copy(
@@ -349,8 +349,11 @@
     every_copy = [copies(u) for u in range(count)]
 
     def hop(u, h):
-        local, along = every_copy[u][:2]
+        (take, local), along = every_copy[u][:2]
         if h == 1:
+            take.wait()
+            local.start()
+        if h == 4:
             local.wait()
         for origin, there, edge, direction in (
             (z - (h - 1), z >= h - 1, z < 3, 1),
@@ -363,10 +366,10 @@
                 if h < 4:
                     @pl.when(edge)
                     def _():
-                        along(origin, direction).start()
+                        along(origin, direction, h == 1).start()
 
     for copies_here in every_copy:
-        copies_here[0].start()
+        copies_here[0][0].start()
     for h in range(1, 4):
         for u in range(HOP_LAG * (4 - h)):
             hop(u, h)
@@ -481,6 +484,7 @@
             pltpu.VMEM((tokens, width), f32),
             pltpu.VMEM((tokens, width), BFLOAT),
             pltpu.VMEM((mem_tokens, width), BFLOAT),
+            pltpu.VMEM((sum(ROWS if n in Z_FULL else 32 for n in range(count)), TILE), BFLOAT),
             dma((count,)),
             dma((count, 2, 4)),
             dma((count, 4)),
@@ -492,7 +496,7 @@
         + [dma((SLOTS_IN_FLIGHT,))]
         + [dma]
         + [dma((3,))] * 4
-        + [dma((len(kept),)), dma((2,))],
+        + [dma((len(kept),)), dma((2,)), dma((count,))],
         compiler_params=pltpu.CompilerParams(
             collective_id=0, has_side_effects=True, vmem_limit_bytes=62 * 2**20
         ),
@@ -1193,11 +1197,16 @@
 
 
 def widen_kernel(embed_rows, *refs):
-    parts, pieces, norms = refs[:7], refs[7], refs[8]
-    outs, embed_out, gains_out, shifts_out = refs[9:16], refs[16], refs[17], refs[18]
-    low, wide = refs[19:26], refs[26:33]
-    embed_low, embed_wide, norm_here = refs[33:36]
-    in_sem, out_sem, embed_in, embed_out_sem, norm_sem = refs[36:]
+    parts, pieces, norms, done = refs[:7], refs[7], refs[8], refs[9:11]
+    outs, embed_out, done_out = refs[11:18], refs[18], refs[19:21]
+    gains_out, shifts_out = refs[21:23]
+    low, wide = refs[23:30], refs[30:37]
+    embed_low, embed_wide, norm_here, done_here = refs[37:40] + (refs[40:42],)
+    in_sem, out_sem, embed_in, embed_out_sem, norm_sem, done_sem = refs[42:]
+    done_in = [pltpu.make_async_copy(done[n], done_here[n], done_sem.at[n]) for n in range(2)]
+    done_copies = [
+        pltpu.make_async_copy(done_here[n], done_out[n], done_sem.at[n + 2]) for n in range(2)
+    ]
     here = norm_here.shape[1]
     norm_copy = pltpu.make_async_copy(
         norms.at[:, pl.ds(pl.multiple_of(lax.axis_index("pa") * here, here), here)], norm_here, norm_sem
@@ -1225,6 +1234,8 @@
         load(n, sizes[n]).start()
     for n in range(7):
         pltpu.make_async_copy(parts[n], low[n], in_sem.at[n]).start()
+    for copy in done_in:
+        copy.start()
     for n, rows in enumerate(sizes):
         load(n, rows).wait()
         if n >= WIDE_SLOTS:
@@ -1247,6 +1258,9 @@
             wide[n][part, :] = low[n][part, :].astype(jnp.float32)
 
         pltpu.make_async_copy(wide[n], outs[n], out_sem.at[n]).start()
+    for n in range(2):
+        done_in[n].wait()
+        done_copies[n].start()
     norm_copy.wait()
     gains_out[...] = norm_here[0:3, :]
     shifts_out[...] = norm_here[3:6, :]
@@ -1254,9 +1268,11 @@
         store(n, sizes[n]).wait()
     for n in range(7):
         pltpu.make_async_copy(wide[n], outs[n], out_sem.at[n]).wait()
-
-
-def widen(parts, pieces, norms, embed_rows, norm_here):
+    for copy in done_copies:
+        copy.wait()
+
+
+def widen(parts, pieces, norms, done, embed_rows, norm_here):
     every = pl.BlockSpec(memory_space=pl.ANY)
     vmem = pl.BlockSpec(memory_space=pltpu.VMEM)
     f32 = jnp.float32
@@ -1266,25 +1282,29 @@
         functools.partial(widen_kernel, embed_rows),
         out_shape=tuple(jax.ShapeDtypeStruct(part.shape, f32) for part in parts)
         + (jax.ShapeDtypeStruct((embed_rows, width), f32),)
+        + tuple(jax.ShapeDtypeStruct(part.shape, part.dtype) for part in done)
         + (jax.ShapeDtypeStruct((3, norm_here), f32),) * 2,
-        in_specs=[every] * 9,
-        out_specs=(every,) * 8 + (vmem,) * 2,
+        in_specs=[every] * 11,
+        out_specs=(every,) * 10 + (vmem,) * 2,
         scratch_shapes=[pltpu.VMEM(part.shape, BFLOAT) for part in parts]
         + [pltpu.VMEM(part.shape, f32) for part in parts]
         + [
             pltpu.VMEM((WIDE_SLOTS, WIDE_ROWS, width), BFLOAT),
             pltpu.VMEM((WIDE_SLOTS, WIDE_ROWS, width), f32),
             pltpu.VMEM((8, norm_here), f32),
+            pltpu.VMEM(done[0].shape, f32),
+            pltpu.VMEM(done[1].shape, f32),
             dma((7,)),
             dma((7,)),
             dma((WIDE_SLOTS,)),
             dma((WIDE_SLOTS,)),
             dma,
+            dma((4,)),
         ],
         compiler_params=pltpu.CompilerParams(vmem_limit_bytes=60 * 2**20),
         name="widen",
-    )(*parts, pieces, norms)
-    return results[:7], results[7], results[8], results[9]
+    )(*parts, pieces, norms, *done)
+    return results[:7], results[7:]
 
 
 VOCAB_CUTS = 3
@@ -1298,13 +1318,13 @@
     small_out, gemb_out, third_out = refs[3:6]
     (
         emb, emb_t, held, logit, expo, part, sib_part, part_one, part_two, part_z,
-        mine, theirs, lined, prior, usable, weight, scaled, picked_grad,
-    ) = refs[6:24]
+        mine, theirs, crossed, lined, prior, usable, weight, scaled, picked_grad,
+    ) = refs[6:25]
     (
         local_sem, z_send, z_recv, one_send, one_recv, two_send, two_recv, sib_send, sib_recv,
         st_send, st_recv, stz_send, stz_recv,
         dd_send, dd_recv, r1_send, r1_recv, r2_send, r2_recv, rz_send, rz_recv,
-    ) = refs[24:]
+    ) = refs[25:]
     x, y, z, c = whereami()
     pb, pa = y * 2 + x, z * 2 + c
     size = hid.shape[0]
@@ -1331,7 +1351,8 @@
         first = (k * 2 + core) * size + (0 if n is None else n * rows_here)
         return held.at[pl.ds(pl.multiple_of(first, rows_here), rows_here), :]
 
-    greet(neighbours(x, y, z, c))
+    across = [at(1 - x, y, z, c), at(x, 1 - y, z, c), at(1 - x, 1 - y, z, c)]
+    greet(neighbours(x, y, z, c) + across[2:])
     own_copy = pltpu.make_async_copy(hid, spot(own, c), local_sem.at[0])
     own_copy.start()
     emb_copy = pltpu.make_async_copy(
@@ -1516,24 +1537,33 @@
     def rows_of(ref, n):
         return ref[n, 0], ref[n, 1], ref[n, 2]
 
-    for n, (peer, side) in enumerate(((sibling, c), (x_peer, x), (y_peer, y))):
-        copy = remote(mine.at[n], theirs.at[n], st_send.at[n], st_recv.at[n], peer)
+    copy = remote(mine.at[0], theirs, st_send.at[0], st_recv.at[0], sibling)
+    copy.start()
+    copy.wait()
+    here, there = rows_of(mine, 0), (theirs[0], theirs[1], theirs[2])
+    early = tuple(jnp.where(c == 0, p, q) for p, q in zip(here, there))
+    late = tuple(jnp.where(c == 0, q, p) for p, q in zip(here, there))
+    for r, value in enumerate(joined((early, late))):
+        mine[1, r] = value
+        crossed[pb, r] = value
+    pb_copies = [
+        remote(mine.at[1], crossed.at[pb], st_send.at[n + 1], st_recv.at[n + 1], peer)
+        for n, peer in enumerate(across)
+    ]
+    for copy in pb_copies:
         copy.start()
+    for copy in pb_copies:
         copy.wait()
-        here, there = rows_of(mine, n), rows_of(theirs, n)
-        early = tuple(jnp.where(side == 0, a, b) for a, b in zip(here, there))
-        late = tuple(jnp.where(side == 0, b, a) for a, b in zip(here, there))
-        for r, value in enumerate(joined((early, late))):
-            mine[n + 1, r] = value
+    for r, value in enumerate(joined([rows_of(crossed, n) for n in range(4)])):
+        mine[2, r] = value
+        lined[z, r] = value
 
     def stat_copy(d):
         other = lax.rem(z + d, 4)
-        return remote(mine.at[3], lined.at[z], stz_send.at[d - 1], stz_recv.at[d - 1], at(x, y, other, c))
+        return remote(mine.at[2], lined.at[z], stz_send.at[d - 1], stz_recv.at[d - 1], at(x, y, other, c))
 
     for d in (1, 2, 3):
         stat_copy(d).start()
-    for r in range(3):
-        lined[z, r] = mine[3, r]
     for d in (1, 2, 3):
         stat_copy(d).wait()
     highest, total, picked = joined([rows_of(lined, n) for n in range(4)])
@@ -1611,20 +1641,32 @@
             first_peer,
         )
 
-    def r2_copy(zz):
+    def half(n):
+        return pl.ds(n * (width // 2), width // 2)
+
+    def r2_copy(zz, n):
         _, g, _, second_peer, _ = order(zz)
-        return remote(part_one.at[zz, 1 - g], part_two.at[zz], r2_send.at[zz], r2_recv.at[zz], second_peer)
-
-    def rz_copy(zz):
-        return remote(part_two.at[zz], part_z.at[z], rz_send.at[zz], rz_recv.at[z], at(x, y, zz, c))
-
-    def rz_arrival(zz):
-        return remote(part_two.at[zz], part_z.at[zz], rz_send.at[zz], rz_recv.at[zz], at(x, y, zz, c))
+        return remote(
+            part_one.at[zz, 1 - g, half(n), :], part_two.at[zz, half(n), :], r2_send.at[zz, n],
+            r2_recv.at[zz, n], second_peer,
+        )
+
+    def rz_copy(zz, n):
+        return remote(
+            part_two.at[zz, half(n), :], part_z.at[z, half(n), :], rz_send.at[zz, n], rz_recv.at[z, n],
+            at(x, y, zz, c),
+        )
+
+    def rz_arrival(zz, n):
+        return remote(
+            part_two.at[zz, half(n), :], part_z.at[zz, half(n), :], rz_send.at[zz, n],
+            rz_recv.at[zz, n], at(x, y, zz, c),
+        )
 
     step = 128
 
     def add_into(target_ref, other_ref):
-        @pl.loop(0, width // step)
+        @pl.loop(0, target_ref.shape[0] // step)
         def _(n):
             rows_here = pl.ds(pl.multiple_of(n * step, step), step)
             target_ref[rows_here, :] = (
@@ -1670,18 +1712,20 @@
             for j in range(2):
                 r1_copy(zz, j).wait_recv()
                 add_into(part_one.at[zz, j], sib_part.at[block(f, j)])
-            r2_copy(zz).start()
+            for n in range(2):
+                r2_copy(zz, n).start()
 
         @pl.when((lax.rem(s, 2) == 0) & (s >= 16) & (s < 24))
         def _():
             zz = group((s - 16) // 2)
             _, g, _, _, _ = order(zz)
-            r2_copy(zz).wait_recv()
-            add_into(part_two.at[zz], part_one.at[zz, g])
-
-            @pl.when(zz != z)
-            def _():
-                rz_copy(zz).start()
+            for n in range(2):
+                r2_copy(zz, n).wait_recv()
+                add_into(part_two.at[zz, half(n), :], part_one.at[zz, g, half(n), :])
+
+                @pl.when(zz != z)
+                def _():
+                    rz_copy(zz, n).start()
 
         @pl.when(s < 16)
         def _():
@@ -1694,7 +1738,8 @@
             chunk(s - 16)
 
     for d in (1, 2, 3):
-        rz_arrival(lax.rem(z + d, 4)).wait_recv()
+        for n in range(2):
+            rz_arrival(lax.rem(z + d, 4), n).wait_recv()
 
     @pl.loop(0, width // step)
     def _(n):
@@ -1705,7 +1750,8 @@
         third_out[rows_here, :] = value
 
     for d in (1, 2, 3):
-        rz_copy(lax.rem(z + d, 4)).wait_send()
+        for n in range(2):
+            rz_copy(lax.rem(z + d, 4), n).wait_send()
 
     @pl.loop(0, 4)
     def _(zz):
@@ -1716,7 +1762,8 @@
                 two_copy(zz, j, n).wait_send()
         for j in range(2):
             r1_copy(zz, j).wait_send()
-        r2_copy(zz).wait_send()
+        for n in range(2):
+            r2_copy(zz, n).wait_send()
 
     @pl.loop(0, 16)
     def _(k):
@@ -1754,8 +1801,9 @@
             pltpu.VMEM((4, 2) + block, BFLOAT),
             pltpu.VMEM((4,) + block, BFLOAT),
             pltpu.VMEM((4,) + block, BFLOAT),
+            pltpu.VMEM((3,) + stat, f32),
+            pltpu.VMEM(stat, f32),
             pltpu.VMEM((4,) + stat, f32),
-            pltpu.VMEM((3,) + stat, f32),
             pltpu.VMEM((4,) + stat, f32),
         ]
         + [pltpu.VMEM((16, 2 * size), f32)] * 5
@@ -1764,10 +1812,11 @@
         + [dma((4, 2))] * 2
         + [dma((4, 2, 2))] * 2
         + [dma((16, 2))] * 2
-        + [dma((3,))] * 4
+        + [dma((4,))] * 2
+        + [dma((3,))] * 2
         + [dma((16,))] * 2
         + [dma((4, 2))] * 2
-        + [dma((4,))] * 4,
+        + [dma((4, 2))] * 4,
         compiler_params=pltpu.CompilerParams(
             collective_id=2, has_side_effects=True, vmem_limit_bytes=60 * 2**20
         ),
@@ -2286,8 +2335,13 @@
         length,
     )
     pieces = pieces.reshape(4 * grad_embed.shape[0], model_width)
-    shares, grad_embed, grad_gains, grad_shifts = widen(
-        shares, pieces, norm_sums, embedding.shape[0], norm_gains.shape[1]
+    shares, (grad_embed, grad_inputs, grad_encoded, grad_gains, grad_shifts) = widen(
+        shares,
+        pieces,
+        norm_sums,
+        (grad_inputs, grad_encoded),
+        embedding.shape[0],
+        norm_gains.shape[1],
     )
     return (
         loss_value,

time: 562 us -> 555 us (0.988)
  no operation moved by 1% of the time
where the time goes in v9:
time: 555 us; the launch traced here: 551 us
  Pallas kernels  542 us (98%)
    pallas_call x1, Pallas kernels, backward_layer(): pl.pallas_call(functools.partial(backward_kernel, length, mem_length), ou...  244 us
    pallas_call x1, Pallas kernels, forward_layer(): pl.pallas_call(functools.partial(forward_kernel, length, mem_length), out...  155 us
    pallas_call x1, Pallas kernels, vocabulary_head(): pl.pallas_call(functools.partial(head_kernel, slots, length, vocab_here),...  124 us
    pallas_call x1, Pallas kernels, widen(): pl.pallas_call(functools.partial(widen_kernel, embed_rows), out_shape=tup...  20.2 us

profile of v9, /device:TPU:0, one launch (start us, length us, event | category | flops | bytes accessed | tf_op | source)
XLA Modules:
  0.0 550.9 jit_solution(13547634978448759294)
XLA Ops:
  1.3 0.7 fusion
  2.0 0.1 broadcast_in_dim.20
  2.0 0.1 broadcast_in_dim.21
  2.1 0.7 broadcast_in_dim.18
  2.8 0.1 broadcast_in_dim.19
  2.9 0.7 convert_element_type.25
  3.6 0.1 convert_element_type.26
  3.7 0.1 pad.3.clone
  3.8 0.7 maximum_maximum_fusion.refs_8_
  4.4 0.1 pad.6.clone
  4.5 1.4 maximum_convert_fusion.refs_7_
  5.9 154.5 %forward_layer.1 = (bf16[4,2,128,3072]{3,2,1,0:T(8,128)(2,1)}, bf16[4,2,128,1024]{3,2,1,0:T(8,128)(2,1)}, bf16[4,2,128,1024]{3,2,1,0:T(8,128)(2,1)}, bf16[4,2,12...) custom-call(bf16[128,3072]{1,0:T(8,128)(2,1)} %refs_0_.1, ...), custom_call_target="tpu_custom_call" | custom-call | tf_op jit(solution)/shard_map/forward_layer/pallas_call | solution.py:474
  160.4 123.7 %vocabulary_head.1 = (f32[8,128]{1,0:T(8,128)}, bf16[1584,1024]{1,0:T(8,128)(2,1)}, f32[1024,128]{1,0:T(8,128)}) custom-call(bf16[128,1024]{1,0:T(8,128)(2,1)} %get-tuple-element.65.refs_0_, f32[2,2,4,8,256]{4,3,2,1,0:T(8,128)} %get-tuple-element.66.refs_1_, bf16[6288,1024]{1,0:T(8,128)(2,1)} %refs_2_.3), custom_call_target="tpu_custom_call" | custom-call | tf_op jit(solution)/shard_map/vocabulary_head/pallas_call | solution.py:1784
  284.1 243.8 %backward_layer.1 = (bf16[128,3072]{1,0:T(8,128)(2,1)}, bf16[128,1024]{1,0:T(8,128)(2,1)}, bf16[128,1024]{1,0:T(8,128)(2,1)}, bf16[128,2048]{1,0:T(8,128)(2,1)},...) custom-call(bf16[1024,3072]{1,0:T(8,128)(2,1)} %bitcast.24, ...), custom_call_target="tpu_custom_call" | custom-call | tf_op jit(solution)/shard_map/backward_layer/pallas_call | solution.py:1144
  528.0 20.2 %widen.1 = (f32[128,3072]{1,0:T(8,128)}, f32[128,1024]{1,0:T(8,128)}, f32[128,1024]{1,0:T(8,128)}, f32[128,2048]{1,0:T(8,128)}, f32[128,1024]{1,0:T(8,128)}, /*i...) custom-call(bf16[128,3072]{1,0:T(8,128)(2,1)} %get-tuple-element.93., ...), custom_call_target="tpu_custom_call" | custom-call | tf_op jit(solution)/shard_map/widen/pallas_call | solution.py:1281
  548.1 0.7 slice_reduce_fusion.1
  548.8 0.1 reshape_squeeze.3
  548.9 0.6 slice_reduce_fusion
  549.6 1.2 slice.9
  (2 shorter events, 0.0 us)

commit v10 on v9

--- a/solution.py
+++ b/solution.py
@@ -158,7 +158,7 @@
                 dst_ref=block,
                 send_sem=z_send.at[u, (direction + 1) // 2, origin],
                 recv_sem=z_recv.at[u, origin],
-                device_id=at(x, y, z + direction, c),
+                device_id=at(x, y, lax.rem(z + direction + 4, 4), c),
                 device_id_type=MESH,
             )
 
@@ -667,7 +667,7 @@
     def line_copy(q, side, h, dest, step):
         return remote(
             got.at[q, dest], landing.at[q, side, h - 1], z_send.at[q, side, h - 1],
-            z_recv.at[q, side, h - 1], at(x, y, z + step, c),
+            z_recv.at[q, side, h - 1], at(x, y, lax.rem(z + step + 4, 4), c),
         )
 
     def line_sides(h):
@@ -1369,11 +1369,11 @@
 
     def up_copy(origin, n):
         block = spot(pb * 4 + origin, c, n)
-        return remote(block, block, z_send.at[0, origin, n], z_recv.at[origin, n], at(x, y, z + 1, c))
+        return remote(block, block, z_send.at[0, origin, n], z_recv.at[origin, n], at(x, y, lax.rem(z + 1, 4), c))
 
     def down_copy(origin, n):
         block = spot(pb * 4 + origin, c, n)
-        return remote(block, block, z_send.at[1, origin, n], z_recv.at[origin, n], at(x, y, z - 1, c))
+        return remote(block, block, z_send.at[1, origin, n], z_recv.at[origin, n], at(x, y, lax.rem(z + 3, 4), c))
 
     def pass_along(origin, n, action):
         @pl.when((origin <= z) & (z < 3))

time: 555 us -> 555 us (level)
  no operation moved by 1% of the time
where the time goes in v10:
time: 555 us; the launch traced here: 551 us
  Pallas kernels  542 us (98%)
    pallas_call x1, Pallas kernels, backward_layer(): pl.pallas_call(functools.partial(backward_kernel, length, mem_length), ou...  244 us
    pallas_call x1, Pallas kernels, forward_layer(): pl.pallas_call(functools.partial(forward_kernel, length, mem_length), out...  155 us
    pallas_call x1, Pallas kernels, vocabulary_head(): pl.pallas_call(functools.partial(head_kernel, slots, length, vocab_here),...  124 us
    pallas_call x1, Pallas kernels, widen(): pl.pallas_call(functools.partial(widen_kernel, embed_rows), out_shape=tup...  20.2 us

profile of v10, /device:TPU:0, one launch (start us, length us, event | category | flops | bytes accessed | tf_op | source)
XLA Modules:
  0.0 550.9 jit_solution(14587549779694229669)
XLA Ops:
  1.3 0.7 fusion
  2.0 0.1 broadcast_in_dim.20
  2.0 0.1 broadcast_in_dim.21
  2.1 0.7 broadcast_in_dim.18
  2.8 0.1 broadcast_in_dim.19
  2.9 0.7 convert_element_type.25
  3.6 0.1 convert_element_type.26
  3.7 0.1 pad.3.clone
  3.8 0.7 maximum_maximum_fusion.refs_8_
  4.4 0.1 pad.6.clone
  4.5 1.4 maximum_convert_fusion.refs_7_
  5.9 154.5 %forward_layer.1 = (bf16[4,2,128,3072]{3,2,1,0:T(8,128)(2,1)}, bf16[4,2,128,1024]{3,2,1,0:T(8,128)(2,1)}, bf16[4,2,128,1024]{3,2,1,0:T(8,128)(2,1)}, bf16[4,2,12...) custom-call(bf16[128,3072]{1,0:T(8,128)(2,1)} %refs_0_.1, ...), custom_call_target="tpu_custom_call" | custom-call | tf_op jit(solution)/shard_map/forward_layer/pallas_call | solution.py:474
  160.4 123.7 %vocabulary_head.1 = (f32[8,128]{1,0:T(8,128)}, bf16[1584,1024]{1,0:T(8,128)(2,1)}, f32[1024,128]{1,0:T(8,128)}) custom-call(bf16[128,1024]{1,0:T(8,128)(2,1)} %get-tuple-element.65.refs_0_, f32[2,2,4,8,256]{4,3,2,1,0:T(8,128)} %get-tuple-element.66.refs_1_, bf16[6288,1024]{1,0:T(8,128)(2,1)} %refs_2_.3), custom_call_target="tpu_custom_call" | custom-call | tf_op jit(solution)/shard_map/vocabulary_head/pallas_call | solution.py:1784
  284.1 243.8 %backward_layer.1 = (bf16[128,3072]{1,0:T(8,128)(2,1)}, bf16[128,1024]{1,0:T(8,128)(2,1)}, bf16[128,1024]{1,0:T(8,128)(2,1)}, bf16[128,2048]{1,0:T(8,128)(2,1)},...) custom-call(bf16[1024,3072]{1,0:T(8,128)(2,1)} %bitcast.24, ...), custom_call_target="tpu_custom_call" | custom-call | tf_op jit(solution)/shard_map/backward_layer/pallas_call | solution.py:1144
  528.0 20.2 %widen.1 = (f32[128,3072]{1,0:T(8,128)}, f32[128,1024]{1,0:T(8,128)}, f32[128,1024]{1,0:T(8,128)}, f32[128,2048]{1,0:T(8,128)}, f32[128,1024]{1,0:T(8,128)}, /*i...) custom-call(bf16[128,3072]{1,0:T(8,128)(2,1)} %get-tuple-element.93., ...), custom_call_target="tpu_custom_call" | custom-call | tf_op jit(solution)/shard_map/widen/pallas_call | solution.py:1281
  548.1 0.7 slice_reduce_fusion.1
  548.8 0.1 reshape_squeeze.3
  548.9 0.6 slice_reduce_fusion
  549.6 1.2 slice.9
  (2 shorter events, 0.0 us)
